TPU v7x, 128 devices: a whole 4x4x4 slice. The times are simulated.
128 devices in a mesh: dp: 16 (over z_hi, y, core), tensor: 8 (over x, z_lo).
Axes of the slice: x: 4, y: 4, z: 4 (z_hi: 2, z_lo: 2; z = z_hi * 2 + z_lo), core: 2. Of those that a mesh axis runs over, the one named last changes fastest.
Arguments:
- tokens: bfloat16 [16384, 1024], P(('dp', 'tensor')), may hold values from -6 to 6
- out_grad: bfloat16 [16384, 1024], P(('dp', 'tensor')), may hold values from -6 to 6
- lengths: int32 [16, 4], P('dp'), may hold values from 0 to 1024, as said below
- w_query: float32 [1024, 2048], P('dp', 'tensor'), may hold values from -0.1875 to 0.1875
- key_weight: float32 [1024, 1024], P('dp', 'tensor'), may hold values from -0.1875 to 0.1875
- value_weight: float32 [1024, 1024], P('dp', 'tensor'), may hold values from -0.1875 to 0.1875
- w_output: float32 [2048, 1024], P('tensor', 'dp'), may hold values from -0.5 to 0.5
- w_gate: float32 [1024, 3072], P('dp', 'tensor'), may hold values from -0.1875 to 0.1875
- w_up: float32 [1024, 3072], P('dp', 'tensor'), may hold values from -0.1875 to 0.1875
- w_down: float32 [3072, 1024], P('tensor', 'dp'), may hold values from -0.109375 to 0.109375
- momentum_query: float32 [1024, 2048], P('dp', 'tensor'), may hold values from -224 to 224
- key_momentum_buffer: float32 [1024, 1024], P('dp', 'tensor'), may hold values from -224 to 224
- value_momentum_buffer: float32 [1024, 1024], P('dp', 'tensor'), may hold values from -768 to 768
- momentum_output: float32 [2048, 1024], P('tensor', 'dp'), may hold values from -160 to 160
- momentum_gate: float32 [1024, 3072], P('dp', 'tensor'), may hold values from -224 to 224
- momentum_up: float32 [1024, 3072], P('dp', 'tensor'), may hold values from -224 to 224
- momentum_down: float32 [3072, 1024], P('tensor', 'dp'), may hold values from -448 to 448
- gains: float32 [2304], replicated, may hold values from 0.5 to 1.5
- gain_first: float32 [2304], replicated, may hold values from -32 to 32
- gain_second: float32 [2304], replicated, may hold values from 137.6256 to 557.056
Outputs:
- out: bfloat16 [16384, 1024], P(('dp', 'tensor'))
- tokens_grad: float32 [16384, 1024], P(('dp', 'tensor'))
- grad_query: float32 [1024, 2048], P('dp', 'tensor')
- grad_key: float32 [1024, 1024], P('dp', 'tensor')
- grad_value: float32 [1024, 1024], P('dp', 'tensor')
- grad_output: float32 [2048, 1024], P('tensor', 'dp')
- grad_gate: float32 [1024, 3072], P('dp', 'tensor')
- grad_up: float32 [1024, 3072], P('dp', 'tensor')
- grad_down: float32 [3072, 1024], P('tensor', 'dp')
- renewed_query: float32 [1024, 2048], P('dp', 'tensor')
- renewed_key: float32 [1024, 1024], P('dp', 'tensor')
- renewed_value: float32 [1024, 1024], P('dp', 'tensor')
- renewed_output: float32 [2048, 1024], P('tensor', 'dp')
- renewed_gate: float32 [1024, 3072], P('dp', 'tensor')
- renewed_up: float32 [1024, 3072], P('dp', 'tensor')
- renewed_down: float32 [3072, 1024], P('tensor', 'dp')
- updated_query: float32 [1024, 2048], P('dp', 'tensor')
- updated_key: float32 [1024, 1024], P('dp', 'tensor')
- updated_value: float32 [1024, 1024], P('dp', 'tensor')
- updated_output: float32 [2048, 1024], P('tensor', 'dp')
- updated_gate: float32 [1024, 3072], P('dp', 'tensor')
- updated_up: float32 [1024, 3072], P('dp', 'tensor')
- updated_down: float32 [3072, 1024], P('tensor', 'dp')
- gain_grad: float32 [2304], replicated
- renewed_first: float32 [2304], replicated
- renewed_second: float32 [2304], replicated
- updated_gains: float32 [2304], replicated
Inputs may be any that keep to these rules, and one draw needn't show every extreme that they name: In each group the 4 lengths sum to 1024; some lengths may be zero.
All inputs are finite; a program needn't handle non-finite values.
Results may differ from a plain program's by a relative error of at most 0.013.
The roundings to bfloat16 on the way count: a program that leaves them out, or rounds other values in their place, can miss the bound.
Values may be sent and summed in bfloat16 or wider, within the bound.
No kernel may reach another device: no remote copies, remote signals or barrier semaphores. Data moves between devices by JAX's collectives and lax.ppermute only.
A program may use at most 128 MiB of HBM per device.

v0:
```python
import math

import jax
import jax.numpy as jnp
from jax import lax
from jax.sharding import PartitionSpec as P

MODEL_WIDTH = 1024
QUERY_HEADS = 16
HEAD_SIZE = 128
FF = 3072
NS_ITERS = 5
ADAM_STEP = 10


EPS = 1e-06
THETA = 1000000.0
NS_A = 3.4445
NS_B = -4.775
NS_C = 2.0315
MOMENTUM = 0.95
BETA_ONE = 0.9
BETA_TWO = 0.95
GAIN_RATE = 0.2
ADAM_EPS = 1e-08
MASKED = -1e30


def precise_product(left, right):
    return jnp.dot(left, right, precision=lax.Precision.HIGHEST)


def root_mean_square_norm(values, scaling):
    return values * lax.rsqrt(jnp.mean(values * values, axis=-1, keepdims=True) + EPS) * scaling


def rotary_embed(values, token_position):
    half_dim = values.shape[-1] // 2
    frequency = THETA ** (-jnp.arange(half_dim, dtype=jnp.float32) * 2.0 / values.shape[-1])
    angles = token_position.astype(jnp.float32)[:, None] * frequency[None, :]
    cosine = jnp.cos(angles)[:, None, :]
    sine_part = jnp.sin(angles)[:, None, :]
    lower_half = values[..., :half_dim]
    upper_half = values[..., half_dim:]
    return jnp.concatenate(
        [
            lower_half * cosine - upper_half * sine_part,
            upper_half * cosine + lower_half * sine_part,
        ],
        axis=-1,
    )


def sequence_layout(seq_lengths, every_row_packed):
    seq_ends = jnp.cumsum(seq_lengths)
    seq_starts = seq_ends - seq_lengths
    row_index = jnp.arange(every_row_packed, dtype=jnp.int32)
    segment = jnp.sum((row_index[:, None] >= seq_ends[None, :]).astype(jnp.int32), axis=1)
    chosen = segment[:, None] == jnp.arange(seq_lengths.shape[0], dtype=jnp.int32)[None, :]
    token_position = row_index - jnp.sum(jnp.where(chosen, seq_starts[None, :], 0), axis=1)
    return (segment, token_position)


def orthogonal(matrix):
    current = matrix / (jnp.sqrt(jnp.sum(matrix * matrix)) + 1e-07)
    for turn in range(NS_ITERS):
        gram = precise_product(current.T, current)
        poly = NS_B * gram + NS_C * precise_product(gram, gram)
        current = NS_A * current + precise_product(current, poly)
    return current


def orient(matrix, is_row):
    return matrix.T if is_row else matrix


def local(
    tokens,
    out_grad,
    lengths,
    w_query,
    key_weight,
    value_weight,
    w_output,
    w_gate,
    w_up,
    w_down,
    momentum_query,
    key_momentum_buffer,
    value_momentum_buffer,
    momentum_output,
    momentum_gate,
    momentum_up,
    momentum_down,
    gains,
    gain_first,
    gain_second,
):
    masters = (w_query, key_weight, value_weight, w_output, w_gate, w_up, w_down)
    moments = (
        momentum_query,
        key_momentum_buffer,
        value_momentum_buffer,
        momentum_output,
        momentum_gate,
        momentum_up,
        momentum_down,
    )
    rowwise = (False, False, False, True, False, False, True)
    rates = (
        1.0,
        1.0,
        1.0,
        math.sqrt(MODEL_WIDTH / (QUERY_HEADS * HEAD_SIZE // 16)),
        1.0,
        1.0,
        math.sqrt(MODEL_WIDTH / FF),
    )
    tensor_count = lax.axis_size("tensor")
    data_count = lax.axis_size("dp")
    tensor_index = lax.axis_index("tensor")
    tok_rows = tokens.shape[0]
    every_row_packed = tok_rows * tensor_count
    score_scale = HEAD_SIZE ** (-0.5)
    block_rows = min(512, every_row_packed)
    blocks = every_row_packed // block_rows
    lowered = tuple((matrix.astype(jnp.bfloat16) for matrix in masters))
    fetched = (
        lax.all_gather(lowered[0], "dp", axis=0, tiled=True),
        lax.all_gather(lowered[1], "dp", axis=0, tiled=True),
        lax.all_gather(lowered[2], "dp", axis=0, tiled=True),
        lax.all_gather(lowered[3], "dp", axis=1, tiled=True),
        lax.all_gather(lowered[4], "dp", axis=0, tiled=True),
        lax.all_gather(lowered[5], "dp", axis=0, tiled=True),
        lax.all_gather(lowered[6], "dp", axis=1, tiled=True),
    )
    query_full, key_full, value_full, output_full, gate_full, up_full, down_full = fetched
    q_heads = query_full.shape[1] // HEAD_SIZE
    kv_heads = key_full.shape[1] // HEAD_SIZE
    repeat_heads = q_heads // kv_heads
    segment, token_position = sequence_layout(lengths[0], every_row_packed)
    g_attn = gains[:MODEL_WIDTH]
    g_mlp = gains[MODEL_WIDTH : 2 * MODEL_WIDTH]
    query_gradient = gains[2 * MODEL_WIDTH : 2 * MODEL_WIDTH + HEAD_SIZE]
    g_key = gains[2 * MODEL_WIDTH + HEAD_SIZE :]
    inputs = tokens.astype(jnp.float32)
    first_normalized = lax.all_gather(
        root_mean_square_norm(inputs, g_attn).astype(jnp.bfloat16), "tensor", axis=0, tiled=True
    )
    query_raw = jnp.dot(first_normalized, query_full, preferred_element_type=jnp.float32)
    key_unrotated = jnp.dot(first_normalized, key_full, preferred_element_type=jnp.float32)
    value_projected = jnp.dot(first_normalized, value_full, preferred_element_type=jnp.float32)

    def prepare(product, scaling):
        return rotary_embed(
            root_mean_square_norm(product.reshape(every_row_packed, -1, HEAD_SIZE), scaling),
            token_position,
        )

    query_rotated = (
        prepare(query_raw, query_gradient)
        .astype(jnp.bfloat16)
        .reshape(every_row_packed, kv_heads, repeat_heads, HEAD_SIZE)
    )
    k_rot = prepare(key_unrotated, g_key).astype(jnp.bfloat16)
    v_low = value_projected.astype(jnp.bfloat16).reshape(every_row_packed, kv_heads, HEAD_SIZE)
    key_index = jnp.arange(every_row_packed, dtype=jnp.int32)

    def scores_for(block_index):
        first_row = block_index * block_rows
        q_block = lax.dynamic_slice_in_dim(query_rotated, first_row, block_rows, 0)
        product = (
            jnp.einsum("qkrd,skd->krqs", q_block, k_rot, preferred_element_type=jnp.float32)
            * score_scale
        )
        query_seg = lax.dynamic_slice_in_dim(segment, first_row, block_rows, 0)
        query_row = first_row + jnp.arange(block_rows, dtype=jnp.int32)
        allowed = (query_seg[:, None] == segment[None, :]) & (
            query_row[:, None] >= key_index[None, :]
        )
        return (q_block, jnp.where(allowed[None, None], product, MASKED))

    def attend(block_index):
        q_block, scores = scores_for(block_index)
        row_max = jnp.max(scores, axis=-1, keepdims=True)
        exponent = jnp.exp(scores - row_max)
        summed = jnp.sum(exponent, axis=-1, keepdims=True)
        probability = (exponent / summed).astype(jnp.bfloat16)
        out_block = jnp.einsum(
            "krqs,skd->qkrd", probability, v_low, preferred_element_type=jnp.float32
        )
        return (out_block, row_max + jnp.log(summed))

    attended, logsum = lax.map(attend, jnp.arange(blocks))
    attn_low = attended.reshape(every_row_packed, q_heads * HEAD_SIZE).astype(jnp.bfloat16)
    rows_part = attn_low
    branch_out = lax.psum_scatter(
        jnp.dot(rows_part, output_full, preferred_element_type=jnp.float32),
        "tensor",
        scatter_dimension=0,
        tiled=True,
    )
    hidden_in = inputs + branch_out
    n_two = lax.all_gather(
        root_mean_square_norm(hidden_in, g_mlp).astype(jnp.bfloat16), "tensor", axis=0, tiled=True
    )
    gate_act = jnp.dot(n_two, gate_full, preferred_element_type=jnp.float32)
    up_act = jnp.dot(n_two, up_full, preferred_element_type=jnp.float32)
    sigmoid_gate = jax.nn.sigmoid(gate_act)
    silu_gate = gate_act * sigmoid_gate
    inner_act = (silu_gate * up_act).astype(jnp.bfloat16)
    rows_part = inner_act
    mlp_out = lax.psum_scatter(
        jnp.dot(rows_part, down_full, preferred_element_type=jnp.float32),
        "tensor",
        scatter_dimension=0,
        tiled=True,
    )
    result = (hidden_in + mlp_out).astype(jnp.bfloat16)
    grad_rows = lax.all_gather(out_grad, "tensor", axis=0, tiled=True)
    d_hidden = jnp.einsum("gd,fd->gf", grad_rows, down_full, preferred_element_type=jnp.float32)
    grad_down = jnp.einsum("gf,gd->fd", inner_act, grad_rows, preferred_element_type=jnp.float32)
    d_gate = (d_hidden * up_act * sigmoid_gate * (1.0 + gate_act * (1.0 - sigmoid_gate))).astype(
        jnp.bfloat16
    )
    d_up = (d_hidden * silu_gate).astype(jnp.bfloat16)
    grad_gate = jnp.einsum("gd,gf->df", n_two, d_gate, preferred_element_type=jnp.float32)
    grad_up = jnp.einsum("gd,gf->df", n_two, d_up, preferred_element_type=jnp.float32)
    summed = jnp.einsum("gf,df->gd", d_gate, gate_full, preferred_element_type=jnp.float32)
    d_norm_two = lax.psum_scatter(
        summed + jnp.einsum("gf,df->gd", d_up, up_full, preferred_element_type=jnp.float32),
        "tensor",
        scatter_dimension=0,
        tiled=True,
    )
    _, norm_two_back = jax.vjp(root_mean_square_norm, hidden_in, g_mlp)
    d_hidden_in, dg_mlp = norm_two_back(d_norm_two)
    d_residual = out_grad.astype(jnp.float32) + d_hidden_in
    residual_rows = lax.all_gather(d_residual.astype(jnp.bfloat16), "tensor", axis=0, tiled=True)
    d_attended = jnp.einsum(
        "gd,cd->gc", residual_rows, output_full, preferred_element_type=jnp.float32
    )
    d_attended = d_attended.astype(jnp.bfloat16).reshape(
        every_row_packed, kv_heads, repeat_heads, HEAD_SIZE
    )
    grad_output = jnp.einsum(
        "gc,gd->cd", attn_low, residual_rows, preferred_element_type=jnp.float32
    )

    def attend_back(carry, block_index):
        key_sum, value_sum = carry
        q_block, scores = scores_for(block_index)
        d_block = lax.dynamic_slice_in_dim(d_attended, block_index * block_rows, block_rows, 0)
        probability = jnp.exp(scores - logsum[block_index])
        d_prob = jnp.einsum("qkrd,skd->krqs", d_block, v_low, preferred_element_type=jnp.float32)
        row_dot = jnp.sum(probability * d_prob, axis=-1, keepdims=True)
        d_score = (probability * (d_prob - row_dot)).astype(jnp.bfloat16)
        dq_block = (
            jnp.einsum("krqs,skd->qkrd", d_score, k_rot, preferred_element_type=jnp.float32)
            * score_scale
        )
        key_sum = (
            key_sum
            + jnp.einsum("krqs,qkrd->skd", d_score, q_block, preferred_element_type=jnp.float32)
            * score_scale
        )
        value_sum = value_sum + jnp.einsum(
            "krqs,qkrd->skd",
            probability.astype(jnp.bfloat16),
            d_block,
            preferred_element_type=jnp.float32,
        )
        return ((key_sum, value_sum), dq_block)

    empty_sum = jnp.zeros((every_row_packed, kv_heads, HEAD_SIZE), jnp.float32)
    (d_key_rot, d_value), d_query_rot = lax.scan(
        attend_back, (empty_sum, empty_sum), jnp.arange(blocks)
    )
    _, query_back = jax.vjp(prepare, query_raw, query_gradient)
    d_query, dg_query = query_back(d_query_rot.reshape(every_row_packed, q_heads, HEAD_SIZE))
    _, key_back = jax.vjp(prepare, key_unrotated, g_key)
    d_key, dg_key = key_back(d_key_rot)
    d_query = d_query.astype(jnp.bfloat16)
    d_key = d_key.astype(jnp.bfloat16)
    d_value = d_value.reshape(every_row_packed, kv_heads * HEAD_SIZE).astype(jnp.bfloat16)
    grad_query = jnp.einsum(
        "gd,gc->dc", first_normalized, d_query, preferred_element_type=jnp.float32
    )
    grad_key = jnp.einsum("gd,gc->dc", first_normalized, d_key, preferred_element_type=jnp.float32)
    grad_value = jnp.einsum(
        "gd,gc->dc", first_normalized, d_value, preferred_element_type=jnp.float32
    )
    summed = jnp.einsum("gc,dc->gd", d_query, query_full, preferred_element_type=jnp.float32)
    summed = summed + jnp.einsum("gc,dc->gd", d_key, key_full, preferred_element_type=jnp.float32)
    d_norm_one = lax.psum_scatter(
        summed + jnp.einsum("gc,dc->gd", d_value, value_full, preferred_element_type=jnp.float32),
        "tensor",
        scatter_dimension=0,
        tiled=True,
    )
    _, norm_one_back = jax.vjp(root_mean_square_norm, inputs, g_attn)
    d_inputs, dg_attn = norm_one_back(d_norm_one)
    tokens_grad = d_residual + d_inputs
    gain_grad = lax.psum(jnp.concatenate([dg_attn, dg_mlp, dg_query, dg_key]), ("dp", "tensor"))
    local_grads = (grad_query, grad_key, grad_value, grad_output, grad_gate, grad_up, grad_down)
    reduced = tuple(
        (
            lax.psum_scatter(local_grads[0], "dp", scatter_dimension=0, tiled=True),
            lax.psum_scatter(local_grads[1], "dp", scatter_dimension=0, tiled=True),
            lax.psum_scatter(local_grads[2], "dp", scatter_dimension=0, tiled=True),
            lax.psum_scatter(local_grads[3], "dp", scatter_dimension=1, tiled=True),
            lax.psum_scatter(local_grads[4], "dp", scatter_dimension=0, tiled=True),
            lax.psum_scatter(local_grads[5], "dp", scatter_dimension=0, tiled=True),
            lax.psum_scatter(local_grads[6], "dp", scatter_dimension=1, tiled=True),
        )
    )
    renewed = tuple((MOMENTUM * moment + gradient for moment, gradient in zip(moments, reduced)))
    oriented = [orient(matrix, is_row) for matrix, is_row in zip(renewed, rowwise)]
    pad_width = max((matrix.shape[1] for matrix in oriented))
    stacked = jnp.stack(
        [jnp.pad(matrix, ((0, 0), (0, pad_width - matrix.shape[1]))) for matrix in oriented]
    )
    owner_of = (jnp.arange(7, dtype=jnp.int32) + 7 * tensor_index) % data_count
    owners_hot = (owner_of[:, None] == jnp.arange(data_count, dtype=jnp.int32)[None, :]).astype(
        jnp.float32
    )
    outgoing = jnp.einsum("mo,mrp->orp", owners_hot, stacked, precision=lax.Precision.HIGHEST)
    incoming = lax.all_to_all(outgoing, "dp", split_axis=0, concat_axis=1, tiled=True)
    orthogonal_block = orthogonal(incoming[0])
    returned = lax.all_to_all(orthogonal_block[None], "dp", split_axis=1, concat_axis=0, tiled=True)
    my_blocks = jnp.einsum("mo,orp->mrp", owners_hot, returned, precision=lax.Precision.HIGHEST)
    updated = []
    for number in range(7):
        piece_cols = my_blocks[number][:, : oriented[number].shape[1]]
        updated.append(masters[number] - rates[number] * orient(piece_cols, rowwise[number]))
    renewed_first = BETA_ONE * gain_first + (1.0 - BETA_ONE) * gain_grad
    renewed_second = BETA_TWO * gain_second + (1.0 - BETA_TWO) * gain_grad * gain_grad
    corrected_first = renewed_first / (1.0 - BETA_ONE**ADAM_STEP)
    corrected_second = renewed_second / (1.0 - BETA_TWO**ADAM_STEP)
    updated_gains = gains - GAIN_RATE * corrected_first / (jnp.sqrt(corrected_second) + ADAM_EPS)
    return (
        result,
        tokens_grad,
        reduced[0],
        reduced[1],
        reduced[2],
        reduced[3],
        reduced[4],
        reduced[5],
        reduced[6],
        renewed[0],
        renewed[1],
        renewed[2],
        renewed[3],
        renewed[4],
        renewed[5],
        renewed[6],
        updated[0],
        updated[1],
        updated[2],
        updated[3],
        updated[4],
        updated[5],
        updated[6],
        gain_grad,
        renewed_first,
        renewed_second,
        updated_gains,
    )


def solution(mesh):
    placed = (
        P(("dp", "tensor"), None),
        P(("dp", "tensor"), None),
        P("dp", None),
        P("dp", "tensor"),
        P("dp", "tensor"),
        P("dp", "tensor"),
        P("tensor", "dp"),
        P("dp", "tensor"),
        P("dp", "tensor"),
        P("tensor", "dp"),
        P("dp", "tensor"),
        P("dp", "tensor"),
        P("dp", "tensor"),
        P("tensor", "dp"),
        P("dp", "tensor"),
        P("dp", "tensor"),
        P("tensor", "dp"),
        P(),
        P(),
        P(),
    )
    return jax.shard_map(
        local,
        mesh=mesh,
        in_specs=placed,
        out_specs=(
            P(("dp", "tensor"), None),
            P(("dp", "tensor"), None),
            P("dp", "tensor"),
            P("dp", "tensor"),
            P("dp", "tensor"),
            P("tensor", "dp"),
            P("dp", "tensor"),
            P("dp", "tensor"),
            P("tensor", "dp"),
            P("dp", "tensor"),
            P("dp", "tensor"),
            P("dp", "tensor"),
            P("tensor", "dp"),
            P("dp", "tensor"),
            P("dp", "tensor"),
            P("tensor", "dp"),
            P("dp", "tensor"),
            P("dp", "tensor"),
            P("dp", "tensor"),
            P("tensor", "dp"),
            P("dp", "tensor"),
            P("dp", "tensor"),
            P("tensor", "dp"),
            P(),
            P(),
            P(),
            P(),
        ),
        check_vma=False,
    )
```

profile of v0, /device:TPU:30, one launch (start us, length us, event | category | flops | bytes accessed | tf_op | source)
XLA Modules:
  0.0 1264.9 jit_solution(14604089973582880078)
XLA Ops:
  17.0 21.5 %all_gather.36 = bf16[1024,128]{1,0:T(8,128)(2,1)} all-gather(bf16[64,128]{1,0:T(8,128)(2,1)S(1)} %convert_element_type.130), channel_id=1, replica_groups=mesh['dp'=16,'tensor'=8] {'dp'}, dimensions={0}, use_global_device_ids=true | all-gather | bytes 278528 | tf_op jit(solution)/shard_map/all_gather | solution.py:131
  38.5 22.6 %all_gather.35 = bf16[1024,128]{1,0:T(8,128)(2,1)S(1)} all-gather(bf16[64,128]{1,0:T(8,128)(2,1)S(1)} %convert_element_type.129), channel_id=1, replica_groups=mesh['dp'=16,'tensor'=8] {'dp'}, dimensions={0}, use_global_device_ids=true | all-gather | bytes 278528 | tf_op jit(solution)/shard_map/all_gather | solution.py:130
  61.9 22.3 %all_gather.37 = bf16[256,1024]{0,1:T(8,128)(2,1)} all-gather(bf16[256,64]{0,1:T(8,128)(2,1)S(1)} %convert_element_type.134), channel_id=1, replica_groups=mesh['dp'=16,'tensor'=8] {'dp'}, dimensions={1}, use_global_device_ids=true | all-gather | bytes 557056 | tf_op jit(solution)/shard_map/all_gather | solution.py:132
  84.1 22.0 %all_gather.34 = bf16[1024,256]{1,0:T(8,128)(2,1)S(1)} all-gather(bf16[64,256]{1,0:T(8,128)(2,1)S(1)} %convert_element_type.127), channel_id=1, replica_groups=mesh['dp'=16,'tensor'=8] {'dp'}, dimensions={0}, use_global_device_ids=true | all-gather | bytes 557056 | tf_op jit(solution)/shard_map/all_gather | solution.py:129
  106.2 3.0 multiply_cosine_fusion
  120.0 13.4 %while.28 = (s32[]{:T(128)}, bf16[2,512,1,2,128]{4,1,3,2,0:T(8,128)(2,1)}, f32[2,1,2,512,1]{3,2,4,1,0:T(2,128)S(1)}, s32[2]{0:T(128)S(1)}, s32[1024]{0:T(1024)S(...) while((s32[]{:T(128)}, ...), condition=%wide.region_9.10_spmd.clone, body=%wide.region_6.9_spmd.clone.sunk | while | flops 551026176 | bytes 20232452 | solution.py:194
  135.9 3.8 fusion.90
  139.8 91.8 %reduce-scatter.12.cloned.1.call-done = f32[128,1024]{1,0:T(8,128)} async-done(((f32[1024,1024]{1,0:T(8,128)}), f32[128,1024]{1,0:T(8,128)}) %reduce-scatter.12.cloned.1.call-update) | async-done | bytes 524304 | tf_op jit(solution)/shard_map/reduce_scatter | solution.py:197
  237.3 22.8 %all_gather.41 = bf16[384,1024]{0,1:T(8,128)(2,1)} all-gather(bf16[384,64]{0,1:T(8,128)(2,1)S(1)} %convert_element_type.139), channel_id=1, replica_groups=mesh['dp'=16,'tensor'=8] {'dp'}, dimensions={1}, use_global_device_ids=true | all-gather | bytes 835584 | tf_op jit(solution)/shard_map/all_gather | solution.py:135
  260.0 26.1 %all_gather.40 = bf16[1024,384]{1,0:T(8,128)(2,1)} all-gather(bf16[64,384]{1,0:T(8,128)(2,1)S(1)} %convert_element_type.137), channel_id=1, replica_groups=mesh['dp'=16,'tensor'=8] {'dp'}, dimensions={0}, use_global_device_ids=true | all-gather | bytes 835584 | tf_op jit(solution)/shard_map/all_gather | solution.py:134
  286.1 36.0 %all_gather.39 = bf16[1024,384]{1,0:T(8,128)(2,1)} all-gather(bf16[64,384]{1,0:T(8,128)(2,1)S(1)} %convert_element_type.136), channel_id=1, replica_groups=mesh['dp'=16,'tensor'=8] {'dp'}, dimensions={0}, use_global_device_ids=true | all-gather | bytes 835584 | tf_op jit(solution)/shard_map/all_gather | solution.py:133
  322.1 4.3 fusion.135
  328.9 21.0 %all-gather.9.cloned.1.call-done = bf16[1024,1024]{1,0:T(8,128)(2,1)} async-done(((bf16[128,1024]{1,0:T(8,128)(2,1)}), bf16[1024,1024]{1,0:T(8,128)(2,1)}) %all-gather.9.cloned.1.call-update) | async-done | bytes 2097168 | tf_op jit(solution)/shard_map/all_gather | solution.py:220
  349.9 5.5 multiply_convert_fusion
  357.1 3.2 convolution_add_fusion
  360.4 90.0 %reduce-scatter.16.cloned.1.call-done = f32[128,1024]{1,0:T(8,128)} async-done(((f32[1024,1024]{1,0:T(8,128)}), f32[128,1024]{1,0:T(8,128)}) %reduce-scatter.16.cloned.1.call-update) | async-done | bytes 524304 | tf_op jit(solution)/shard_map/reduce_scatter | solution.py:230
  455.0 51.5 %all-gather.11.cloned.1.call-done = bf16[1024,1024]{1,0:T(8,128)(2,1)} async-done(((bf16[128,1024]{1,0:T(8,128)(2,1)}), bf16[1024,1024]{1,0:T(8,128)(2,1)}) %all-gather.11.cloned.1.call-update) | async-done | bytes 2097168 | tf_op jit(solution)/shard_map/all_gather | solution.py:239
  506.5 3.2 convolution_convert_fusion
  510.2 26.9 %while.29 = (s32[]{:T(128)}, f32[1024,1,128]{0,2,1:T(8,128)S(1)}, f32[1024,1,128]{0,2,1:T(8,128)}, f32[2,512,1,2,128]{4,1,0,3,2:T(8,128)}, s32[2]{0:T(128)}, /*i...) while((s32[]{:T(128)}, f32[1024,1,128]{0,2,1:T(8,128)S(1)}, ...), condition=%wide.region_17.18_spmd.clone, body=%wide.region_15.17_spmd.clone.sunk | while | flops 1360264704 | bytes 53782984 | solution.py:276
  548.7 2.9 fusion.74
  554.7 3.6 fusion.88
  558.8 4.1 fusion.142
  562.9 4.2 fusion.143
  567.2 4.1 fusion.144
  573.4 2.8 add_add_fusion
  576.3 32.4 %reduce-scatter.22.cloned.1.call-done = f32[64,128]{1,0:T(8,128)} async-done(((f32[1024,128]{1,0:T(8,128)}), f32[64,128]{1,0:T(8,128)}) %reduce-scatter.22.cloned.1.call-update) | async-done | bytes 32784 | tf_op jit(solution)/shard_map/reduce_scatter | solution.py:309
  609.5 68.5 %reduce-scatter.24.cloned.1.call-done = f32[64,128]{1,0:T(8,128)} async-done(((f32[1024,128]{1,0:T(8,128)}), f32[64,128]{1,0:T(8,128)}) %reduce-scatter.24.cloned.1.call-update) | async-done | bytes 32784 | tf_op jit(solution)/shard_map/reduce_scatter | solution.py:310
  678.7 69.5 %reduce-scatter.20.cloned.1.call-done = f32[64,256]{1,0:T(8,128)} async-done(((f32[1024,256]{1,0:T(8,128)}), f32[64,256]{1,0:T(8,128)}) %reduce-scatter.20.cloned.1.call-update) | async-done | bytes 65552 | tf_op jit(solution)/shard_map/reduce_scatter | solution.py:308
  749.1 69.7 %reduce-scatter.26.cloned.1.call-done = f32[256,64]{0,1:T(8,128)} async-done(((f32[256,1024]{0,1:T(8,128)}), f32[256,64]{0,1:T(8,128)}) %reduce-scatter.26.cloned.1.call-update) | async-done | bytes 65552 | tf_op jit(solution)/shard_map/reduce_scatter | solution.py:311
  819.7 71.4 %reduce-scatter.28.cloned.1.call-done = f32[64,384]{1,0:T(8,128)} async-done(((f32[1024,384]{1,0:T(8,128)}), f32[64,384]{1,0:T(8,128)}) %reduce-scatter.28.cloned.1.call-update) | async-done | bytes 98320 | tf_op jit(solution)/shard_map/reduce_scatter | solution.py:312
  892.7 70.6 %reduce-scatter.30.cloned.1.call-done = f32[64,384]{1,0:T(8,128)} async-done(((f32[1024,384]{1,0:T(8,128)}), f32[64,384]{1,0:T(8,128)}) %reduce-scatter.30.cloned.1.call-update) | async-done | bytes 98320 | tf_op jit(solution)/shard_map/reduce_scatter | solution.py:313
  964.9 70.7 %reduce-scatter.32.cloned.1.call-done = f32[384,64]{0,1:T(8,128)} async-done(((f32[384,1024]{0,1:T(8,128)}), f32[384,64]{0,1:T(8,128)}) %reduce-scatter.32.cloned.1.call-update) | async-done | bytes 98320 | tf_op jit(solution)/shard_map/reduce_scatter | solution.py:314
  1040.1 5.5 all-to-all-start
  1045.8 3.3 fusion.136
  1049.1 29.7 %all-to-all-done = f32[16,64,384]{2,1,0:T(8,128)S(1)} async-done(((f32[16,64,384]{2,1,0:T(8,128)}), f32[16,64,384]{2,1,0:T(8,128)S(1)}, u32[]{:S(2)}, u32[]{:S(2)}) %all-to-all-start) | async-done | bytes 1572896 | tf_op jit(solution)/shard_map/all_to_all | solution.py:328
  1081.5 2.8 convolution_bitcast_fusion.1
  1086.1 3.2 multiply_add_fusion.3
  1089.3 3.0 fusion.145
  1093.6 3.2 multiply_add_fusion.2
  1096.9 2.8 fusion.146
  1100.9 3.6 multiply_add_fusion.1
  1104.6 2.8 fusion.147
  1108.6 3.2 multiply_add_fusion
  1111.9 2.8 fusion.148
  1116.0 3.3 add_bitcast_fusion
  1120.9 34.2 %all_to_all.21 = f32[1,1024,384]{2,0,1:T(1,128)S(1)} all-to-all(f32[1,1024,384]{2,0,1:T(1,128)S(1)} %copy.123), channel_id=1, replica_groups=mesh['dp'=16,'tensor'=8] {'dp'}, dimensions={1} | all-to-all | bytes 3145728 | tf_op jit(solution)/shard_map/all_to_all | solution.py:330
  1162.7 77.9 %psum.7 = f32[2304]{0:T(1024)S(1)} all-reduce(f32[2304]{0:T(1024)S(1)} %pad_maximum_fusion.2), channel_id=1, replica_groups=mesh['dp'=16,'tensor'=8] {'dp','tensor'}, use_global_device_ids=true, to_apply=%region_34.35 | all-reduce | flops 2304 | bytes 18432 | tf_op jit(solution)/shard_map/psum | solution.py:304
  1241.3 14.5 %reduce-scatter.14.cloned.1.call-done = f32[128,1024]{1,0:T(8,128)} async-done(((f32[1024,1024]{1,0:T(8,128)}), f32[128,1024]{1,0:T(8,128)}) %reduce-scatter.14.cloned.1.call-update) | async-done | bytes 524304 | tf_op jit(solution)/shard_map/reduce_scatter | solution.py:213
  (354 shorter events, 121.2 us)
Async XLA Ops:
  7.2 102.0 %all-gather.5.cloned.1.call-start = ((), (), s32[]{:S(2)}) async-start(), calls=%async_computation.13 | async-start | bytes 2359296 | tf_op jit(solution)/shard_map/all_gather | solution.py:147
  12.0 219.6 %reduce-scatter.12.cloned.1.call-start = ((), (), s32[]{:S(2)}) async-start(), calls=%async_computation.14 | async-start | bytes 4718592 | tf_op jit(solution)/shard_map/reduce_scatter | solution.py:197
  16.1 95.6 %copy-start.75 = (f32[64]{0:T(128)}, f32[64]{0:T(128)S(1)}, u32[]{:S(2)}) copy-start(f32[64]{0:T(128)S(1)} %multiply_power_fusion) | copy-start | bytes 772
  61.1 48.1 %copy-start.33 = (bf16[1024,128]{1,0:T(8,128)(2,1)}, bf16[1024,128]{1,0:T(8,128)(2,1)S(1)}, u32[]{:S(2)}) copy-start(bf16[1024,128]{1,0:T(8,128)(2,1)S(1)} %all_gather.35) | copy-start | bytes 786436
  61.9 49.8 %copy-start.67 = (f32[128]{0:T(128)}, f32[128]{0:T(128)S(1)}, u32[]{:S(2)}) copy-start(f32[128]{0:T(128)S(1)} %get-tuple-element.378) | copy-start | bytes 1540
  61.9 54.9 %copy-start.71 = (f32[128]{0:T(128)}, f32[128]{0:T(128)S(1)}, u32[]{:S(2)}) copy-start(f32[128]{0:T(128)S(1)} %get-tuple-element.379) | copy-start | bytes 1540
  106.2 7.0 copy-start.12
  133.4 6.3 copy-start.5
  139.7 95.7 %copy-start.43 = (f32[64,384]{1,0:T(8,128)S(1)}, f32[64,384]{1,0:T(8,128)}, u32[]{:S(2)}) copy-start(f32[64,384]{1,0:T(8,128)} %param.31) | copy-start | bytes 294916
  139.7 182.4 %all-gather.7.cloned.1.call-start = ((), (), s32[]{:S(2)}) async-start(), calls=%async_computation.15 | async-start | bytes 2359296 | tf_op jit(solution)/shard_map/all_gather | solution.py:204
  232.9 219.4 %copy-start.3 = (f32[128,1024]{1,0:T(8,128)}, f32[128,1024]{1,0:T(8,128)S(1)}, u32[]{:S(2)}) copy-start(f32[128,1024]{1,0:T(8,128)S(1)} %get-tuple-element.351) | copy-start | bytes 1572868
  234.8 115.1 %all-gather.9.cloned.1.call-start = ((), (), s32[]{:S(2)}) async-start(), calls=%async_computation.17 | async-start | bytes 2359296 | tf_op jit(solution)/shard_map/all_gather | solution.py:220
  235.4 215.1 %reduce-scatter.16.cloned.1.call-start = ((), (), s32[]{:S(2)}) async-start(), calls=%async_computation.18 | async-start | bytes 4718592 | tf_op jit(solution)/shard_map/reduce_scatter | solution.py:230
  360.4 146.1 %all-gather.11.cloned.1.call-start = ((), (), s32[]{:S(2)}) async-start(), calls=%async_computation.19 | async-start | bytes 2359296 | tf_op jit(solution)/shard_map/all_gather | solution.py:239
  454.9 153.8 %reduce-scatter.22.cloned.1.call-start = ((), (), s32[]{:S(2)}) async-start(), calls=%async_computation.22 | async-start | bytes 557056 | tf_op jit(solution)/shard_map/reduce_scatter | solution.py:309
  542.5 135.5 %reduce-scatter.24.cloned.1.call-start = ((), (), s32[]{:S(2)}) async-start(), calls=%async_computation.23 | async-start | bytes 557056 | tf_op jit(solution)/shard_map/reduce_scatter | solution.py:310
  548.6 199.6 %reduce-scatter.20.cloned.1.call-start = ((), (), s32[]{:S(2)}) async-start(), calls=%async_computation.21 | async-start | bytes 1114112 | tf_op jit(solution)/shard_map/reduce_scatter | solution.py:308
  554.6 264.2 %reduce-scatter.26.cloned.1.call-start = ((), (), s32[]{:S(2)}) async-start(), calls=%async_computation.24 | async-start | bytes 1114112 | tf_op jit(solution)/shard_map/reduce_scatter | solution.py:311
  558.3 332.8 %reduce-scatter.28.cloned.1.call-start = ((), (), s32[]{:S(2)}) async-start(), calls=%async_computation.25 | async-start | bytes 1671168 | tf_op jit(solution)/shard_map/reduce_scatter | solution.py:312
  562.9 400.5 %reduce-scatter.30.cloned.1.call-start = ((), (), s32[]{:S(2)}) async-start(), calls=%async_computation.26 | async-start | bytes 1671168 | tf_op jit(solution)/shard_map/reduce_scatter | solution.py:313
  567.1 468.5 %reduce-scatter.32.cloned.1.call-start = ((), (), s32[]{:S(2)}) async-start(), calls=%async_computation.27 | async-start | bytes 1671168 | tf_op jit(solution)/shard_map/reduce_scatter | solution.py:314
  571.3 590.2 %reduce-scatter.18.cloned.1.call-start = ((), (), s32[]{:S(2)}) async-start(), calls=%async_computation.20 | async-start | bytes 4718592 | tf_op jit(solution)/shard_map/reduce_scatter | solution.py:295
  576.2 32.5 %copy-start.63 = (f32[64,128]{1,0:T(8,128)S(1)}, f32[64,128]{1,0:T(8,128)}, u32[]{:S(2)}) copy-start(f32[64,128]{1,0:T(8,128)} %param.35) | copy-start | bytes 98308
  576.2 101.8 %copy-start.64 = (f32[64,128]{1,0:T(8,128)S(1)}, f32[64,128]{1,0:T(8,128)}, u32[]{:S(2)}) copy-start(f32[64,128]{1,0:T(8,128)} %param.36) | copy-start | bytes 98308
  576.2 172.0 %copy-start.59 = (f32[64,256]{1,0:T(8,128)S(1)}, f32[64,256]{1,0:T(8,128)}, u32[]{:S(2)}) copy-start(f32[64,256]{1,0:T(8,128)} %param.34) | copy-start | bytes 196612
  576.2 242.6 %copy-start.60 = (f32[256,64]{0,1:T(8,128)S(1)}, f32[256,64]{0,1:T(8,128)}, u32[]{:S(2)}) copy-start(f32[256,64]{0,1:T(8,128)} %param.37) | copy-start | bytes 196612
  576.2 314.9 %copy-start.54 = (f32[64,384]{1,0:T(8,128)S(1)}, f32[64,384]{1,0:T(8,128)}, u32[]{:S(2)}) copy-start(f32[64,384]{1,0:T(8,128)} %param.38) | copy-start | bytes 294916
  576.2 387.1 %copy-start.55 = (f32[64,384]{1,0:T(8,128)S(1)}, f32[64,384]{1,0:T(8,128)}, u32[]{:S(2)}) copy-start(f32[64,384]{1,0:T(8,128)} %param.39) | copy-start | bytes 294916
  576.2 459.4 %copy-start.56 = (f32[384,64]{0,1:T(8,128)S(1)}, f32[384,64]{0,1:T(8,128)}, u32[]{:S(2)}) copy-start(f32[384,64]{0,1:T(8,128)} %param.40) | copy-start | bytes 294916
  609.5 429.0 %copy-start.52 = (f32[64,128]{1,0:T(8,128)}, f32[64,128]{1,0:T(8,128)S(1)}, u32[]{:S(2)}) copy-start(f32[64,128]{1,0:T(8,128)S(1)} %multiply_add_fusion.12) | copy-start | bytes 98308
  678.7 359.7 %copy-start.53 = (f32[64,128]{1,0:T(8,128)}, f32[64,128]{1,0:T(8,128)S(1)}, u32[]{:S(2)}) copy-start(f32[64,128]{1,0:T(8,128)S(1)} %multiply_add_fusion.11) | copy-start | bytes 98308
  749.1 289.4 %copy-start.48 = (f32[64,256]{1,0:T(8,128)}, f32[64,256]{1,0:T(8,128)S(1)}, u32[]{:S(2)}) copy-start(f32[64,256]{1,0:T(8,128)S(1)} %multiply_add_fusion.10) | copy-start | bytes 196612
  819.7 220.4 %copy-start.49 = (f32[256,64]{0,1:T(8,128)}, f32[256,64]{0,1:T(8,128)S(1)}, u32[]{:S(2)}) copy-start(f32[256,64]{0,1:T(8,128)S(1)} %multiply_add_fusion.9) | copy-start | bytes 196612
  1040.1 5.7 copy-start.27
  1040.1 38.8 %all-to-all-start = ((f32[16,64,384]{2,1,0:T(8,128)}), f32[16,64,384]{2,1,0:T(8,128)S(1)}, u32[]{:S(2)}, u32[]{:S(2)}) async-start(f32[16,64,384]{2,1,0:T(8,128)} %copy.120), calls=%async_computation.11 | async-start | bytes 3145728 | tf_op jit(solution)/shard_map/all_to_all | solution.py:328
  1045.6 210.2 %reduce-scatter.14.cloned.1.call-start = ((), (), s32[]{:S(2)}) async-start(), calls=%async_computation.16 | async-start | bytes 4718592 | tf_op jit(solution)/shard_map/reduce_scatter | solution.py:213
  1156.8 5.8 copy-start.76
  1156.8 5.8 copy-start.79
  1156.9 83.8 %copy-start.81 = (f32[128]{0:T(128)S(1)}, f32[128]{0:T(128)}, u32[]{:S(2)}) copy-start(f32[128]{0:T(128)} %copy-done.80) | copy-start | bytes 1540
  1156.9 83.8 %copy-start.62 = (f32[2304]{0:T(1024)S(1)}, f32[2304]{0:T(1024)}, u32[]{:S(2)}) copy-start(f32[2304]{0:T(1024)} %param.41) | copy-start | bytes 27652
  1156.9 83.8 %copy-start.65 = (f32[2304]{0:T(1024)S(1)}, f32[2304]{0:T(1024)}, u32[]{:S(2)}) copy-start(f32[2304]{0:T(1024)} %param.43) | copy-start | bytes 27652
  1156.9 83.8 %copy-start.66 = (f32[2304]{0:T(1024)S(1)}, f32[2304]{0:T(1024)}, u32[]{:S(2)}) copy-start(f32[2304]{0:T(1024)} %param.42) | copy-start | bytes 27652
  1156.9 98.9 %copy-start.4 = (f32[128,1024]{1,0:T(8,128)S(1)}, f32[128,1024]{1,0:T(8,128)}, u32[]{:S(2)}) copy-start(f32[128,1024]{1,0:T(8,128)} %copy-done.3) | copy-start | bytes 1572868
  1156.9 98.9 %copy-start.16 = (f32[128,1024]{1,0:T(8,128)S(1)}, f32[128,1024]{1,0:T(8,128)}, u32[]{:S(2)}) copy-start(f32[128,1024]{1,0:T(8,128)} %reduce-scatter.16.cloned.1.call-done) | copy-start | bytes 1572868
  1156.9 98.9 %copy-start.32 = (bf16[128,1024]{1,0:T(8,128)(2,1)S(1)}, bf16[128,1024]{1,0:T(8,128)(2,1)}, u32[]{:S(2)}) copy-start(bf16[128,1024]{1,0:T(8,128)(2,1)} %param.25) | copy-start | bytes 786436
  1156.9 98.9 %copy-start.70 = (f32[128]{0:T(128)S(1)}, f32[128]{0:T(128)}, u32[]{:S(2)}) copy-start(f32[128]{0:T(128)} %copy-done.69) | copy-start | bytes 1540
  1156.9 98.9 %copy-start.78 = (f32[128]{0:T(128)S(1)}, f32[128]{0:T(128)}, u32[]{:S(2)}) copy-start(f32[128]{0:T(128)} %copy-done.77) | copy-start | bytes 1540
  1240.6 17.5 %copy-start.61 = (f32[2304]{0:T(1024)}, f32[2304]{0:T(1024)S(1)}, u32[]{:S(2)}) copy-start(f32[2304]{0:T(1024)S(1)} %psum.7) | copy-start | bytes 27652
  (60 other events, 134.6 us)
Sparse Core Ops, SparseCore 0:
  12.1 55.5 all-gather.4
  139.8 91.7 reduce-scatter.11
  234.9 56.3 all-gather.6
  292.8 57.0 all-gather.8
  360.5 89.9 reduce-scatter.15
  455.0 51.3 all-gather.10
  542.6 66.0 reduce-scatter.21
  613.5 64.4 reduce-scatter.23
  682.4 65.8 reduce-scatter.19
  752.9 65.8 reduce-scatter.25
  823.3 67.8 reduce-scatter.27
  895.4 67.8 reduce-scatter.29
  967.8 67.8 reduce-scatter.31
  1037.9 122.9 reduce-scatter.17
  1163.2 92.5 reduce-scatter.13
where the time goes:
time: 1280 us; the launch traced here: 1260 us
  waiting for transfers between devices  752 us (59%)
  blocking collectives  285 us (22%)
  matrix products  113 us (9%)
  other arithmetic  56.9 us (4%)
  local copies, waits for them, and re-layouts  27.8 us (2%)
  between operations  15.9 us (1%)
    reduce_scatter x1, waiting for transfers between devices, local(): lax.psum_scatter(jnp.dot(rows_part, output_full, preferred_element_type=j...  91.8 us
    reduce_scatter x1, waiting for transfers between devices, local(): lax.psum_scatter(summed + jnp.einsum('gf,df->gd', d_up, up_full, preferre...  90 us
    psum x1, blocking collectives, local(): lax.psum(jnp.concatenate([dg_attn, dg_mlp, dg_query, dg_key]), ('dp', 'te...  77.9 us
    reduce_scatter x1, waiting for transfers between devices, local(): lax.psum_scatter(local_grads[4], 'dp', scatter_dimension=0, tiled=True)  71.4 us
    reduce_scatter x1, waiting for transfers between devices, local(): lax.psum_scatter(local_grads[6], 'dp', scatter_dimension=1, tiled=True)  70.7 us
    reduce_scatter x1, waiting for transfers between devices, local(): lax.psum_scatter(local_grads[5], 'dp', scatter_dimension=0, tiled=True)  70.6 us
    reduce_scatter x1, waiting for transfers between devices, local(): lax.psum_scatter(local_grads[3], 'dp', scatter_dimension=1, tiled=True)  69.7 us
    reduce_scatter x1, waiting for transfers between devices, local(): lax.psum_scatter(local_grads[0], 'dp', scatter_dimension=0, tiled=True)  69.5 us
  transfers between devices with their start and end apart: 16, of which 13 were waited for; matrix products, arithmetic and copies ran while one was open for 9% of the time, Pallas kernels for 0%

commit v1 on v0

v1 whole, which is shorter than its diff:
```python
import math

import jax
import jax.numpy as jnp
from jax import lax
from jax.experimental import pallas as pl
from jax.experimental.pallas import tpu as pltpu
from jax.sharding import PartitionSpec as P

MODEL_WIDTH = 1024
QUERY_HEADS = 16
HEAD_SIZE = 128
FF = 3072
NS_ITERS = 5
ADAM_STEP = 10
TENSOR = 8
DATA = 16
ROWS = 128
SHARD = 64
BF = jnp.bfloat16
F32 = jnp.float32


EPS = 1e-06
THETA = 1000000.0
NS_A = 3.4445
NS_B = -4.775
NS_C = 2.0315
MOMENTUM = 0.95
BETA_ONE = 0.9
BETA_TWO = 0.95
GAIN_RATE = 0.2
ADAM_EPS = 1e-08
MASKED = -1e30


def root_mean_square_norm(values, scaling):
    return values * lax.rsqrt(jnp.mean(values * values, axis=-1, keepdims=True) + EPS) * scaling


def rotary_embed(values, token_position):
    half_dim = values.shape[-1] // 2
    frequency = THETA ** (-jnp.arange(half_dim, dtype=jnp.float32) * 2.0 / values.shape[-1])
    angles = token_position.astype(jnp.float32)[:, None] * frequency[None, :]
    cosine = jnp.cos(angles)[:, None, :]
    sine_part = jnp.sin(angles)[:, None, :]
    lower_half = values[..., :half_dim]
    upper_half = values[..., half_dim:]
    return jnp.concatenate(
        [
            lower_half * cosine - upper_half * sine_part,
            upper_half * cosine + lower_half * sine_part,
        ],
        axis=-1,
    )


def sequence_layout(seq_lengths, row_index):
    seq_ends = jnp.cumsum(seq_lengths)
    seq_starts = seq_ends - seq_lengths
    segment = jnp.sum((row_index[:, None] >= seq_ends[None, :]).astype(jnp.int32), axis=1)
    chosen = segment[:, None] == jnp.arange(seq_lengths.shape[0], dtype=jnp.int32)[None, :]
    token_position = row_index - jnp.sum(jnp.where(chosen, seq_starts[None, :], 0), axis=1)
    return (segment, token_position)


def whole_specs(number):
    return [pl.BlockSpec(memory_space=pltpu.VMEM)] * number


TURN_Z = ("tensor", [(t, t ^ 1) for t in range(TENSOR)])
UP_X = ("tensor", [(t, (t + 2) % TENSOR) for t in range(TENSOR)])
DOWN_X = ("tensor", [(t, (t - 2) % TENSOR) for t in range(TENSOR)])
TURN_CORE = ("dp", [(d, d ^ 1) for d in range(DATA)])
TURN_FAR = ("dp", [(d, d ^ 8) for d in range(DATA)])
TURN_BOTH = ("dp", [(d, d ^ 9) for d in range(DATA)])
UP_Y = ("dp", [(d, d // 8 * 8 + (d + 2) % 8) for d in range(DATA)])
DOWN_Y = ("dp", [(d, d // 8 * 8 + (d - 2) % 8) for d in range(DATA)])
OVER_TENSOR = (TURN_Z, UP_X, DOWN_X)
OVER_DATA = (TURN_FAR, UP_Y, DOWN_Y)
STEPS = (0, 0, -1, -1, 1, 1, 2, 2)


def send(block, link):
    return lax.ppermute(block, link[0], link[1])


def ring_spread(pair, up, down):
    half = pair.shape[0] // 2
    below = send(pair, up)
    above = send(pair, down)
    return [below, above, send(below[:half], up), send(above[half:], down)]


def ring_gather(block, links):
    turn, up, down = links
    pair = jnp.concatenate([block, send(block, turn)], axis=0)
    return [pair] + ring_spread(pair, up, down)


def ring_scatter(partial, rows, links):
    turn, up, down = links

    def slot(first, count=1):
        return partial[first * rows : (first + count) * rows]

    low = send(slot(6).astype(BF), down)
    high = send(slot(7).astype(BF), up)
    to_low = jnp.concatenate([slot(2) + low.astype(F32), slot(3).astype(F32)], axis=0).astype(BF)
    to_high = jnp.concatenate([slot(4).astype(F32), slot(5) + high.astype(F32)], axis=0).astype(BF)
    summed = slot(0, 2) + send(to_low, down).astype(F32) + send(to_high, up).astype(F32)
    return summed[:rows] + send(summed[rows:].astype(BF), turn).astype(F32)


def gather_tensor(block):
    return jnp.concatenate(ring_gather(block, OVER_TENSOR), axis=0)


def scatter_tensor(partial):
    return ring_scatter(partial, ROWS, OVER_TENSOR)


def slot_place(me, slot, core):
    far = jnp.bitwise_xor(me // 8, slot % 2)
    row = lax.rem(lax.rem(me // 2, 4) + STEPS[slot] + 4, 4)
    return pl.multiple_of((far * 8 + row * 2 + core) * SHARD, SHARD)


def place_kernel(me_ref, *refs):
    *near, other, out = refs
    me = me_ref[0]
    core = lax.rem(me, 2)
    slot = 0
    for part in near:
        for at in range(0, part.shape[0], SHARD):
            out[pl.ds(slot_place(me, slot, core), SHARD), :] = part[at : at + SHARD]
            out[pl.ds(slot_place(me, slot, 1 - core), SHARD), :] = other[
                slot * SHARD : (slot + 1) * SHARD
            ]
            slot += 1


def gather_data(block, me):
    near = ring_gather(block, OVER_DATA)
    other = send(jnp.concatenate(near, axis=0), TURN_CORE)
    return pl.pallas_call(
        place_kernel,
        in_specs=[pl.BlockSpec(memory_space=pltpu.SMEM)] + whole_specs(len(near) + 1),
        out_specs=whole_specs(1)[0],
        out_shape=jax.ShapeDtypeStruct((DATA * SHARD, block.shape[1]), BF),
        compiler_params=pltpu.CompilerParams(vmem_limit_bytes=32 * 2**20),
        name="place_weights",
    )(me, *near, other)


def split_kernel(me_ref, whole_ref, keep_ref, send_ref):
    me = me_ref[0]
    core = lax.rem(me, 2)
    for slot in range(8):
        at = slice(slot * SHARD, (slot + 1) * SHARD)
        keep_ref[at] = whole_ref[pl.ds(slot_place(me, slot, core), SHARD), :]
        send_ref[at] = whole_ref[pl.ds(slot_place(me, slot, 1 - core), SHARD), :].astype(BF)


SCALAR = pl.BlockSpec(memory_space=pltpu.SMEM)
BLOCK = 256
ALL_ROWS = TENSOR * ROWS
SCORE_SCALE = HEAD_SIZE**-0.5


def cost(flops, moved):
    return pl.CostEstimate(flops=int(flops), bytes_accessed=int(moved), transcendentals=0)


def room(megabytes):
    return pltpu.CompilerParams(vmem_limit_bytes=megabytes * 2**20)


def inverse_size(values):
    return lax.rsqrt(jnp.mean(values * values, axis=-1, keepdims=True) + EPS)


def scores_of(keys, queries, key_row, query_row, query_start):
    product = dot_f32(keys, queries, ((1,), (1,))) * SCORE_SCALE
    allowed = (key_row >= query_start) & (key_row <= query_row)
    return jnp.where(allowed, product, MASKED)


def forward_kernel(
    rows_ref, weight_ref, out_weight_ref, cos_ref, sin_ref, gain_ref, key_row_ref, row_ref, start_ref,
    raw_ref, low_ref, attended_ref, log_ref, part_ref, value_t,
):
    def project(block, carry):
        at = pl.ds(pl.multiple_of(block * BLOCK, BLOCK), BLOCK)
        product = dot_f32(rows_ref[at, :], weight_ref[...], ((1,), (0,)))
        raw_ref[at, :] = product
        cosine, sine = cos_ref[at, :], sin_ref[at, :]
        for head in range(3):
            lanes = slice(head * HEAD_SIZE, (head + 1) * HEAD_SIZE)
            values = product[:, lanes]
            gain = gain_ref[head // 2 : head // 2 + 1, :]
            scaled = values * inverse_size(values) * gain
            turned = scaled * cosine + pltpu.roll(scaled, HEAD_SIZE // 2, 1) * sine
            low_ref[at, lanes] = turned.astype(BF)
        low_ref[at, 3 * HEAD_SIZE :] = product[:, 3 * HEAD_SIZE :].astype(BF)
        return carry

    lax.fori_loop(0, ALL_ROWS // BLOCK, project, 0)
    value_t[...] = low_ref[:, 3 * HEAD_SIZE :].T
    for block in range(ALL_ROWS // BLOCK):
        at = slice(block * BLOCK, (block + 1) * BLOCK)
        for head in range(2):
            lanes = slice(head * HEAD_SIZE, (head + 1) * HEAD_SIZE)
            scores = scores_of(
                low_ref[:, 2 * HEAD_SIZE : 3 * HEAD_SIZE], low_ref[at, lanes],
                key_row_ref[...], row_ref[:, at], start_ref[:, at],
            )
            top = jnp.max(scores, axis=0, keepdims=True)
            exponent = jnp.exp(scores - top)
            summed = jnp.sum(exponent, axis=0, keepdims=True)
            probability = (exponent * (1.0 / summed)).astype(BF)
            out_t = dot_f32(value_t[...], probability, ((1,), (0,)))
            attended_ref[at, lanes] = out_t.T.astype(BF)
            log_ref[head : head + 1, at] = top + jnp.log(summed)
        part_ref[at, :] = dot_f32(
            attended_ref[at, :], out_weight_ref[...], ((1,), (1,))
        ).astype(BF)


def mlp_kernel(
    slot_ref, rows_ref, grad_ref, weight_ref, hid_ref, d_ref, back_ref, part_ref
):
    def turn(block, carry):
        at = pl.ds(pl.multiple_of(block * BLOCK, BLOCK), BLOCK)
        grads = jnp.concatenate([grad_ref[slot_ref[2 * block]], grad_ref[slot_ref[2 * block + 1]]])
        both = dot_f32(rows_ref[at, :], weight_ref[:, :768], ((1,), (0,)))
        gate, up = both[:, :384], both[:, 384:]
        sigmoid = jax.nn.sigmoid(gate)
        silu = gate * sigmoid
        hid = (silu * up).astype(BF)
        hid_ref[at, :] = hid
        d_hid = dot_f32(grads, weight_ref[:, 768:], ((1,), (0,)))
        d_gate = (d_hid * up * sigmoid * (1.0 + gate * (1.0 - sigmoid))).astype(BF)
        d_both = jnp.concatenate([d_gate, (d_hid * silu).astype(BF)], axis=1)
        d_ref[at, :] = d_both
        back_ref[at, :] = dot_f32(d_both, weight_ref[:, :768], ((1,), (1,))).astype(BF)
        part_ref[at, :] = dot_f32(hid, weight_ref[:, 768:], ((1,), (1,))).astype(BF)
        return carry

    lax.fori_loop(0, ALL_ROWS // BLOCK, turn, 0)


def split_rows(me, whole, keep_ref, send_ref):
    core = lax.rem(me, 2)
    for slot in range(8):
        at = slice(slot * SHARD, (slot + 1) * SHARD)
        keep_ref[at] = whole[pl.ds(slot_place(me, slot, core), SHARD), :]
        send_ref[at] = whole[pl.ds(slot_place(me, slot, 1 - core), SHARD), :].astype(BF)


def mlp_grads_kernel(
    me_ref, slot_ref, rows_ref, grad_ref, hid_ref, d_ref, keep_ref, send_ref, whole, grads
):
    for slot in range(TENSOR):
        grads[slot * ROWS : (slot + 1) * ROWS] = grad_ref[slot_ref[slot]]
    for block in range(MODEL_WIDTH // BLOCK):
        at = slice(block * BLOCK, (block + 1) * BLOCK)
        whole[at, :768] = dot_f32(rows_ref[:, at], d_ref[...], ((0,), (0,)))
        whole[at, 768:] = dot_f32(grads[:, at], hid_ref[...], ((0,), (0,)))
    split_rows(me_ref[0], whole, keep_ref, send_ref)


def attn_grads_kernel(me_ref, rows_ref, d_ref, back_ref, attended_ref, keep_ref, send_ref, whole):
    for block in range(MODEL_WIDTH // BLOCK):
        at = slice(block * BLOCK, (block + 1) * BLOCK)
        whole[at, :512] = dot_f32(rows_ref[:, at], d_ref[...], ((0,), (0,)))
        whole[at, 512:] = dot_f32(back_ref[:, at], attended_ref[...], ((0,), (0,)))
    split_rows(me_ref[0], whole, keep_ref, send_ref)


def backward_kernel(
    back_ref, raw_ref, low_ref, log_ref, weight_ref, out_weight_ref, cos_ref, sin_ref, gain_ref,
    key_row_ref, row_ref, start_ref,
    d_ref, gain_grad_ref, part_ref, d_key, d_value, key_t,
):
    keys = slice(2 * HEAD_SIZE, 3 * HEAD_SIZE)
    values = slice(3 * HEAD_SIZE, 4 * HEAD_SIZE)
    key_t[...] = low_ref[:, keys].T
    d_key[...] = jnp.zeros_like(d_key)
    d_value[...] = jnp.zeros_like(d_value)

    def through_norm(turned, raw, cosine, sine, gain):
        scaled = turned * cosine + pltpu.roll(turned * sine, HEAD_SIZE // 2, 1)
        inverse = inverse_size(raw)
        weighted = scaled * gain
        mean = jnp.mean(weighted * raw, axis=-1, keepdims=True)
        grad = inverse * weighted - raw * (inverse * inverse * inverse * mean)
        return grad.astype(BF), jnp.sum(scaled * raw * inverse, axis=0, keepdims=True)

    query_gain_grad = jnp.zeros((1, HEAD_SIZE), F32)
    for block in range(ALL_ROWS // BLOCK):
        at = slice(block * BLOCK, (block + 1) * BLOCK)
        d_attended = dot_f32(back_ref[at, :], out_weight_ref[...], ((1,), (0,))).astype(BF)
        for head in range(2):
            lanes = slice(head * HEAD_SIZE, (head + 1) * HEAD_SIZE)
            queries = low_ref[at, lanes]
            d_out = d_attended[:, lanes]
            scores = scores_of(
                low_ref[:, keys], queries, key_row_ref[...], row_ref[:, at], start_ref[:, at]
            )
            probability = jnp.exp(scores - log_ref[head : head + 1, at])
            d_prob = dot_f32(low_ref[:, values], d_out, ((1,), (1,)))
            row_dot = jnp.sum(probability * d_prob, axis=0, keepdims=True)
            d_score = (probability * (d_prob - row_dot)).astype(BF)
            d_value[...] += dot_f32(probability.astype(BF), d_out, ((1,), (0,)))
            d_key[...] += dot_f32(d_score, queries, ((1,), (0,)))
            d_query_t = dot_f32(key_t[...], d_score, ((1,), (0,)))
            grad, gain_part = through_norm(
                d_query_t.T * SCORE_SCALE, raw_ref[at, lanes], cos_ref[at, :], sin_ref[at, :],
                gain_ref[0:1, :],
            )
            d_ref[at, lanes] = grad
            query_gain_grad = query_gain_grad + gain_part
    key_gain_grad = jnp.zeros((1, HEAD_SIZE), F32)
    for block in range(ALL_ROWS // BLOCK):
        at = slice(block * BLOCK, (block + 1) * BLOCK)
        grad, gain_part = through_norm(
            d_key[at, :] * SCORE_SCALE, raw_ref[at, keys], cos_ref[at, :], sin_ref[at, :],
            gain_ref[1:2, :],
        )
        d_ref[at, keys] = grad
        d_ref[at, values] = d_value[at, :].astype(BF)
        key_gain_grad = key_gain_grad + gain_part
        part_ref[at, :] = dot_f32(d_ref[at, :], weight_ref[...], ((1,), (1,))).astype(BF)
    gain_grad_ref[0:1, :] = query_gain_grad
    gain_grad_ref[1:2, :] = key_gain_grad


def scatter_data(pair):
    keep, other = pair
    return ring_scatter(keep + send(other, TURN_CORE).astype(F32), SHARD, OVER_DATA)


def shape(rows, columns, kind):
    return jax.ShapeDtypeStruct((rows, columns), kind)


def split_shapes(width):
    return [shape(8 * SHARD, width, F32), shape(8 * SHARD, width, BF)]


def pack_kernel(me_ref, rows_ref, *outs):
    me = me_ref[0]
    kind = lax.rem(me, 2) + 2 * (me // 8)
    width = outs[0].shape[1]
    for turn in range(4):
        number = jnp.minimum(jnp.bitwise_xor(kind, turn), 2)
        for choice in range(3):

            @pl.when(number == choice)
            def _(turn=turn, choice=choice):
                outs[turn][...] = rows_ref[:, choice * width : (choice + 1) * width].astype(BF)


def split_low(value):
    high = value.astype(BF)
    return high, (value - high.astype(F32)).astype(BF)


def dot_f32(left, right, dims):
    return lax.dot_general(left, right, (dims, ((), ())), preferred_element_type=F32)


def orthogonal_kernel(paired, me_ref, *refs):
    parts, outs, current = refs[:5], refs[5:9], refs[9]
    me = me_ref[0]
    kind = lax.rem(me, 2) + 2 * (me // 8)
    width = outs[0].shape[1]
    at = 0
    for part in parts:
        current[at : at + part.shape[0]] = part[...].astype(F32)
        at += part.shape[0]
    matrix = current[...]
    columns = jnp.sum(matrix * matrix, axis=0, keepdims=True)
    size = jnp.sum(columns, keepdims=True)
    if paired is not None:
        place = lax.broadcasted_iota(jnp.int32, (1, width), 1) < width // 2
        first = jnp.sum(jnp.where(place, columns, 0.0), keepdims=True)
        second = jnp.sum(jnp.where(place, 0.0, columns), keepdims=True)
        size = jnp.where(kind == paired, jnp.where(place, first, second), size)
        down = lax.broadcasted_iota(jnp.int32, (width, width), 0) < width // 2
        across = lax.broadcasted_iota(jnp.int32, (width, width), 1) < width // 2
        apart = (down != across) & (kind == paired)
    current[...] = matrix / (jnp.sqrt(size) + 1e-07)

    def polynomial(high, low):
        cross = dot_f32(high, low, ((0,), (0,)))
        gram = dot_f32(high, high, ((0,), (0,))) + (cross + cross.T)
        if paired is not None:
            gram = jnp.where(apart, 0.0, gram)
        gram_high, gram_low = split_low(gram)
        cross = dot_f32(gram_high, gram_low, ((1,), (0,)))
        square = dot_f32(gram_high, gram_high, ((1,), (0,))) + (cross + cross.T)
        return split_low(NS_B * gram + NS_C * square)

    def moved(value, high, low, poly_high, poly_low):
        change = dot_f32(high, poly_high, ((1,), (0,)))
        change = change + dot_f32(high, poly_low, ((1,), (0,)))
        change = change + dot_f32(low, poly_high, ((1,), (0,)))
        return NS_A * value + change

    def turn(_, carry):
        value = current[...]
        high, low = split_low(value)
        poly_high, poly_low = polynomial(high, low)
        current[...] = moved(value, high, low, poly_high, poly_low)
        return carry

    lax.fori_loop(0, NS_ITERS - 1, turn, 0)
    high, low = split_low(current[...])
    poly_high, poly_low = polynomial(high, low)
    rows = 4 * SHARD
    last = moved(current[:rows], high[:rows], low[:rows], poly_high, poly_low)
    for number in range(4):
        outs[number][...] = last[number * SHARD : (number + 1) * SHARD].astype(BF)


def update_kernel(rates, me_ref, master_ref, *refs):
    turned, out = refs[:4], refs[4]
    me = me_ref[0]
    kind = lax.rem(me, 2) + 2 * (me // 8)
    width = turned[0].shape[1]
    for turn in range(4):
        for number in range(3):

            @pl.when(jnp.bitwise_xor(kind, turn) == number)
            def _(turn=turn, number=number):
                at = slice(number * width, (number + 1) * width)
                out[:, at] = master_ref[:, at] - rates[number] * turned[turn][...].astype(F32)


def muon(me, renewed, masters, rates, paired):
    width = renewed.shape[1] // 3
    scalar = [pl.BlockSpec(memory_space=pltpu.SMEM)]
    limit = pltpu.CompilerParams(vmem_limit_bytes=48 * 2**20)
    turns = (TURN_CORE, TURN_FAR, TURN_BOTH)
    quarter = jax.ShapeDtypeStruct((SHARD, width), BF)
    packed = pl.pallas_call(
        pack_kernel,
        in_specs=scalar + whole_specs(1),
        out_specs=whole_specs(4),
        out_shape=[quarter] * 4,
        compiler_params=limit,
        name="muon_pack",
    )(me, renewed)
    own = jnp.concatenate(
        [packed[0]] + [send(block, turn) for block, turn in zip(packed[1:], turns)], axis=0
    )
    parts = [own] + ring_spread(own, UP_Y, DOWN_Y)
    turned = pl.pallas_call(
        lambda *refs: orthogonal_kernel(paired, *refs),
        in_specs=scalar + whole_specs(5),
        out_specs=whole_specs(4),
        out_shape=[quarter] * 4,
        scratch_shapes=[pltpu.VMEM((DATA * SHARD, width), F32)],
        compiler_params=limit,
        name="muon_turns",
    )(me, *parts)
    back = [turned[0]] + [send(block, turn) for block, turn in zip(turned[1:], turns)]
    return pl.pallas_call(
        lambda *refs: update_kernel(rates, *refs),
        in_specs=scalar + whole_specs(5),
        out_specs=whole_specs(1)[0],
        out_shape=jax.ShapeDtypeStruct(masters.shape, F32),
        compiler_params=limit,
        name="muon_update",
    )(me, masters, *back)


def local(
    tokens,
    out_grad,
    lengths,
    w_query,
    key_weight,
    value_weight,
    w_output,
    w_gate,
    w_up,
    w_down,
    momentum_query,
    key_momentum_buffer,
    value_momentum_buffer,
    momentum_output,
    momentum_gate,
    momentum_up,
    momentum_down,
    gains,
    gain_first,
    gain_second,
):
    tensor_index = lax.axis_index("tensor")
    data_index = lax.axis_index("dp")
    me = data_index.astype(jnp.int32).reshape(1)
    attn_masters = jnp.concatenate([w_query, key_weight, value_weight, w_output.T], axis=1)
    mlp_masters = jnp.concatenate([w_gate, w_up, w_down.T], axis=1)
    attn_moments = jnp.concatenate(
        [momentum_query, key_momentum_buffer, value_momentum_buffer, momentum_output.T], axis=1
    )
    mlp_moments = jnp.concatenate([momentum_gate, momentum_up, momentum_down.T], axis=1)
    g_attn = gains[:MODEL_WIDTH]
    g_mlp = gains[MODEL_WIDTH : 2 * MODEL_WIDTH]
    query_gain = gains[2 * MODEL_WIDTH : 2 * MODEL_WIDTH + HEAD_SIZE]
    g_key = gains[2 * MODEL_WIDTH + HEAD_SIZE :]
    inputs = tokens.astype(F32)
    first_normalized = gather_tensor(root_mean_square_norm(inputs, g_attn).astype(BF))
    attn_weights = gather_data(attn_masters.astype(BF), me)
    mlp_lowered, first_normalized = lax.optimization_barrier(
        (mlp_masters.astype(BF), first_normalized)
    )
    mlp_weights = gather_data(mlp_lowered, me)
    slots = [
        lax.rem(tensor_index // 2 + STEPS[s] + 4, 4) * 2 + jnp.bitwise_xor(tensor_index % 2, s % 2)
        for s in range(TENSOR)
    ]
    in_order = lax.all_gather(out_grad, "tensor", axis=0)
    qkv_full, output_full = attn_weights[:, :512], attn_weights[:, 512:]
    slot_list = jnp.stack(slots).astype(jnp.int32)
    row_index = jnp.concatenate([slot * ROWS + jnp.arange(ROWS, dtype=jnp.int32) for slot in slots])
    segment, token_position = sequence_layout(lengths[0], row_index)
    half = HEAD_SIZE // 2
    frequency = THETA ** (-jnp.arange(half, dtype=F32) * 2.0 / HEAD_SIZE)
    angles = token_position.astype(F32)[:, None] * frequency[None, :]
    cosine, sine = jnp.cos(angles), jnp.sin(angles)
    cosine = jnp.concatenate([cosine, cosine], axis=1)
    sine = jnp.concatenate([-sine, sine], axis=1)
    head_gains = jnp.stack([query_gain, g_key])
    key_row = row_index[:, None]
    query_row = row_index[None, :]
    query_start = (row_index - token_position)[None, :]
    raw, rotated, attn_low, logsum, branch_part = pl.pallas_call(
        forward_kernel,
        in_specs=whole_specs(9),
        out_specs=whole_specs(5),
        out_shape=[
            shape(ALL_ROWS, 512, F32),
            shape(ALL_ROWS, 512, BF),
            shape(ALL_ROWS, 256, BF),
            shape(2, ALL_ROWS, F32),
            shape(ALL_ROWS, MODEL_WIDTH, BF),
        ],
        scratch_shapes=[pltpu.VMEM((HEAD_SIZE, ALL_ROWS), BF)],
        compiler_params=room(48),
        cost_estimate=cost(2.7e9, 12e6),
        name="attention_forward",
    )(
        first_normalized, qkv_full, output_full, cosine, sine, head_gains,
        key_row, query_row, query_start,
    )
    branch_out = scatter_tensor(branch_part)
    hidden_in = inputs + branch_out
    n_two = gather_tensor(root_mean_square_norm(hidden_in, g_mlp).astype(BF))
    inner_act, d_both, back_part, mlp_part = pl.pallas_call(
        mlp_kernel,
        in_specs=[SCALAR] + whole_specs(3),
        out_specs=whole_specs(4),
        out_shape=[
            shape(ALL_ROWS, 384, BF),
            shape(ALL_ROWS, 768, BF),
            shape(ALL_ROWS, MODEL_WIDTH, BF),
            shape(ALL_ROWS, MODEL_WIDTH, BF),
        ],
        compiler_params=room(48),
        cost_estimate=cost(4.9e9, 12e6),
        name="mlp_both_ways",
    )(slot_list, n_two, in_order, mlp_weights)
    d_norm_two = scatter_tensor(back_part)
    mlp_grads = pl.pallas_call(
        mlp_grads_kernel,
        in_specs=[SCALAR] * 2 + whole_specs(4),
        out_specs=whole_specs(2),
        out_shape=split_shapes(1152),
        scratch_shapes=[
            pltpu.VMEM((MODEL_WIDTH, 1152), F32),
            pltpu.VMEM((ALL_ROWS, MODEL_WIDTH), BF),
        ],
        compiler_params=room(48),
        cost_estimate=cost(2.4e9, 10e6),
        name="mlp_grads",
    )(me, slot_list, n_two, in_order, inner_act, d_both)
    mlp_reduced = scatter_data(mlp_grads)
    mlp_renewed = MOMENTUM * mlp_moments + mlp_reduced
    mlp_updated = muon(
        me, mlp_renewed, mlp_masters, (1.0, 1.0, math.sqrt(MODEL_WIDTH / FF)), None
    )
    _, norm_two_back = jax.vjp(root_mean_square_norm, hidden_in, g_mlp)
    d_hidden_in, dg_mlp = norm_two_back(d_norm_two)
    d_residual = out_grad.astype(F32) + d_hidden_in
    residual_rows = gather_tensor(d_residual.astype(BF))
    d_qkv, head_gain_grads, d_norm_part = pl.pallas_call(
        backward_kernel,
        in_specs=whole_specs(12),
        out_specs=whole_specs(3),
        out_shape=[
            shape(ALL_ROWS, 512, BF),
            shape(2, HEAD_SIZE, F32),
            shape(ALL_ROWS, MODEL_WIDTH, BF),
        ],
        scratch_shapes=[
            pltpu.VMEM((ALL_ROWS, HEAD_SIZE), F32),
            pltpu.VMEM((ALL_ROWS, HEAD_SIZE), F32),
            pltpu.VMEM((HEAD_SIZE, ALL_ROWS), BF),
        ],
        compiler_params=room(48),
        cost_estimate=cost(4.2e9, 14e6),
        name="attention_backward",
    )(
        residual_rows, raw, rotated, logsum, qkv_full, output_full, cosine, sine, head_gains,
        key_row, query_row, query_start,
    )
    attn_grads = pl.pallas_call(
        attn_grads_kernel,
        in_specs=[SCALAR] + whole_specs(4),
        out_specs=whole_specs(2),
        out_shape=split_shapes(768),
        scratch_shapes=[pltpu.VMEM((MODEL_WIDTH, 768), F32)],
        compiler_params=room(48),
        cost_estimate=cost(1.6e9, 10e6),
        name="attention_grads",
    )(me, first_normalized, d_qkv, residual_rows, attn_low)
    attn_reduced = scatter_data(attn_grads)
    attn_renewed = MOMENTUM * attn_moments + attn_reduced
    attn_updated = muon(
        me,
        attn_renewed,
        attn_masters,
        (1.0, 1.0, math.sqrt(MODEL_WIDTH / (QUERY_HEADS * HEAD_SIZE // 16))),
        1,
    )
    both = scatter_tensor(jnp.concatenate([d_norm_part, mlp_part], axis=1))
    d_norm_one, mlp_out = both[:, :MODEL_WIDTH], both[:, MODEL_WIDTH:]
    result = (hidden_in + mlp_out).astype(BF)
    _, norm_one_back = jax.vjp(root_mean_square_norm, inputs, g_attn)
    d_inputs, dg_attn = norm_one_back(d_norm_one)
    tokens_grad = d_residual + d_inputs
    gain_grad = jnp.concatenate([dg_attn, dg_mlp, head_gain_grads[0], head_gain_grads[1]])
    for axis, count in (("tensor", TENSOR), ("dp", DATA)):
        turn = 1
        while turn < count:
            gain_grad = gain_grad + send(gain_grad, (axis, [(i, i ^ turn) for i in range(count)]))
            turn *= 2
    renewed_first = BETA_ONE * gain_first + (1.0 - BETA_ONE) * gain_grad
    renewed_second = BETA_TWO * gain_second + (1.0 - BETA_TWO) * gain_grad * gain_grad
    corrected_first = renewed_first / (1.0 - BETA_ONE**ADAM_STEP)
    corrected_second = renewed_second / (1.0 - BETA_TWO**ADAM_STEP)
    updated_gains = gains - GAIN_RATE * corrected_first / (jnp.sqrt(corrected_second) + ADAM_EPS)

    def unpack(attn, mlp):
        return (
            attn[:, :256],
            attn[:, 256:384],
            attn[:, 384:512],
            attn[:, 512:].T,
            mlp[:, :384],
            mlp[:, 384:768],
            mlp[:, 768:].T,
        )

    return (
        result,
        tokens_grad,
        *unpack(attn_reduced, mlp_reduced),
        *unpack(attn_renewed, mlp_renewed),
        *unpack(attn_updated, mlp_updated),
        gain_grad,
        renewed_first,
        renewed_second,
        updated_gains,
    )


def solution(mesh):
    placed = (
        P(("dp", "tensor"), None),
        P(("dp", "tensor"), None),
        P("dp", None),
        P("dp", "tensor"),
        P("dp", "tensor"),
        P("dp", "tensor"),
        P("tensor", "dp"),
        P("dp", "tensor"),
        P("dp", "tensor"),
        P("tensor", "dp"),
        P("dp", "tensor"),
        P("dp", "tensor"),
        P("dp", "tensor"),
        P("tensor", "dp"),
        P("dp", "tensor"),
        P("dp", "tensor"),
        P("tensor", "dp"),
        P(),
        P(),
        P(),
    )
    return jax.shard_map(
        local,
        mesh=mesh,
        in_specs=placed,
        out_specs=(
            P(("dp", "tensor"), None),
            P(("dp", "tensor"), None),
            P("dp", "tensor"),
            P("dp", "tensor"),
            P("dp", "tensor"),
            P("tensor", "dp"),
            P("dp", "tensor"),
            P("dp", "tensor"),
            P("tensor", "dp"),
            P("dp", "tensor"),
            P("dp", "tensor"),
            P("dp", "tensor"),
            P("tensor", "dp"),
            P("dp", "tensor"),
            P("dp", "tensor"),
            P("tensor", "dp"),
            P("dp", "tensor"),
            P("dp", "tensor"),
            P("dp", "tensor"),
            P("tensor", "dp"),
            P("dp", "tensor"),
            P("dp", "tensor"),
            P("tensor", "dp"),
            P(),
            P(),
            P(),
            P(),
        ),
        check_vma=False,
    )
```

time: 1280 us -> 385 us (0.30)
  waiting for transfers between devices: 752 us -> 138 us
  blocking collectives: 285 us -> 0 us
  matrix products: 113 us -> 0 us
  starting transfers between devices: 6.7 us -> 93.9 us
  Pallas kernels: 0 us -> 72.3 us
  other arithmetic: 56.9 us -> 20.6 us
    reduce_scatter x11 -> x0, waiting for transfers between devices: 649 us -> none  [the longest x1 91.8 us: local(): lax.psum_scatter(jnp.dot(rows_part, output_full, preferred_element_type=j...]
    all_gather x7 -> x0, blocking collectives: 173 us -> none  [the longest x1 36 us: local(): lax.all_gather(lowered[4], 'dp', axis=0, tiled=True)]
    ppermute x0 -> x81, waiting for transfers between devices: none -> 138 us  [send(): return lax.ppermute(block, link[0], link[1])]
    dot_general x52 -> x0, matrix products: 113 us -> none  [the longest x15 37.2 us: precise_product(): return jnp.dot(left, right, precision=lax.Precision.HIGHEST)]
    ppermute x0 -> x81, starting transfers between devices: none -> 93.8 us  [send(): return lax.ppermute(block, link[0], link[1])]
    psum x1 -> x0, blocking collectives: 77.9 us -> none  [local(): lax.psum(jnp.concatenate([dg_attn, dg_mlp, dg_query, dg_key]), ('dp', 'te...]
    all_gather x4 -> x1, waiting for transfers between devices: 72.5 us -> 0.01 us  [local(): in_order = lax.all_gather(out_grad, 'tensor', axis=0)]
    pallas_call x0 -> x13, Pallas kernels: none -> 72.3 us  [the longest x2 22 us: muon(): pl.pallas_call(lambda *refs: orthogonal_kernel(paired, *refs), in_specs=s...]
  transfers between devices with their start and end apart: 16 -> 82, of which waited for: 13 -> 42; matrix products, arithmetic and copies ran while one was open for 9% -> 14% of each run, Pallas kernels for 0% -> 16%
where the time goes in v1:
time: 385 us; the launch traced here: 380 us
  waiting for transfers between devices  138 us (36%)
  starting transfers between devices  93.9 us (24%)
  Pallas kernels  72.3 us (19%)
  local copies, waits for them, and re-layouts  39.1 us (10%)
  other arithmetic  20.6 us (5%)
  between operations  15.8 us (4%)
    ppermute x81, waiting for transfers between devices, send(): return lax.ppermute(block, link[0], link[1])  138 us
    ppermute x81, starting transfers between devices, send(): return lax.ppermute(block, link[0], link[1])  93.8 us
    pallas_call x2, Pallas kernels, muon(): pl.pallas_call(lambda *refs: orthogonal_kernel(paired, *refs), in_specs=s...  22 us
    unnamed x130, local copies, waits for them, and re-layouts  21.6 us
    pallas_call x1, Pallas kernels, local(): pl.pallas_call(backward_kernel, in_specs=whole_specs(12), out_specs=whole...  14.4 us
    pallas_call x1, Pallas kernels, local(): pl.pallas_call(forward_kernel, in_specs=whole_specs(9), out_specs=whole_s...  14.1 us
    pallas_call x1, Pallas kernels, local(): pl.pallas_call(mlp_kernel, in_specs=[SCALAR] + whole_specs(3), out_specs=...  10.7 us
  transfers between devices with their start and end apart: 82, of which 42 were waited for; matrix products, arithmetic and copies ran while one was open for 14% of the time, Pallas kernels for 16%

profile of v1, /device:TPU:30, one launch (start us, length us, event | category | flops | bytes accessed | tf_op | source)
XLA Modules:
  0.0 379.9 jit_solution(2634359268825899260)
XLA Ops:
  14.4 3.6 collective-permute-start.5
  19.9 3.0 fusion.17
  43.4 7.6 %collective-permute-done.2 = bf16[256,1024]{1,0:T(8,128)(2,1)} collective-permute-done((bf16[256,1024]{1,0:T(8,128)(2,1)}, bf16[256,1024]{1,0:T(8,128)(2,1)}, u32[]{:S(2)}, u32[]{:S(2)}) %collective-permute-start.2) | collective-permute-done | bytes 524320 | tf_op jit(solution)/shard_map/ppermute | solution.py:85
  51.9 2.2 collective-permute-start.4
  56.4 6.9 %collective-permute-done.4 = bf16[128,1024]{1,0:T(8,128)(2,1)S(1)} collective-permute-done((bf16[128,1024]{1,0:T(8,128)(2,1)S(1)}, bf16[128,1024]{1,0:T(8,128)(2,1)S(1)}, u32[]{:S(2)}, u32[]{:S(2)}) %collective-permute-start.4) | collective-permute-done | bytes 262176 | tf_op jit(solution)/shard_map/ppermute | solution.py:85
  63.3 3.5 collective-permute-start.21
  67.1 14.1 %attention_forward.1 = (f32[1024,512]{1,0:T(8,128)}, bf16[1024,512]{1,0:T(8,128)(2,1)S(1)}, bf16[1024,256]{1,0:T(8,128)(2,1)S(1)}, f32[2,1024]{1,0:T(2,128)S(1)}, bf16[1024,1024]{1,0:T(8,128)(2,1)}) custom-call(bf16[1024,1024]{1,0:T(8,128)(2,1)} %copy-done.10, bf16[1024,512]{1,0:T(8,128)(2,1)S(1)} %slice.377.weight_ref, ...), custom_call_target="tpu_custom_call" | custom-call | flops 2700000000 | bytes 12000000 | tf_op jit(solution)/shard_map/attention_forward/pallas_call | solution.py:541
  83.7 2.7 collective-permute-start.13
  92.1 3.8 collective-permute-start.14
  99.7 2.8 collective-permute-done.14
  102.6 3.8 collective-permute-done.12
  108.6 4.5 %collective-permute-done.15 = bf16[128,1024]{1,0:T(8,128)(2,1)S(1)} collective-permute-done((bf16[128,1024]{1,0:T(8,128)(2,1)S(1)}, bf16[128,1024]{1,0:T(8,128)(2,1)S(1)}, u32[]{:S(2)}, u32[]{:S(2)}) %collective-permute-start.15) | collective-permute-done | bytes 262176 | tf_op jit(solution)/shard_map/ppermute | solution.py:85
  114.3 6.3 %collective-permute-done.16 = bf16[128,1024]{1,0:T(8,128)(2,1)S(1)} collective-permute-done((bf16[128,1024]{1,0:T(8,128)(2,1)S(1)}, bf16[128,1024]{1,0:T(8,128)(2,1)S(1)}, u32[]{:S(2)}, u32[]{:S(2)}) %collective-permute-start.16) | collective-permute-done | bytes 262176 | tf_op jit(solution)/shard_map/ppermute | solution.py:85
  123.6 9.6 %collective-permute-done.17 = bf16[256,1024]{1,0:T(8,128)(2,1)} collective-permute-done((bf16[256,1024]{1,0:T(8,128)(2,1)}, bf16[256,1024]{1,0:T(8,128)(2,1)}, u32[]{:S(2)}, u32[]{:S(2)}) %collective-permute-start.17) | collective-permute-done | bytes 524320 | tf_op jit(solution)/shard_map/ppermute | solution.py:85
  146.9 10.7 %mlp_both_ways.1 = (bf16[1024,384]{1,0:T(8,128)(2,1)S(1)}, bf16[1024,768]{1,0:T(8,128)(2,1)S(1)}, bf16[1024,1024]{1,0:T(8,128)(2,1)S(1)}, bf16[1024,1024]{1,0:T(8,128)(2,1)}) custom-call(s32[8]{0:T(128)S(1)} %stack.47.slot_ref, bf16[1024,1024]{1,0:T(8,128)(2,1)} %constant_dynamic-update-slice_fusion.13.rows_ref, bf16[8,128,1024]{2,1,0:T(8,128)(2,1)} %bitcast.57, ...), custom_call_target="tpu_custom_call" | custom-call | flops 4899999744 | bytes 12000000 | tf_op jit(solution)/shard_map/mlp_both_ways/pallas_call | solution.py:563
  158.5 2.4 collective-permute-start.29
  160.9 6.9 %mlp_grads.1 = (f32[512,1152]{1,0:T(8,128)}, bf16[512,1152]{1,0:T(8,128)(2,1)S(1)}) custom-call(s32[1]{0:T(128)} %bitcast.1.me_ref.refs_0_, s32[8]{0:T(128)S(1)} %stack.47.slot_ref, bf16[1024,1024]{1,0:T(8,128)(2,1)} %constant_dynamic-update-slice_fusion.13.rows_ref, bf16[8,128,1024]{2,1,0:T(8,128)(2,1)} %bitcast.58, ...), custom_call_target="tpu_custom_call" | custom-call | flops 2400000000 | bytes 10000000 | tf_op jit(solution)/shard_map/mlp_grads/pallas_call | solution.py:578
  170.5 12.1 %collective-permute-done.30 = bf16[256,1024]{1,0:T(8,128)(2,1)S(1)} collective-permute-done((bf16[256,1024]{1,0:T(8,128)(2,1)S(1)}, bf16[256,1024]{1,0:T(8,128)(2,1)S(1)}, u32[]{:S(2)}, u32[]{:S(2)}) %collective-permute-start.30) | collective-permute-done | bytes 524320 | tf_op jit(solution)/shard_map/ppermute | solution.py:85
  185.8 2.9 collective-permute-start.51
  188.7 2.9 collective-permute-done.31
  191.9 3.3 collective-permute-start.52
  199.5 3.8 collective-permute-done.50
  207.9 2.1 collective-permute-done.53
  213.7 2.3 collective-permute-done.65
  224.4 4.2 %collective-permute-done.36 = bf16[128,1024]{1,0:T(8,128)(2,1)S(1)} collective-permute-done((bf16[128,1024]{1,0:T(8,128)(2,1)S(1)}, bf16[128,1024]{1,0:T(8,128)(2,1)S(1)}, u32[]{:S(2)}, u32[]{:S(2)}) %collective-permute-start.36) | collective-permute-done | bytes 262176 | tf_op jit(solution)/shard_map/ppermute | solution.py:85
  229.5 14.4 %attention_backward.1 = (bf16[1024,512]{1,0:T(8,128)(2,1)S(1)}, f32[2,128]{1,0:T(2,128)S(1)}, bf16[1024,1024]{1,0:T(8,128)(2,1)}) custom-call(bf16[1024,1024]{1,0:T(8,128)(2,1)} %constant_dynamic-update-slice_fusion.27.back_ref, f32[1024,512]{1,0:T(8,128)} %get-tuple-element.65.raw_ref, bf16[1024,512]{1,0:T(8,128)(2,1)S(1)} %copy-done.15, ...), custom_call_target="tpu_custom_call" | custom-call | flops 4200000000 | bytes 14000000 | tf_op jit(solution)/shard_map/attention_backward/pallas_call | solution.py:600
  247.3 3.2 collective-permute-start.39
  253.6 3.6 attention_grads.1
  259.0 14.7 %muon_turns.3 = (bf16[64,384]{1,0:T(8,128)(2,1)S(1)}, bf16[64,384]{1,0:T(8,128)(2,1)S(1)}, bf16[64,384]{1,0:T(8,128)(2,1)S(1)}, bf16[64,384]{1,0:T(8,128)(2,1)S(1)}) custom-call(s32[1]{0:T(128)} %bitcast.1.me_ref.refs_0_, bf16[256,384]{1,0:T(8,128)(2,1)S(1)} %constant_dynamic-update-slice_fusion.39.refs_1_, ...), custom_call_target="tpu_custom_call" | custom-call | tf_op jit(solution)/shard_map/muon_turns/pallas_call | solution.py:460
  278.0 3.2 collective-permute-start.45
  281.3 2.9 collective-permute-done.43
  288.6 3.7 collective-permute-done.46
  292.3 2.3 collective-permute-done.44
  294.7 2.2 collective-permute-start.47
  297.6 3.5 collective-permute-done.47
  301.2 7.7 %collective-permute-done.40 = bf16[256,2048]{1,0:T(8,128)(2,1)S(1)} collective-permute-done((bf16[256,2048]{1,0:T(8,128)(2,1)S(1)}, bf16[256,2048]{1,0:T(8,128)(2,1)S(1)}, u32[]{:S(2)}, u32[]{:S(2)}) %collective-permute-start.40) | collective-permute-done | bytes 1048608 | tf_op jit(solution)/shard_map/ppermute | solution.py:85
  312.4 3.1 collective-permute-start.55
  315.7 10.3 %collective-permute-done.55 = bf16[64,256]{1,0:T(8,128)(2,1)S(1)} collective-permute-done((bf16[64,256]{1,0:T(8,128)(2,1)S(1)}, bf16[64,256]{1,0:T(8,128)(2,1)S(1)}, u32[]{:S(2)}, u32[]{:S(2)}) %collective-permute-start.55) | collective-permute-done | bytes 32800 | tf_op jit(solution)/shard_map/ppermute | solution.py:85
  326.1 2.4 collective-permute-start.57
  329.6 2.1 collective-permute-done.57.refs_2_
  331.7 3.5 collective-permute-start.59
  337.1 3.7 collective-permute-done.60.refs_5_
  340.7 7.3 %muon_turns.2 = (bf16[64,256]{1,0:T(8,128)(2,1)S(1)}, bf16[64,256]{1,0:T(8,128)(2,1)S(1)}, bf16[64,256]{1,0:T(8,128)(2,1)S(1)}, bf16[64,256]{1,0:T(8,128)(2,1)S(1)}) custom-call(s32[1]{0:T(128)} %bitcast.1.me_ref.refs_0_, bf16[256,256]{1,0:T(8,128)(2,1)S(1)} %constant_dynamic-update-slice_fusion.35.refs_1_, ...), custom_call_target="tpu_custom_call" | custom-call | tf_op jit(solution)/shard_map/muon_turns/pallas_call | solution.py:460
  348.7 2.8 collective-permute-start.63
  354.0 2.7 collective-permute-done.76
  358.5 3.1 collective-permute-done.78
  361.6 5.2 %collective-permute-done.79 = f32[2304]{0:T(1024)S(1)} collective-permute-done((f32[2304]{0:T(1024)S(1)}, f32[2304]{0:T(1024)S(1)}, u32[]{:S(2)}, u32[]{:S(2)}) %collective-permute-start.79) | collective-permute-done | bytes 9248 | tf_op jit(solution)/shard_map/ppermute | solution.py:85
  368.4 3.6 collective-permute-done.80
  (379 shorter events, 124.8 us)
Async XLA Ops:
  7.2 139.6 %all-gather.3.cloned.1.call-start = ((), (), s32[]{:S(2)}) async-start(), calls=%async_computation | async-start | bytes 2359296 | tf_op jit(solution)/shard_map/all_gather | solution.py:526
  11.0 16.4 %collective-permute-start = (bf16[128,1024]{1,0:T(8,128)(2,1)S(1)}, bf16[128,1024]{1,0:T(8,128)(2,1)S(1)}, u32[]{:S(2)}, u32[]{:S(2)}) collective-permute-start(bf16[128,1024]{1,0:T(8,128)(2,1)S(1)} %get-tuple-element.121), channel_id=1, source_target_pairs={{0,1},{1,0},{2,3},{3,2},{4,5},{5,4},{6,7},{7,6},{8,9},{9,8},{10,11... | collective-permute-start | bytes 786440 | tf_op jit(solution)/shard_map/ppermute | solution.py:85
  14.4 10.1 %collective-permute-start.5 = (bf16[64,768]{1,0:T(8,128)(2,1)S(1)}, bf16[64,768]{1,0:T(8,128)(2,1)S(1)}, u32[]{:S(2)}, u32[]{:S(2)}) collective-permute-start(bf16[64,768]{1,0:T(8,128)(2,1)S(1)} %get-tuple-element.119), channel_id=1, source_target_pairs={{0,64},{8,72},{16,80},{24,88},{32,96},{40,104},{48,112},{56,120},{... | collective-permute-start | bytes 294920 | tf_op jit(solution)/shard_map/ppermute | solution.py:85
  28.2 12.3 %collective-permute-start.1 = (bf16[256,1024]{1,0:T(8,128)(2,1)}, bf16[256,1024]{1,0:T(8,128)(2,1)}, u32[]{:S(2)}, u32[]{:S(2)}) collective-permute-start(bf16[256,1024]{1,0:T(8,128)(2,1)} %pad_maximum_fusion.2), channel_id=1, source_target_pairs={{0,2},{1,3},{2,4},{3,5},{4,6},{5,7},{6,0},{7,1},{8,10},{9,11},{10,... | collective-permute-start | bytes 1572872 | tf_op jit(solution)/shard_map/ppermute | solution.py:85
  28.7 22.3 %collective-permute-start.2 = (bf16[256,1024]{1,0:T(8,128)(2,1)}, bf16[256,1024]{1,0:T(8,128)(2,1)}, u32[]{:S(2)}, u32[]{:S(2)}) collective-permute-start(bf16[256,1024]{1,0:T(8,128)(2,1)} %pad_maximum_fusion.2), channel_id=1, source_target_pairs={{0,6},{1,7},{2,0},{3,1},{4,2},{5,3},{6,4},{7,5},{8,14},{9,15},{10,... | collective-permute-start | bytes 1572872 | tf_op jit(solution)/shard_map/ppermute | solution.py:85
  38.4 28.4 %collective-permute-start.10 = (bf16[512,768]{1,0:T(8,128)(2,1)}, bf16[512,768]{1,0:T(8,128)(2,1)S(1)}, u32[]{:S(2)}, u32[]{:S(2)}) collective-permute-start(bf16[512,768]{1,0:T(8,128)(2,1)} %constant_dynamic-update-slice_fusion.6), channel_id=1, source_target_pairs={{0,8},{8,0},{16,24},{24,16},{32,40},{40,32},{48,56},{56,48},{64,72... | collective-permute-start | bytes 2359304 | tf_op jit(solution)/shard_map/ppermute | solution.py:85
  41.7 14.7 %collective-permute-start.3 = (bf16[128,1024]{1,0:T(8,128)(2,1)S(1)}, bf16[128,1024]{1,0:T(8,128)(2,1)S(1)}, u32[]{:S(2)}, u32[]{:S(2)}) collective-permute-start(bf16[128,1024]{1,0:T(8,128)(2,1)S(1)} %slice.373), channel_id=1, source_target_pairs={{0,2},{1,3},{2,4},{3,5},{4,6},{5,7},{6,0},{7,1},{8,10},{9,11},{10,... | collective-permute-start | bytes 786440 | tf_op jit(solution)/shard_map/ppermute | solution.py:85
  51.9 11.3 %collective-permute-start.4 = (bf16[128,1024]{1,0:T(8,128)(2,1)S(1)}, bf16[128,1024]{1,0:T(8,128)(2,1)S(1)}, u32[]{:S(2)}, u32[]{:S(2)}) collective-permute-start(bf16[128,1024]{1,0:T(8,128)(2,1)S(1)} %slice.374), channel_id=1, source_target_pairs={{0,6},{1,7},{2,0},{3,1},{4,2},{5,3},{6,4},{7,5},{8,14},{9,15},{10,... | collective-permute-start | bytes 786440 | tf_op jit(solution)/shard_map/ppermute | solution.py:85
  63.3 23.7 %collective-permute-start.21 = (bf16[64,1152]{1,0:T(8,128)(2,1)S(1)}, bf16[64,1152]{1,0:T(8,128)(2,1)S(1)}, u32[]{:S(2)}, u32[]{:S(2)}) collective-permute-start(bf16[64,1152]{1,0:T(8,128)(2,1)S(1)} %copy-done.25), channel_id=1, source_target_pairs={{0,64},{8,72},{16,80},{24,88},{32,96},{40,104},{48,112},{56,120},{... | collective-permute-start | bytes 442376 | tf_op jit(solution)/shard_map/ppermute | solution.py:85
  83.1 7.7 %collective-permute-start.11 = (bf16[128,1024]{1,0:T(8,128)(2,1)S(1)}, bf16[128,1024]{1,0:T(8,128)(2,1)S(1)}, u32[]{:S(2)}, u32[]{:S(2)}) collective-permute-start(bf16[128,1024]{1,0:T(8,128)(2,1)S(1)} %get-tuple-element.138), channel_id=1, source_target_pairs={{0,6},{1,7},{2,0},{3,1},{4,2},{5,3},{6,4},{7,5},{8,14},{9,15},{10,... | collective-permute-start | bytes 786440 | tf_op jit(solution)/shard_map/ppermute | solution.py:85
  83.7 8.1 %collective-permute-start.13 = (bf16[128,1024]{1,0:T(8,128)(2,1)S(1)}, bf16[128,1024]{1,0:T(8,128)(2,1)S(1)}, u32[]{:S(2)}, u32[]{:S(2)}) collective-permute-start(bf16[128,1024]{1,0:T(8,128)(2,1)S(1)} %get-tuple-element.139), channel_id=1, source_target_pairs={{0,2},{1,3},{2,4},{3,5},{4,6},{5,7},{6,0},{7,1},{8,10},{9,11},{10,... | collective-permute-start | bytes 786440 | tf_op jit(solution)/shard_map/ppermute | solution.py:85
  87.7 8.3 %collective-permute-start.22 = (bf16[128,1152]{1,0:T(8,128)(2,1)S(1)}, bf16[128,1152]{1,0:T(8,128)(2,1)S(1)}, u32[]{:S(2)}, u32[]{:S(2)}) collective-permute-start(bf16[128,1152]{1,0:T(8,128)(2,1)S(1)} %get-tuple-element.176.refs_0_), channel_id=1, source_target_pairs={{0,16},{8,24},{16,32},{24,40},{32,48},{40,56},{48,0},{56,8},{64,80... | collective-permute-start | bytes 884744 | tf_op jit(solution)/shard_map/ppermute | solution.py:85
  89.1 8.4 %collective-permute-start.23 = (bf16[128,1152]{1,0:T(8,128)(2,1)S(1)}, bf16[128,1152]{1,0:T(8,128)(2,1)S(1)}, u32[]{:S(2)}, u32[]{:S(2)}) collective-permute-start(bf16[128,1152]{1,0:T(8,128)(2,1)S(1)} %get-tuple-element.176.refs_0_), channel_id=1, source_target_pairs={{0,48},{8,56},{16,0},{24,8},{32,16},{40,24},{48,32},{56,40},{64,11... | collective-permute-start | bytes 884744 | tf_op jit(solution)/shard_map/ppermute | solution.py:85
  92.1 10.5 %collective-permute-start.14 = (bf16[256,1024]{1,0:T(8,128)(2,1)S(1)}, bf16[256,1024]{1,0:T(8,128)(2,1)S(1)}, u32[]{:S(2)}, u32[]{:S(2)}) collective-permute-start(bf16[256,1024]{1,0:T(8,128)(2,1)S(1)} %pad_maximum_fusion.6), channel_id=1, source_target_pairs={{0,2},{1,3},{2,4},{3,5},{4,6},{5,7},{6,0},{7,1},{8,10},{9,11},{10,... | collective-permute-start | bytes 1572872 | tf_op jit(solution)/shard_map/ppermute | solution.py:85
  95.9 10.5 %collective-permute-start.12 = (bf16[256,1024]{1,0:T(8,128)(2,1)S(1)}, bf16[256,1024]{1,0:T(8,128)(2,1)S(1)}, u32[]{:S(2)}, u32[]{:S(2)}) collective-permute-start(bf16[256,1024]{1,0:T(8,128)(2,1)S(1)} %pad_maximum_fusion.5), channel_id=1, source_target_pairs={{0,6},{1,7},{2,0},{3,1},{4,2},{5,3},{6,4},{7,5},{8,14},{9,15},{10,... | collective-permute-start | bytes 1572872 | tf_op jit(solution)/shard_map/ppermute | solution.py:85
  96.1 10.8 %collective-permute-start.24 = (bf16[64,1152]{1,0:T(8,128)(2,1)S(1)}, bf16[64,1152]{1,0:T(8,128)(2,1)S(1)}, u32[]{:S(2)}, u32[]{:S(2)}) collective-permute-start(bf16[64,1152]{1,0:T(8,128)(2,1)S(1)} %slice.383), channel_id=1, source_target_pairs={{0,16},{8,24},{16,32},{24,40},{32,48},{40,56},{48,0},{56,8},{64,80... | collective-permute-start | bytes 442376 | tf_op jit(solution)/shard_map/ppermute | solution.py:85
  97.5 10.0 %collective-permute-start.25 = (bf16[64,1152]{1,0:T(8,128)(2,1)S(1)}, bf16[64,1152]{1,0:T(8,128)(2,1)S(1)}, u32[]{:S(2)}, u32[]{:S(2)}) collective-permute-start(bf16[64,1152]{1,0:T(8,128)(2,1)S(1)} %slice.384), channel_id=1, source_target_pairs={{0,48},{8,56},{16,0},{24,8},{32,16},{40,24},{48,32},{56,40},{64,11... | collective-permute-start | bytes 442376 | tf_op jit(solution)/shard_map/ppermute | solution.py:85
  108.2 27.7 %collective-permute-start.26 = (bf16[512,1152]{1,0:T(8,128)(2,1)}, bf16[512,1152]{1,0:T(8,128)(2,1)S(1)}, u32[]{:S(2)}, u32[]{:S(2)}) collective-permute-start(bf16[512,1152]{1,0:T(8,128)(2,1)} %constant_dynamic-update-slice_fusion.21), channel_id=1, source_target_pairs={{0,8},{8,0},{16,24},{24,16},{32,40},{40,32},{48,56},{56,48},{64,72... | collective-permute-start | bytes 3538952 | tf_op jit(solution)/shard_map/ppermute | solution.py:85
  121.5 11.7 %collective-permute-start.17 = (bf16[256,1024]{1,0:T(8,128)(2,1)}, bf16[256,1024]{1,0:T(8,128)(2,1)}, u32[]{:S(2)}, u32[]{:S(2)}) collective-permute-start(bf16[256,1024]{1,0:T(8,128)(2,1)} %pad_maximum_fusion.7), channel_id=1, source_target_pairs={{0,2},{1,3},{2,4},{3,5},{4,6},{5,7},{6,0},{7,1},{8,10},{9,11},{10,... | collective-permute-start | bytes 1572872 | tf_op jit(solution)/shard_map/ppermute | solution.py:85
  121.5 16.0 %collective-permute-start.18 = (bf16[256,1024]{1,0:T(8,128)(2,1)}, bf16[256,1024]{1,0:T(8,128)(2,1)}, u32[]{:S(2)}, u32[]{:S(2)}) collective-permute-start(bf16[256,1024]{1,0:T(8,128)(2,1)} %pad_maximum_fusion.7), channel_id=1, source_target_pairs={{0,6},{1,7},{2,0},{3,1},{4,2},{5,3},{6,4},{7,5},{8,14},{9,15},{10,... | collective-permute-start | bytes 1572872 | tf_op jit(solution)/shard_map/ppermute | solution.py:85
  134.2 10.1 %collective-permute-start.19 = (bf16[128,1024]{1,0:T(8,128)(2,1)S(1)}, bf16[128,1024]{1,0:T(8,128)(2,1)S(1)}, u32[]{:S(2)}, u32[]{:S(2)}) collective-permute-start(bf16[128,1024]{1,0:T(8,128)(2,1)S(1)} %slice.381), channel_id=1, source_target_pairs={{0,2},{1,3},{2,4},{3,5},{4,6},{5,7},{6,0},{7,1},{8,10},{9,11},{10,... | collective-permute-start | bytes 786440 | tf_op jit(solution)/shard_map/ppermute | solution.py:85
  138.5 7.7 %collective-permute-start.20 = (bf16[128,1024]{1,0:T(8,128)(2,1)S(1)}, bf16[128,1024]{1,0:T(8,128)(2,1)S(1)}, u32[]{:S(2)}, u32[]{:S(2)}) collective-permute-start(bf16[128,1024]{1,0:T(8,128)(2,1)S(1)} %slice.382), channel_id=1, source_target_pairs={{0,6},{1,7},{2,0},{3,1},{4,2},{5,3},{6,4},{7,5},{8,14},{9,15},{10,... | collective-permute-start | bytes 786440 | tf_op jit(solution)/shard_map/ppermute | solution.py:85
  157.6 10.3 %collective-permute-start.27 = (bf16[128,1024]{1,0:T(8,128)(2,1)S(1)}, bf16[128,1024]{1,0:T(8,128)(2,1)S(1)}, u32[]{:S(2)}, u32[]{:S(2)}) collective-permute-start(bf16[128,1024]{1,0:T(8,128)(2,1)S(1)} %get-tuple-element.132), channel_id=1, source_target_pairs={{0,6},{1,7},{2,0},{3,1},{4,2},{5,3},{6,4},{7,5},{8,14},{9,15},{10,... | collective-permute-start | bytes 786440 | tf_op jit(solution)/shard_map/ppermute | solution.py:85
  158.5 9.5 %collective-permute-start.29 = (bf16[128,1024]{1,0:T(8,128)(2,1)S(1)}, bf16[128,1024]{1,0:T(8,128)(2,1)S(1)}, u32[]{:S(2)}, u32[]{:S(2)}) collective-permute-start(bf16[128,1024]{1,0:T(8,128)(2,1)S(1)} %get-tuple-element.133), channel_id=1, source_target_pairs={{0,2},{1,3},{2,4},{3,5},{4,6},{5,7},{6,0},{7,1},{8,10},{9,11},{10,... | collective-permute-start | bytes 786440 | tf_op jit(solution)/shard_map/ppermute | solution.py:85
  167.9 17.2 %collective-permute-start.48 = (bf16[512,1152]{1,0:T(8,128)(2,1)S(1)}, bf16[512,1152]{1,0:T(8,128)(2,1)S(1)}, u32[]{:S(2)}, u32[]{:S(2)}) collective-permute-start(bf16[512,1152]{1,0:T(8,128)(2,1)S(1)} %get-tuple-element.77), channel_id=1, source_target_pairs={{0,8},{8,0},{16,24},{24,16},{32,40},{40,32},{48,56},{56,48},{64,72... | collective-permute-start | bytes 3538952 | tf_op jit(solution)/shard_map/ppermute | solution.py:85
  168.2 14.4 %collective-permute-start.30 = (bf16[256,1024]{1,0:T(8,128)(2,1)S(1)}, bf16[256,1024]{1,0:T(8,128)(2,1)S(1)}, u32[]{:S(2)}, u32[]{:S(2)}) collective-permute-start(bf16[256,1024]{1,0:T(8,128)(2,1)S(1)} %pad_maximum_fusion.9), channel_id=1, source_target_pairs={{0,2},{1,3},{2,4},{3,5},{4,6},{5,7},{6,0},{7,1},{8,10},{9,11},{10,... | collective-permute-start | bytes 1572872 | tf_op jit(solution)/shard_map/ppermute | solution.py:85
  168.9 15.1 %collective-permute-start.28 = (bf16[256,1024]{1,0:T(8,128)(2,1)S(1)}, bf16[256,1024]{1,0:T(8,128)(2,1)S(1)}, u32[]{:S(2)}, u32[]{:S(2)}) collective-permute-start(bf16[256,1024]{1,0:T(8,128)(2,1)S(1)} %pad_maximum_fusion.8), channel_id=1, source_target_pairs={{0,6},{1,7},{2,0},{3,1},{4,2},{5,3},{6,4},{7,5},{8,14},{9,15},{10,... | collective-permute-start | bytes 1572872 | tf_op jit(solution)/shard_map/ppermute | solution.py:85
  191.9 7.5 %collective-permute-start.52 = (bf16[128,1152]{1,0:T(8,128)(2,1)S(1)}, bf16[128,1152]{1,0:T(8,128)(2,1)S(1)}, u32[]{:S(2)}, u32[]{:S(2)}) collective-permute-start(bf16[128,1152]{1,0:T(8,128)(2,1)S(1)} %pad_maximum_fusion.13), channel_id=1, source_target_pairs={{0,16},{8,24},{16,32},{24,40},{32,48},{40,56},{48,0},{56,8},{64,80... | collective-permute-start | bytes 884744 | tf_op jit(solution)/shard_map/ppermute | solution.py:85
  195.2 8.0 %collective-permute-start.50 = (bf16[128,1152]{1,0:T(8,128)(2,1)S(1)}, bf16[128,1152]{1,0:T(8,128)(2,1)S(1)}, u32[]{:S(2)}, u32[]{:S(2)}) collective-permute-start(bf16[128,1152]{1,0:T(8,128)(2,1)S(1)} %pad_maximum_fusion.12), channel_id=1, source_target_pairs={{0,48},{8,56},{16,0},{24,8},{32,16},{40,24},{48,32},{56,40},{64,11... | collective-permute-start | bytes 884744 | tf_op jit(solution)/shard_map/ppermute | solution.py:85
  196.3 8.8 %collective-permute-start.32 = (bf16[128,1024]{1,0:T(8,128)(2,1)S(1)}, bf16[128,1024]{1,0:T(8,128)(2,1)S(1)}, u32[]{:S(2)}, u32[]{:S(2)}) collective-permute-start(bf16[128,1024]{1,0:T(8,128)(2,1)S(1)} %get-tuple-element.112), channel_id=1, source_target_pairs={{0,1},{1,0},{2,3},{3,2},{4,5},{5,4},{6,7},{7,6},{8,9},{9,8},{10,11... | collective-permute-start | bytes 786440 | tf_op jit(solution)/shard_map/ppermute | solution.py:85
  205.1 11.0 %collective-permute-start.33 = (bf16[256,1024]{1,0:T(8,128)(2,1)S(1)}, bf16[256,1024]{1,0:T(8,128)(2,1)S(1)}, u32[]{:S(2)}, u32[]{:S(2)}) collective-permute-start(bf16[256,1024]{1,0:T(8,128)(2,1)S(1)} %pad_maximum_fusion.10), channel_id=1, source_target_pairs={{0,2},{1,3},{2,4},{3,5},{4,6},{5,7},{6,0},{7,1},{8,10},{9,11},{10,... | collective-permute-start | bytes 1572872 | tf_op jit(solution)/shard_map/ppermute | solution.py:85
  205.3 14.1 %collective-permute-start.34 = (bf16[256,1024]{1,0:T(8,128)(2,1)S(1)}, bf16[256,1024]{1,0:T(8,128)(2,1)S(1)}, u32[]{:S(2)}, u32[]{:S(2)}) collective-permute-start(bf16[256,1024]{1,0:T(8,128)(2,1)S(1)} %pad_maximum_fusion.10), channel_id=1, source_target_pairs={{0,6},{1,7},{2,0},{3,1},{4,2},{5,3},{6,4},{7,5},{8,14},{9,15},{10,... | collective-permute-start | bytes 1572872 | tf_op jit(solution)/shard_map/ppermute | solution.py:85
  216.1 7.6 %collective-permute-start.35 = (bf16[128,1024]{1,0:T(8,128)(2,1)S(1)}, bf16[128,1024]{1,0:T(8,128)(2,1)S(1)}, u32[]{:S(2)}, u32[]{:S(2)}) collective-permute-start(bf16[128,1024]{1,0:T(8,128)(2,1)S(1)} %slice.387), channel_id=1, source_target_pairs={{0,2},{1,3},{2,4},{3,5},{4,6},{5,7},{6,0},{7,1},{8,10},{9,11},{10,... | collective-permute-start | bytes 786440 | tf_op jit(solution)/shard_map/ppermute | solution.py:85
  217.3 33.9 %collective-permute-start.67 = (bf16[256,384]{1,0:T(8,128)(2,1)S(1)}, bf16[256,384]{1,0:T(8,128)(2,1)S(1)}, u32[]{:S(2)}, u32[]{:S(2)}) collective-permute-start(bf16[256,384]{1,0:T(8,128)(2,1)S(1)} %constant_dynamic-update-slice_fusion.39.refs_1_), channel_id=1, source_target_pairs={{0,16},{8,24},{16,32},{24,40},{32,48},{40,56},{48,0},{56,8},{64,80... | collective-permute-start | bytes 589832 | tf_op jit(solution)/shard_map/ppermute | solution.py:85
  217.6 35.3 %collective-permute-start.68 = (bf16[256,384]{1,0:T(8,128)(2,1)S(1)}, bf16[256,384]{1,0:T(8,128)(2,1)S(1)}, u32[]{:S(2)}, u32[]{:S(2)}) collective-permute-start(bf16[256,384]{1,0:T(8,128)(2,1)S(1)} %constant_dynamic-update-slice_fusion.39.refs_1_), channel_id=1, source_target_pairs={{0,48},{8,56},{16,0},{24,8},{32,16},{40,24},{48,32},{56,40},{64,11... | collective-permute-start | bytes 589832 | tf_op jit(solution)/shard_map/ppermute | solution.py:85
  219.4 9.3 %collective-permute-start.36 = (bf16[128,1024]{1,0:T(8,128)(2,1)S(1)}, bf16[128,1024]{1,0:T(8,128)(2,1)S(1)}, u32[]{:S(2)}, u32[]{:S(2)}) collective-permute-start(bf16[128,1024]{1,0:T(8,128)(2,1)S(1)} %slice.388), channel_id=1, source_target_pairs={{0,6},{1,7},{2,0},{3,1},{4,2},{5,3},{6,4},{7,5},{8,14},{9,15},{10,... | collective-permute-start | bytes 786440 | tf_op jit(solution)/shard_map/ppermute | solution.py:85
  247.3 28.6 %collective-permute-start.37 = (bf16[128,2048]{1,0:T(8,128)(2,1)}, bf16[128,2048]{1,0:T(8,128)(2,1)S(1)}, u32[]{:S(2)}, u32[]{:S(2)}) collective-permute-start(bf16[128,2048]{1,0:T(8,128)(2,1)} %get-tuple-element.124), channel_id=1, source_target_pairs={{0,6},{1,7},{2,0},{3,1},{4,2},{5,3},{6,4},{7,5},{8,14},{9,15},{10,... | collective-permute-start | bytes 1572872 | tf_op jit(solution)/shard_map/ppermute | solution.py:85
  247.3 29.9 %collective-permute-start.39 = (bf16[128,2048]{1,0:T(8,128)(2,1)S(1)}, bf16[128,2048]{1,0:T(8,128)(2,1)S(1)}, u32[]{:S(2)}, u32[]{:S(2)}) collective-permute-start(bf16[128,2048]{1,0:T(8,128)(2,1)S(1)} %get-tuple-element.125), channel_id=1, source_target_pairs={{0,2},{1,3},{2,4},{3,5},{4,6},{5,7},{6,0},{7,1},{8,10},{9,11},{10,... | collective-permute-start | bytes 1572872 | tf_op jit(solution)/shard_map/ppermute | solution.py:85
  257.3 20.4 %collective-permute-start.42 = (bf16[512,768]{1,0:T(8,128)(2,1)S(1)}, bf16[512,768]{1,0:T(8,128)(2,1)S(1)}, u32[]{:S(2)}, u32[]{:S(2)}) collective-permute-start(bf16[512,768]{1,0:T(8,128)(2,1)S(1)} %get-tuple-element.73), channel_id=1, source_target_pairs={{0,8},{8,0},{16,24},{24,16},{32,40},{40,32},{48,56},{56,48},{64,72... | collective-permute-start | bytes 2359304 | tf_op jit(solution)/shard_map/ppermute | solution.py:85
  273.8 12.7 %collective-permute-start.71 = (bf16[64,384]{1,0:T(8,128)(2,1)S(1)}, bf16[64,384]{1,0:T(8,128)(2,1)S(1)}, u32[]{:S(2)}, u32[]{:S(2)}) collective-permute-start(bf16[64,384]{1,0:T(8,128)(2,1)S(1)} %get-tuple-element.91), channel_id=1, source_target_pairs={{0,8},{8,0},{16,24},{24,16},{32,40},{40,32},{48,56},{56,48},{64,72... | collective-permute-start | bytes 147464 | tf_op jit(solution)/shard_map/ppermute | solution.py:85
  273.9 13.7 %collective-permute-start.72 = (bf16[64,384]{1,0:T(8,128)(2,1)S(1)}, bf16[64,384]{1,0:T(8,128)(2,1)S(1)}, u32[]{:S(2)}, u32[]{:S(2)}) collective-permute-start(bf16[64,384]{1,0:T(8,128)(2,1)S(1)} %get-tuple-element.92), channel_id=1, source_target_pairs={{0,64},{8,72},{16,80},{24,88},{32,96},{40,104},{48,112},{56,120},{... | collective-permute-start | bytes 147464 | tf_op jit(solution)/shard_map/ppermute | solution.py:85
  275.8 12.7 %collective-permute-start.73 = (bf16[64,384]{1,0:T(8,128)(2,1)S(1)}, bf16[64,384]{1,0:T(8,128)(2,1)S(1)}, u32[]{:S(2)}, u32[]{:S(2)}) collective-permute-start(bf16[64,384]{1,0:T(8,128)(2,1)S(1)} %get-tuple-element.93), channel_id=1, source_target_pairs={{0,72},{8,64},{16,88},{24,80},{32,104},{40,96},{48,120},{56,112},{... | collective-permute-start | bytes 147464 | tf_op jit(solution)/shard_map/ppermute | solution.py:85
  284.3 24.6 %collective-permute-start.40 = (bf16[256,2048]{1,0:T(8,128)(2,1)S(1)}, bf16[256,2048]{1,0:T(8,128)(2,1)S(1)}, u32[]{:S(2)}, u32[]{:S(2)}) collective-permute-start(bf16[256,2048]{1,0:T(8,128)(2,1)S(1)} %pad_maximum_fusion.1), channel_id=1, source_target_pairs={{0,2},{1,3},{2,4},{3,5},{4,6},{5,7},{6,0},{7,1},{8,10},{9,11},{10,... | collective-permute-start | bytes 3145736 | tf_op jit(solution)/shard_map/ppermute | solution.py:85
  284.3 25.8 %collective-permute-start.38 = (bf16[256,2048]{1,0:T(8,128)(2,1)S(1)}, bf16[256,2048]{1,0:T(8,128)(2,1)S(1)}, u32[]{:S(2)}, u32[]{:S(2)}) collective-permute-start(bf16[256,2048]{1,0:T(8,128)(2,1)S(1)} %pad_maximum_fusion), channel_id=1, source_target_pairs={{0,6},{1,7},{2,0},{3,1},{4,2},{5,3},{6,4},{7,5},{8,14},{9,15},{10,... | collective-permute-start | bytes 3145736 | tf_op jit(solution)/shard_map/ppermute | solution.py:85
  310.7 17.8 %collective-permute-start.41 = (bf16[128,2048]{1,0:T(8,128)(2,1)S(1)}, bf16[128,2048]{1,0:T(8,128)(2,1)S(1)}, u32[]{:S(2)}, u32[]{:S(2)}) collective-permute-start(bf16[128,2048]{1,0:T(8,128)(2,1)S(1)} %slice.507), channel_id=1, source_target_pairs={{0,1},{1,0},{2,3},{3,2},{4,5},{5,4},{6,7},{7,6},{8,9},{9,8},{10,11... | collective-permute-start | bytes 1572872 | tf_op jit(solution)/shard_map/ppermute | solution.py:85
  312.4 13.7 %collective-permute-start.55 = (bf16[64,256]{1,0:T(8,128)(2,1)S(1)}, bf16[64,256]{1,0:T(8,128)(2,1)S(1)}, u32[]{:S(2)}, u32[]{:S(2)}) collective-permute-start(bf16[64,256]{1,0:T(8,128)(2,1)S(1)} %get-tuple-element.80), channel_id=1, source_target_pairs={{0,64},{8,72},{16,80},{24,88},{32,96},{40,104},{48,112},{56,120},{... | collective-permute-start | bytes 98312 | tf_op jit(solution)/shard_map/ppermute | solution.py:85
  315.5 10.6 %collective-permute-start.56 = (bf16[64,256]{1,0:T(8,128)(2,1)S(1)}, bf16[64,256]{1,0:T(8,128)(2,1)S(1)}, u32[]{:S(2)}, u32[]{:S(2)}) collective-permute-start(bf16[64,256]{1,0:T(8,128)(2,1)S(1)} %get-tuple-element.81), channel_id=1, source_target_pairs={{0,72},{8,64},{16,88},{24,80},{32,104},{40,96},{48,120},{56,112},{... | collective-permute-start | bytes 98312 | tf_op jit(solution)/shard_map/ppermute | solution.py:85
  335.3 16.2 %collective-permute-start.75 = (f32[2304]{0:T(1024)S(1)}, f32[2304]{0:T(1024)S(1)}, u32[]{:S(2)}, u32[]{:S(2)}) collective-permute-start(f32[2304]{0:T(1024)S(1)} %fusion.22), channel_id=1, source_target_pairs={{0,2},{1,3},{2,0},{3,1},{4,6},{5,7},{6,4},{7,5},{8,10},{9,11},{10,... | collective-permute-start | bytes 27656 | tf_op jit(solution)/shard_map/ppermute | solution.py:85
  (85 other events, 810.7 us)
Sparse Core Ops, SparseCore 0:
  18.2 50.8 all-gather.2

commit v2 on v1

--- a/solution.py
+++ b/solution.py
@@ -1,3 +1,4 @@
+import functools
 import math
 
 import jax
@@ -85,11 +86,16 @@
     return lax.ppermute(block, link[0], link[1])
 
 
-def ring_spread(pair, up, down):
+def plain(*payload):
+    return payload
+
+
+def ring_spread(pair, up, down, beside=plain):
     half = pair.shape[0] // 2
     below = send(pair, up)
     above = send(pair, down)
-    return [below, above, send(below[:half], up), send(above[half:], down)]
+    first, second = beside(below[:half], above[half:])
+    return [below, above, send(first, up), send(second, down)]
 
 
 def ring_gather(block, links):
@@ -98,26 +104,37 @@
     return [pair] + ring_spread(pair, up, down)
 
 
-def ring_scatter(partial, rows, links):
+def ring_scatter(parts, links, beside=plain):
     turn, up, down = links
-
-    def slot(first, count=1):
-        return partial[first * rows : (first + count) * rows]
-
-    low = send(slot(6).astype(BF), down)
-    high = send(slot(7).astype(BF), up)
-    to_low = jnp.concatenate([slot(2) + low.astype(F32), slot(3).astype(F32)], axis=0).astype(BF)
-    to_high = jnp.concatenate([slot(4).astype(F32), slot(5) + high.astype(F32)], axis=0).astype(BF)
-    summed = slot(0, 2) + send(to_low, down).astype(F32) + send(to_high, up).astype(F32)
-    return summed[:rows] + send(summed[rows:].astype(BF), turn).astype(F32)
-
-
-def gather_tensor(block):
-    return jnp.concatenate(ring_gather(block, OVER_TENSOR), axis=0)
-
-
-def scatter_tensor(partial):
-    return ring_scatter(partial, ROWS, OVER_TENSOR)
+    own, below, above, low, high = parts
+    rows = low.shape[0]
+    low, high = beside(low.astype(BF), high.astype(BF))
+    low = send(low, down).astype(F32)
+    high = send(high, up).astype(F32)
+    to_low = jnp.concatenate([below[:rows] + low, below[rows:].astype(F32)], axis=0).astype(BF)
+    to_high = jnp.concatenate([above[:rows].astype(F32), above[rows:] + high], axis=0).astype(BF)
+    to_low, to_high = beside(to_low, to_high)
+    summed = own + send(to_low, down).astype(F32) + send(to_high, up).astype(F32)
+    (last,) = beside(summed[rows:].astype(BF))
+    return summed[:rows] + send(last, turn).astype(F32)
+
+
+def part_rows(rows):
+    return (2 * rows, 2 * rows, 2 * rows, rows, rows)
+
+
+def block_of(parts, block):
+    if block < 3:
+        return parts[block][...]
+    return jnp.concatenate([parts[3][...], parts[4][...]], axis=0)
+
+
+def store_block(parts, block, lanes, value):
+    if block < 3:
+        parts[block][:, lanes] = value
+    else:
+        parts[3][:, lanes] = value[:ROWS]
+        parts[4][:, lanes] = value[ROWS:]
 
 
 def slot_place(me, slot, core):
@@ -127,39 +144,34 @@
 
 
 def place_kernel(me_ref, *refs):
-    *near, other, out = refs
+    near, other, outs = refs[:5], refs[5], refs[6:]
     me = me_ref[0]
     core = lax.rem(me, 2)
     slot = 0
     for part in near:
         for at in range(0, part.shape[0], SHARD):
-            out[pl.ds(slot_place(me, slot, core), SHARD), :] = part[at : at + SHARD]
-            out[pl.ds(slot_place(me, slot, 1 - core), SHARD), :] = other[
-                slot * SHARD : (slot + 1) * SHARD
-            ]
+            here = pl.ds(slot_place(me, slot, core), SHARD)
+            there = pl.ds(slot_place(me, slot, 1 - core), SHARD)
+            first = 0
+            for out in outs:
+                lanes = slice(first, first + out.shape[1])
+                out[here, :] = part[at : at + SHARD, lanes]
+                out[there, :] = other[slot * SHARD : (slot + 1) * SHARD, lanes]
+                first += out.shape[1]
             slot += 1
 
 
-def gather_data(block, me):
+def gather_data(block, me, widths):
     near = ring_gather(block, OVER_DATA)
     other = send(jnp.concatenate(near, axis=0), TURN_CORE)
     return pl.pallas_call(
         place_kernel,
-        in_specs=[pl.BlockSpec(memory_space=pltpu.SMEM)] + whole_specs(len(near) + 1),
-        out_specs=whole_specs(1)[0],
-        out_shape=jax.ShapeDtypeStruct((DATA * SHARD, block.shape[1]), BF),
+        in_specs=[pl.BlockSpec(memory_space=pltpu.SMEM)] + whole_specs(6),
+        out_specs=whole_specs(len(widths)),
+        out_shape=[jax.ShapeDtypeStruct((DATA * SHARD, width), BF) for width in widths],
         compiler_params=pltpu.CompilerParams(vmem_limit_bytes=32 * 2**20),
         name="place_weights",
     )(me, *near, other)
-
-
-def split_kernel(me_ref, whole_ref, keep_ref, send_ref):
-    me = me_ref[0]
-    core = lax.rem(me, 2)
-    for slot in range(8):
-        at = slice(slot * SHARD, (slot + 1) * SHARD)
-        keep_ref[at] = whole_ref[pl.ds(slot_place(me, slot, core), SHARD), :]
-        send_ref[at] = whole_ref[pl.ds(slot_place(me, slot, 1 - core), SHARD), :].astype(BF)
 
 
 SCALAR = pl.BlockSpec(memory_space=pltpu.SMEM)
@@ -186,13 +198,14 @@
     return jnp.where(allowed, product, MASKED)
 
 
-def forward_kernel(
-    rows_ref, weight_ref, out_weight_ref, cos_ref, sin_ref, gain_ref, key_row_ref, row_ref, start_ref,
-    raw_ref, low_ref, attended_ref, log_ref, part_ref, value_t,
-):
-    def project(block, carry):
-        at = pl.ds(pl.multiple_of(block * BLOCK, BLOCK), BLOCK)
-        product = dot_f32(rows_ref[at, :], weight_ref[...], ((1,), (0,)))
+def forward_kernel(*refs):
+    rows, refs = refs[:5], refs[5:]
+    weight_ref, out_weight_ref, cos_ref, sin_ref, gain_ref, key_row_ref, row_ref, start_ref = refs[:8]
+    raw_ref, low_ref, attended_ref, log_ref = refs[8:12]
+    parts, value_t = refs[12:17], refs[17]
+    for block in range(ALL_ROWS // BLOCK):
+        at = slice(block * BLOCK, (block + 1) * BLOCK)
+        product = dot_f32(block_of(rows, block), weight_ref[...], ((1,), (0,)))
         raw_ref[at, :] = product
         cosine, sine = cos_ref[at, :], sin_ref[at, :]
         for head in range(3):
@@ -203,9 +216,6 @@
             turned = scaled * cosine + pltpu.roll(scaled, HEAD_SIZE // 2, 1) * sine
             low_ref[at, lanes] = turned.astype(BF)
         low_ref[at, 3 * HEAD_SIZE :] = product[:, 3 * HEAD_SIZE :].astype(BF)
-        return carry
-
-    lax.fori_loop(0, ALL_ROWS // BLOCK, project, 0)
     value_t[...] = low_ref[:, 3 * HEAD_SIZE :].T
     for block in range(ALL_ROWS // BLOCK):
         at = slice(block * BLOCK, (block + 1) * BLOCK)
@@ -222,18 +232,17 @@
             out_t = dot_f32(value_t[...], probability, ((1,), (0,)))
             attended_ref[at, lanes] = out_t.T.astype(BF)
             log_ref[head : head + 1, at] = top + jnp.log(summed)
-        part_ref[at, :] = dot_f32(
-            attended_ref[at, :], out_weight_ref[...], ((1,), (1,))
-        ).astype(BF)
-
-
-def mlp_kernel(
-    slot_ref, rows_ref, grad_ref, weight_ref, hid_ref, d_ref, back_ref, part_ref
-):
-    def turn(block, carry):
-        at = pl.ds(pl.multiple_of(block * BLOCK, BLOCK), BLOCK)
+        part = dot_f32(attended_ref[at, :], out_weight_ref[...], ((1,), (1,)))
+        store_block(parts, block, slice(None), part.astype(BF))
+
+
+def mlp_kernel(slot_ref, *refs):
+    rows, grad_ref, weight_ref, hid_ref, d_ref = refs[:5], *refs[5:9]
+    back, part = refs[9:14], refs[14:19]
+    for block in range(ALL_ROWS // BLOCK):
+        at = slice(block * BLOCK, (block + 1) * BLOCK)
         grads = jnp.concatenate([grad_ref[slot_ref[2 * block]], grad_ref[slot_ref[2 * block + 1]]])
-        both = dot_f32(rows_ref[at, :], weight_ref[:, :768], ((1,), (0,)))
+        both = dot_f32(block_of(rows, block), weight_ref[:, :768], ((1,), (0,)))
         gate, up = both[:, :384], both[:, 384:]
         sigmoid = jax.nn.sigmoid(gate)
         silu = gate * sigmoid
@@ -243,11 +252,10 @@
         d_gate = (d_hid * up * sigmoid * (1.0 + gate * (1.0 - sigmoid))).astype(BF)
         d_both = jnp.concatenate([d_gate, (d_hid * silu).astype(BF)], axis=1)
         d_ref[at, :] = d_both
-        back_ref[at, :] = dot_f32(d_both, weight_ref[:, :768], ((1,), (1,))).astype(BF)
-        part_ref[at, :] = dot_f32(hid, weight_ref[:, 768:], ((1,), (1,))).astype(BF)
-        return carry
-
-    lax.fori_loop(0, ALL_ROWS // BLOCK, turn, 0)
+        d_rows = dot_f32(d_both, weight_ref[:, :768], ((1,), (1,)))
+        store_block(back, block, slice(None), d_rows.astype(BF))
+        out_rows = dot_f32(hid, weight_ref[:, 768:], ((1,), (1,)))
+        store_block(part, block, slice(None), out_rows.astype(BF))
 
 
 def split_rows(me, whole, keep_ref, send_ref):
@@ -258,31 +266,40 @@
         send_ref[at] = whole[pl.ds(slot_place(me, slot, 1 - core), SHARD), :].astype(BF)
 
 
-def mlp_grads_kernel(
-    me_ref, slot_ref, rows_ref, grad_ref, hid_ref, d_ref, keep_ref, send_ref, whole, grads
-):
+def assemble(parts, whole):
+    for block in range(ALL_ROWS // BLOCK):
+        whole[block * BLOCK : (block + 1) * BLOCK] = block_of(parts, block)
+
+
+def mlp_grads_kernel(me_ref, slot_ref, *refs):
+    grad_ref, hid_ref, d_ref, keep_ref, send_ref, whole, grads, rows = refs[5:]
+    assemble(refs[:5], rows)
     for slot in range(TENSOR):
         grads[slot * ROWS : (slot + 1) * ROWS] = grad_ref[slot_ref[slot]]
     for block in range(MODEL_WIDTH // BLOCK):
         at = slice(block * BLOCK, (block + 1) * BLOCK)
-        whole[at, :768] = dot_f32(rows_ref[:, at], d_ref[...], ((0,), (0,)))
+        whole[at, :768] = dot_f32(rows[:, at], d_ref[...], ((0,), (0,)))
         whole[at, 768:] = dot_f32(grads[:, at], hid_ref[...], ((0,), (0,)))
     split_rows(me_ref[0], whole, keep_ref, send_ref)
 
 
-def attn_grads_kernel(me_ref, rows_ref, d_ref, back_ref, attended_ref, keep_ref, send_ref, whole):
+def attn_grads_kernel(me_ref, *refs):
+    d_ref, attended_ref, keep_ref, send_ref, whole, rows, back = refs[10:]
+    assemble(refs[:5], rows)
+    assemble(refs[5:10], back)
     for block in range(MODEL_WIDTH // BLOCK):
         at = slice(block * BLOCK, (block + 1) * BLOCK)
-        whole[at, :512] = dot_f32(rows_ref[:, at], d_ref[...], ((0,), (0,)))
-        whole[at, 512:] = dot_f32(back_ref[:, at], attended_ref[...], ((0,), (0,)))
+        whole[at, :512] = dot_f32(rows[:, at], d_ref[...], ((0,), (0,)))
+        whole[at, 512:] = dot_f32(back[:, at], attended_ref[...], ((0,), (0,)))
     split_rows(me_ref[0], whole, keep_ref, send_ref)
 
 
-def backward_kernel(
-    back_ref, raw_ref, low_ref, log_ref, weight_ref, out_weight_ref, cos_ref, sin_ref, gain_ref,
-    key_row_ref, row_ref, start_ref,
-    d_ref, gain_grad_ref, part_ref, d_key, d_value, key_t,
-):
+def backward_kernel(*refs):
+    back, rows, mlp_parts, refs = refs[:5], refs[5:10], refs[10:15], refs[15:]
+    raw_ref, low_ref, log_ref, weight_ref, out_weight_ref, cos_ref, sin_ref = refs[:7]
+    gain_ref, norm_gain_ref, key_row_ref, row_ref, start_ref = refs[7:12]
+    d_ref, gain_grad_ref, norm_grad_ref, parts = *refs[12:15], refs[15:20]
+    d_key, d_value, key_t = refs[20:]
     keys = slice(2 * HEAD_SIZE, 3 * HEAD_SIZE)
     values = slice(3 * HEAD_SIZE, 4 * HEAD_SIZE)
     key_t[...] = low_ref[:, keys].T
@@ -300,7 +317,7 @@
     query_gain_grad = jnp.zeros((1, HEAD_SIZE), F32)
     for block in range(ALL_ROWS // BLOCK):
         at = slice(block * BLOCK, (block + 1) * BLOCK)
-        d_attended = dot_f32(back_ref[at, :], out_weight_ref[...], ((1,), (0,))).astype(BF)
+        d_attended = dot_f32(block_of(back, block), out_weight_ref[...], ((1,), (0,))).astype(BF)
         for head in range(2):
             lanes = slice(head * HEAD_SIZE, (head + 1) * HEAD_SIZE)
             queries = low_ref[at, lanes]
@@ -322,6 +339,7 @@
             d_ref[at, lanes] = grad
             query_gain_grad = query_gain_grad + gain_part
     key_gain_grad = jnp.zeros((1, HEAD_SIZE), F32)
+    norm_grad = jnp.zeros((1, MODEL_WIDTH), F32)
     for block in range(ALL_ROWS // BLOCK):
         at = slice(block * BLOCK, (block + 1) * BLOCK)
         grad, gain_part = through_norm(
@@ -331,18 +349,32 @@
         d_ref[at, keys] = grad
         d_ref[at, values] = d_value[at, :].astype(BF)
         key_gain_grad = key_gain_grad + gain_part
-        part_ref[at, :] = dot_f32(d_ref[at, :], weight_ref[...], ((1,), (1,))).astype(BF)
+        part = dot_f32(d_ref[at, :], weight_ref[...], ((1,), (1,)))
+        normal = block_of(rows, block).astype(F32)
+        norm_grad = norm_grad + jnp.sum(part * normal, axis=0, keepdims=True)
+        store_block(parts, block, slice(0, MODEL_WIDTH), part.astype(BF))
+        store_block(parts, block, slice(MODEL_WIDTH, None), block_of(mlp_parts, block))
+    norm_grad_ref[...] = norm_grad / norm_gain_ref[...]
     gain_grad_ref[0:1, :] = query_gain_grad
     gain_grad_ref[1:2, :] = key_gain_grad
 
 
-def scatter_data(pair):
+def scatter_data(pair, beside=plain):
     keep, other = pair
-    return ring_scatter(keep + send(other, TURN_CORE).astype(F32), SHARD, OVER_DATA)
+    both = keep + send(other, TURN_CORE).astype(F32)
+    parts, first = [], 0
+    for rows in part_rows(SHARD):
+        parts.append(both[first : first + rows])
+        first += rows
+    return ring_scatter(parts, OVER_DATA, beside)
 
 
 def shape(rows, columns, kind):
     return jax.ShapeDtypeStruct((rows, columns), kind)
+
+
+def part_shapes(columns):
+    return [shape(rows, columns, BF) for rows in part_rows(ROWS)]
 
 
 def split_shapes(width):
@@ -371,27 +403,31 @@
     return lax.dot_general(left, right, (dims, ((), ())), preferred_element_type=F32)
 
 
-def orthogonal_kernel(paired, me_ref, *refs):
-    parts, outs, current = refs[:5], refs[5:9], refs[9]
-    me = me_ref[0]
-    kind = lax.rem(me, 2) + 2 * (me // 8)
-    width = outs[0].shape[1]
-    at = 0
-    for part in parts:
-        current[at : at + part.shape[0]] = part[...].astype(F32)
-        at += part.shape[0]
-    matrix = current[...]
-    columns = jnp.sum(matrix * matrix, axis=0, keepdims=True)
-    size = jnp.sum(columns, keepdims=True)
+def orthogonal_kernel(paired, turns, first, last, me_ref, *refs):
+    kind = lax.rem(me_ref[0], 2) + 2 * (me_ref[0] // 8)
+    taken = 5 if first else 1
+    parts, outs, current = refs[:taken], refs[taken:-1], refs[-1]
+    width = current.shape[1]
     if paired is not None:
-        place = lax.broadcasted_iota(jnp.int32, (1, width), 1) < width // 2
-        first = jnp.sum(jnp.where(place, columns, 0.0), keepdims=True)
-        second = jnp.sum(jnp.where(place, 0.0, columns), keepdims=True)
-        size = jnp.where(kind == paired, jnp.where(place, first, second), size)
         down = lax.broadcasted_iota(jnp.int32, (width, width), 0) < width // 2
         across = lax.broadcasted_iota(jnp.int32, (width, width), 1) < width // 2
         apart = (down != across) & (kind == paired)
-    current[...] = matrix / (jnp.sqrt(size) + 1e-07)
+    if first:
+        at = 0
+        for part in parts:
+            current[at : at + part.shape[0]] = part[...].astype(F32)
+            at += part.shape[0]
+        matrix = current[...]
+        columns = jnp.sum(matrix * matrix, axis=0, keepdims=True)
+        size = jnp.sum(columns, keepdims=True)
+        if paired is not None:
+            place = lax.broadcasted_iota(jnp.int32, (1, width), 1) < width // 2
+            left = jnp.sum(jnp.where(place, columns, 0.0), keepdims=True)
+            right = jnp.sum(jnp.where(place, 0.0, columns), keepdims=True)
+            size = jnp.where(kind == paired, jnp.where(place, left, right), size)
+        current[...] = matrix / (jnp.sqrt(size) + 1e-07)
+    else:
+        current[...] = parts[0][...]
 
     def polynomial(high, low):
         cross = dot_f32(high, low, ((0,), (0,)))
@@ -416,13 +452,16 @@
         current[...] = moved(value, high, low, poly_high, poly_low)
         return carry
 
-    lax.fori_loop(0, NS_ITERS - 1, turn, 0)
+    lax.fori_loop(0, turns - 1 if last else turns, turn, 0)
+    if not last:
+        outs[0][...] = current[...]
+        return
     high, low = split_low(current[...])
     poly_high, poly_low = polynomial(high, low)
     rows = 4 * SHARD
-    last = moved(current[:rows], high[:rows], low[:rows], poly_high, poly_low)
+    final = moved(current[:rows], high[:rows], low[:rows], poly_high, poly_low)
     for number in range(4):
-        outs[number][...] = last[number * SHARD : (number + 1) * SHARD].astype(BF)
+        outs[number][...] = final[number * SHARD : (number + 1) * SHARD].astype(BF)
 
 
 def update_kernel(rates, me_ref, master_ref, *refs):
@@ -439,42 +478,78 @@
                 out[:, at] = master_ref[:, at] - rates[number] * turned[turn][...].astype(F32)
 
 
-def muon(me, renewed, masters, rates, paired):
-    width = renewed.shape[1] // 3
-    scalar = [pl.BlockSpec(memory_space=pltpu.SMEM)]
-    limit = pltpu.CompilerParams(vmem_limit_bytes=48 * 2**20)
-    turns = (TURN_CORE, TURN_FAR, TURN_BOTH)
-    quarter = jax.ShapeDtypeStruct((SHARD, width), BF)
+MUON_TURNS = (TURN_CORE, TURN_FAR, TURN_BOTH)
+
+
+def muon_quarter(me, renewed, beside=plain):
     packed = pl.pallas_call(
         pack_kernel,
-        in_specs=scalar + whole_specs(1),
+        in_specs=[SCALAR] + whole_specs(1),
         out_specs=whole_specs(4),
-        out_shape=[quarter] * 4,
-        compiler_params=limit,
+        out_shape=[shape(SHARD, renewed.shape[1] // 3, BF)] * 4,
+        compiler_params=room(48),
         name="muon_pack",
     )(me, renewed)
-    own = jnp.concatenate(
-        [packed[0]] + [send(block, turn) for block, turn in zip(packed[1:], turns)], axis=0
-    )
-    parts = [own] + ring_spread(own, UP_Y, DOWN_Y)
-    turned = pl.pallas_call(
-        lambda *refs: orthogonal_kernel(paired, *refs),
-        in_specs=scalar + whole_specs(5),
-        out_specs=whole_specs(4),
-        out_shape=[quarter] * 4,
+    moving = beside(*packed[1:])
+    return jnp.concatenate(
+        [packed[0]] + [send(block, turn) for block, turn in zip(moving, MUON_TURNS)], axis=0
+    )
+
+
+def muon_turns(me, parts, paired, count, first, last):
+    width = parts[0].shape[1]
+    flops = 27.0 * count * DATA * SHARD * width * width
+    return pl.pallas_call(
+        functools.partial(orthogonal_kernel, paired, count, first, last),
+        in_specs=[SCALAR] + whole_specs(len(parts)),
+        out_specs=whole_specs(4 if last else 1),
+        out_shape=[shape(SHARD, width, BF)] * 4 if last else [shape(DATA * SHARD, width, F32)],
         scratch_shapes=[pltpu.VMEM((DATA * SHARD, width), F32)],
-        compiler_params=limit,
+        compiler_params=room(48),
+        cost_estimate=cost(flops, 2e6),
         name="muon_turns",
     )(me, *parts)
-    back = [turned[0]] + [send(block, turn) for block, turn in zip(turned[1:], turns)]
+
+
+def muon_finish(me, turned, masters, rates):
+    back = [turned[0]] + [send(block, turn) for block, turn in zip(turned[1:], MUON_TURNS)]
     return pl.pallas_call(
         lambda *refs: update_kernel(rates, *refs),
-        in_specs=scalar + whole_specs(5),
+        in_specs=[SCALAR] + whole_specs(5),
         out_specs=whole_specs(1)[0],
         out_shape=jax.ShapeDtypeStruct(masters.shape, F32),
-        compiler_params=limit,
+        compiler_params=room(48),
         name="muon_update",
     )(me, masters, *back)
+
+
+GAIN_LINKS = [("tensor", [(i, i ^ turn) for i in range(TENSOR)]) for turn in (1, 2, 4)] + [
+    ("dp", [(i, i ^ turn) for i in range(DATA)]) for turn in (1, 2, 4, 8)
+]
+
+
+class Beside:
+    def __init__(self, me, parts, gain, late):
+        self.me, self.parts, self.gain, self.late = me, list(parts), gain, list(late)
+        self.stage = 0
+
+    def gain_step(self):
+        self.gain = self.gain + send(self.gain, GAIN_LINKS[self.stage])
+        self.stage += 1
+
+    def __call__(self, *payload):
+        late = self.late if self.stage == 1 else []
+        tied = lax.optimization_barrier((*payload, self.gain, *late, *self.parts))
+        payload, rest = tied[: len(payload)], tied[len(payload) :]
+        self.gain, rest = rest[0], rest[1:]
+        if late:
+            self.late, rest = list(rest[: len(late)]), rest[len(late) :]
+        self.parts = list(rest)
+        if self.stage < NS_ITERS:
+            first, last = self.stage == 0, self.stage == NS_ITERS - 1
+            self.parts = muon_turns(self.me, self.parts, None, 1, first, last)
+        self.gain_step()
+        return payload
 
 
 def local(
@@ -513,18 +588,16 @@
     query_gain = gains[2 * MODEL_WIDTH : 2 * MODEL_WIDTH + HEAD_SIZE]
     g_key = gains[2 * MODEL_WIDTH + HEAD_SIZE :]
     inputs = tokens.astype(F32)
-    first_normalized = gather_tensor(root_mean_square_norm(inputs, g_attn).astype(BF))
-    attn_weights = gather_data(attn_masters.astype(BF), me)
-    mlp_lowered, first_normalized = lax.optimization_barrier(
-        (mlp_masters.astype(BF), first_normalized)
-    )
-    mlp_weights = gather_data(mlp_lowered, me)
+    normal_rows = ring_gather(root_mean_square_norm(inputs, g_attn).astype(BF), OVER_TENSOR)
+    qkv_full, output_full, mlp_weights = gather_data(
+        jnp.concatenate([attn_masters, mlp_masters], axis=1).astype(BF), me, (512, 256, 1152)
+    )
     slots = [
         lax.rem(tensor_index // 2 + STEPS[s] + 4, 4) * 2 + jnp.bitwise_xor(tensor_index % 2, s % 2)
         for s in range(TENSOR)
     ]
-    in_order = lax.all_gather(out_grad, "tensor", axis=0)
-    qkv_full, output_full = attn_weights[:, :512], attn_weights[:, 512:]
+    late_grad, *normal_rows = lax.optimization_barrier((out_grad, *normal_rows))
+    in_order = lax.all_gather(late_grad, "tensor", axis=0)
     slot_list = jnp.stack(slots).astype(jnp.int32)
     row_index = jnp.concatenate([slot * ROWS + jnp.arange(ROWS, dtype=jnp.int32) for slot in slots])
     segment, token_position = sequence_layout(lengths[0], row_index)
@@ -538,73 +611,76 @@
     key_row = row_index[:, None]
     query_row = row_index[None, :]
     query_start = (row_index - token_position)[None, :]
-    raw, rotated, attn_low, logsum, branch_part = pl.pallas_call(
+    raw, rotated, attn_low, logsum, *branch_part = pl.pallas_call(
         forward_kernel,
-        in_specs=whole_specs(9),
-        out_specs=whole_specs(5),
+        in_specs=whole_specs(13),
+        out_specs=whole_specs(9),
         out_shape=[
             shape(ALL_ROWS, 512, F32),
             shape(ALL_ROWS, 512, BF),
             shape(ALL_ROWS, 256, BF),
             shape(2, ALL_ROWS, F32),
-            shape(ALL_ROWS, MODEL_WIDTH, BF),
+            *part_shapes(MODEL_WIDTH),
         ],
         scratch_shapes=[pltpu.VMEM((HEAD_SIZE, ALL_ROWS), BF)],
         compiler_params=room(48),
         cost_estimate=cost(2.7e9, 12e6),
         name="attention_forward",
     )(
-        first_normalized, qkv_full, output_full, cosine, sine, head_gains,
+        *normal_rows, qkv_full, output_full, cosine, sine, head_gains,
         key_row, query_row, query_start,
     )
-    branch_out = scatter_tensor(branch_part)
+    branch_out = ring_scatter(branch_part, OVER_TENSOR)
     hidden_in = inputs + branch_out
-    n_two = gather_tensor(root_mean_square_norm(hidden_in, g_mlp).astype(BF))
-    inner_act, d_both, back_part, mlp_part = pl.pallas_call(
+    n_two = ring_gather(root_mean_square_norm(hidden_in, g_mlp).astype(BF), OVER_TENSOR)
+    inner_act, d_both, *mlp_parts = pl.pallas_call(
         mlp_kernel,
-        in_specs=[SCALAR] + whole_specs(3),
-        out_specs=whole_specs(4),
+        in_specs=[SCALAR] + whole_specs(7),
+        out_specs=whole_specs(12),
         out_shape=[
             shape(ALL_ROWS, 384, BF),
             shape(ALL_ROWS, 768, BF),
-            shape(ALL_ROWS, MODEL_WIDTH, BF),
-            shape(ALL_ROWS, MODEL_WIDTH, BF),
+            *part_shapes(MODEL_WIDTH),
+            *part_shapes(MODEL_WIDTH),
         ],
         compiler_params=room(48),
         cost_estimate=cost(4.9e9, 12e6),
         name="mlp_both_ways",
-    )(slot_list, n_two, in_order, mlp_weights)
-    d_norm_two = scatter_tensor(back_part)
+    )(slot_list, *n_two, in_order, mlp_weights)
+    d_norm_two = ring_scatter(mlp_parts[:5], OVER_TENSOR)
     mlp_grads = pl.pallas_call(
         mlp_grads_kernel,
-        in_specs=[SCALAR] * 2 + whole_specs(4),
+        in_specs=[SCALAR] * 2 + whole_specs(8),
         out_specs=whole_specs(2),
         out_shape=split_shapes(1152),
         scratch_shapes=[
             pltpu.VMEM((MODEL_WIDTH, 1152), F32),
             pltpu.VMEM((ALL_ROWS, MODEL_WIDTH), BF),
+            pltpu.VMEM((ALL_ROWS, MODEL_WIDTH), BF),
         ],
         compiler_params=room(48),
         cost_estimate=cost(2.4e9, 10e6),
         name="mlp_grads",
-    )(me, slot_list, n_two, in_order, inner_act, d_both)
+    )(me, slot_list, *n_two, in_order, inner_act, d_both)
     mlp_reduced = scatter_data(mlp_grads)
     mlp_renewed = MOMENTUM * mlp_moments + mlp_reduced
-    mlp_updated = muon(
-        me, mlp_renewed, mlp_masters, (1.0, 1.0, math.sqrt(MODEL_WIDTH / FF)), None
-    )
+    mlp_rates = (1.0, 1.0, math.sqrt(MODEL_WIDTH / FF))
+    mlp_own = muon_quarter(me, mlp_renewed)
     _, norm_two_back = jax.vjp(root_mean_square_norm, hidden_in, g_mlp)
     d_hidden_in, dg_mlp = norm_two_back(d_norm_two)
     d_residual = out_grad.astype(F32) + d_hidden_in
-    residual_rows = gather_tensor(d_residual.astype(BF))
-    d_qkv, head_gain_grads, d_norm_part = pl.pallas_call(
+    residual_rows = ring_gather(d_residual.astype(BF), OVER_TENSOR)
+    mlp_own, *residual_rows = lax.optimization_barrier((mlp_own, *residual_rows))
+    mlp_below, mlp_above = send(mlp_own, UP_Y), send(mlp_own, DOWN_Y)
+    d_qkv, head_gain_grads, dg_attn, *last_parts = pl.pallas_call(
         backward_kernel,
-        in_specs=whole_specs(12),
-        out_specs=whole_specs(3),
+        in_specs=whole_specs(27),
+        out_specs=whole_specs(8),
         out_shape=[
             shape(ALL_ROWS, 512, BF),
             shape(2, HEAD_SIZE, F32),
-            shape(ALL_ROWS, MODEL_WIDTH, BF),
+            shape(1, MODEL_WIDTH, F32),
+            *part_shapes(2 * MODEL_WIDTH),
         ],
         scratch_shapes=[
             pltpu.VMEM((ALL_ROWS, HEAD_SIZE), F32),
@@ -615,40 +691,51 @@
         cost_estimate=cost(4.2e9, 14e6),
         name="attention_backward",
     )(
-        residual_rows, raw, rotated, logsum, qkv_full, output_full, cosine, sine, head_gains,
-        key_row, query_row, query_start,
-    )
+        *residual_rows, *normal_rows, *mlp_parts[5:], raw, rotated, logsum, qkv_full, output_full,
+        cosine, sine, head_gains, g_attn[None, :], key_row, query_row, query_start,
+    )
+    d_qkv, mlp_below, mlp_above = lax.optimization_barrier((d_qkv, mlp_below, mlp_above))
     attn_grads = pl.pallas_call(
         attn_grads_kernel,
-        in_specs=[SCALAR] + whole_specs(4),
+        in_specs=[SCALAR] + whole_specs(12),
         out_specs=whole_specs(2),
         out_shape=split_shapes(768),
-        scratch_shapes=[pltpu.VMEM((MODEL_WIDTH, 768), F32)],
+        scratch_shapes=[
+            pltpu.VMEM((MODEL_WIDTH, 768), F32),
+            pltpu.VMEM((ALL_ROWS, MODEL_WIDTH), BF),
+            pltpu.VMEM((ALL_ROWS, MODEL_WIDTH), BF),
+        ],
         compiler_params=room(48),
         cost_estimate=cost(1.6e9, 10e6),
         name="attention_grads",
-    )(me, first_normalized, d_qkv, residual_rows, attn_low)
-    attn_reduced = scatter_data(attn_grads)
+    )(me, *normal_rows, *residual_rows, d_qkv, attn_low)
+    half = 2 * SHARD
+    gain_grad = jnp.concatenate([dg_attn[0], dg_mlp, head_gain_grads[0], head_gain_grads[1]])
+    keep, other, low_half, high_half = lax.optimization_barrier(
+        (*attn_grads, mlp_below[:half], mlp_above[half:])
+    )
+    far_halves = [send(low_half, UP_Y), send(high_half, DOWN_Y)]
+    turns = Beside(me, [mlp_own, mlp_below, mlp_above] + far_halves, gain_grad, last_parts)
+    attn_reduced = scatter_data((keep, other), turns)
     attn_renewed = MOMENTUM * attn_moments + attn_reduced
-    attn_updated = muon(
+    (attn_own,) = turns(muon_quarter(me, attn_renewed, turns))
+    attn_parts = [attn_own] + ring_spread(attn_own, UP_Y, DOWN_Y, turns)
+    mlp_updated = muon_finish(me, turns.parts, mlp_masters, mlp_rates)
+    attn_updated = muon_finish(
         me,
-        attn_renewed,
+        muon_turns(me, attn_parts, 1, NS_ITERS, True, True),
         attn_masters,
         (1.0, 1.0, math.sqrt(MODEL_WIDTH / (QUERY_HEADS * HEAD_SIZE // 16))),
-        1,
-    )
-    both = scatter_tensor(jnp.concatenate([d_norm_part, mlp_part], axis=1))
+    )
+    both = ring_scatter(turns.late, OVER_TENSOR)
     d_norm_one, mlp_out = both[:, :MODEL_WIDTH], both[:, MODEL_WIDTH:]
     result = (hidden_in + mlp_out).astype(BF)
     _, norm_one_back = jax.vjp(root_mean_square_norm, inputs, g_attn)
-    d_inputs, dg_attn = norm_one_back(d_norm_one)
+    d_inputs, _ = norm_one_back(d_norm_one)
     tokens_grad = d_residual + d_inputs
-    gain_grad = jnp.concatenate([dg_attn, dg_mlp, head_gain_grads[0], head_gain_grads[1]])
-    for axis, count in (("tensor", TENSOR), ("dp", DATA)):
-        turn = 1
-        while turn < count:
-            gain_grad = gain_grad + send(gain_grad, (axis, [(i, i ^ turn) for i in range(count)]))
-            turn *= 2
+    while turns.stage < len(GAIN_LINKS):
+        turns.gain_step()
+    gain_grad = turns.gain
     renewed_first = BETA_ONE * gain_first + (1.0 - BETA_ONE) * gain_grad
     renewed_second = BETA_TWO * gain_second + (1.0 - BETA_TWO) * gain_grad * gain_grad
     corrected_first = renewed_first / (1.0 - BETA_ONE**ADAM_STEP)

time: 385 us -> 402 us (1.044)
  waiting for transfers between devices: 138 us -> 180 us
  local copies, waits for them, and re-layouts: 39.1 us -> 19.4 us
  starting transfers between devices: 93.9 us -> 83.2 us
  other arithmetic: 20.6 us -> 27.7 us
    ppermute x81 -> x75, waiting for transfers between devices: 138 us -> 180 us  [send(): return lax.ppermute(block, link[0], link[1])]
    unnamed x130 -> x106, local copies, waits for them, and re-layouts: 21.6 us -> 8.06 us
    ppermute x81 -> x75, starting transfers between devices: 93.8 us -> 83.1 us  [send(): return lax.ppermute(block, link[0], link[1])]
    unnamed x12 -> x15, other arithmetic: 5.2 us -> 10.3 us
    slice x26 -> x25, local copies, waits for them, and re-layouts: 7.46 us -> 2.8 us  [the longest x10 2.38 us: ring_spread(): first, second = beside(below[:half], above[half:])]
    pallas_call x11 -> x15, Pallas kernels: 71.9 us -> 71 us  [the longest x6 22.1 us: muon_turns(): pl.pallas_call(functools.partial(orthogonal_kernel, paired, count, first,...]
  transfers between devices with their start and end apart: 82 -> 76, of which waited for: 42 -> 41; matrix products, arithmetic and copies ran while one was open for 14% -> 8% of each run, Pallas kernels for 16% -> 11%
where the time goes in v2:
time: 402 us; the launch traced here: 397 us
  waiting for transfers between devices  180 us (45%)
  starting transfers between devices  83.2 us (21%)
  Pallas kernels  71.3 us (18%)
  other arithmetic  27.7 us (7%)
  local copies, waits for them, and re-layouts  19.4 us (5%)
  between operations  15.4 us (4%)
    ppermute x75, waiting for transfers between devices, send(): return lax.ppermute(block, link[0], link[1])  180 us
    ppermute x75, starting transfers between devices, send(): return lax.ppermute(block, link[0], link[1])  83.1 us
    pallas_call x6, Pallas kernels, muon_turns(): pl.pallas_call(functools.partial(orthogonal_kernel, paired, count, first,...  22.1 us
    pallas_call x1, Pallas kernels, local(): pl.pallas_call(backward_kernel, in_specs=whole_specs(27), out_specs=whole...  15.7 us
    pallas_call x1, Pallas kernels, local(): pl.pallas_call(forward_kernel, in_specs=whole_specs(13), out_specs=whole_...  13 us
    unnamed x15, other arithmetic  10.3 us
    pallas_call x1, Pallas kernels, local(): pl.pallas_call(mlp_kernel, in_specs=[SCALAR] + whole_specs(7), out_specs=...  9.17 us
    unnamed x106, local copies, waits for them, and re-layouts  8.06 us
  transfers between devices with their start and end apart: 76, of which 41 were waited for; matrix products, arithmetic and copies ran while one was open for 8% of the time, Pallas kernels for 11%

profile of v2, /device:TPU:30, one launch (start us, length us, event | category | flops | bytes accessed | tf_op | source)
XLA Modules:
  0.0 396.6 jit_solution(5064631560045881632)
XLA Ops:
  17.5 3.9 collective-permute-start.5
  30.4 9.5 %collective-permute-done.6.refs_1_ = bf16[128,1920]{1,0:T(8,128)(2,1)S(1)} collective-permute-done((bf16[128,1920]{1,0:T(8,128)(2,1)S(1)}, bf16[128,1920]{1,0:T(8,128)(2,1)S(1)}, u32[]{:S(2)}, u32[]{:S(2)}) %collective-permute-start.6) | collective-permute-done | bytes 491552 | tf_op jit(solution)/shard_map/ppermute | solution.py:86
  43.7 2.4 collective-permute-done.8.refs_3_
  54.6 3.2 fusion.15
  57.7 8.3 %collective-permute-done.1.refs_1_.refs_6_ = bf16[256,1024]{1,0:T(8,128)(2,1)S(1)} collective-permute-done((bf16[256,1024]{1,0:T(8,128)(2,1)S(1)}, bf16[256,1024]{1,0:T(8,128)(2,1)S(1)}, u32[]{:S(2)}, u32[]{:S(2)}) %collective-permute-start.1) | collective-permute-done | bytes 524320 | tf_op jit(solution)/shard_map/ppermute | solution.py:86
  70.9 2.7 pad_maximum_fusion.3
  75.1 3.7 collective-permute-done.4.refs_4_.refs_9_
  81.5 13.0 %attention_forward.1 = (f32[1024,512]{1,0:T(8,128)}, bf16[1024,512]{1,0:T(8,128)(2,1)}, bf16[1024,256]{1,0:T(8,128)(2,1)S(1)}, f32[2,1024]{1,0:T(2,128)S(1)}, bf...) custom-call(bf16[256,1024]{1,0:T(8,128)(2,1)S(1)} %copy-done.6, ...), custom_call_target="tpu_custom_call" | custom-call | flops 2700000000 | bytes 12000000 | tf_op jit(solution)/shard_map/attention_forward/pallas_call | solution.py:614
  96.6 4.6 %collective-permute-done.13 = bf16[128,1024]{1,0:T(8,128)(2,1)S(1)} collective-permute-done((bf16[128,1024]{1,0:T(8,128)(2,1)S(1)}, bf16[128,1024]{1,0:T(8,128)(2,1)S(1)}, u32[]{:S(2)}, u32[]{:S(2)}) %collective-permute-start.13) | collective-permute-done | bytes 262176 | tf_op jit(solution)/shard_map/ppermute | solution.py:86
  103.6 9.2 %collective-permute-done.14 = bf16[256,1024]{1,0:T(8,128)(2,1)S(1)} collective-permute-done((bf16[256,1024]{1,0:T(8,128)(2,1)S(1)}, bf16[256,1024]{1,0:T(8,128)(2,1)S(1)}, u32[]{:S(2)}, u32[]{:S(2)}) %collective-permute-start.14) | collective-permute-done | bytes 524320 | tf_op jit(solution)/shard_map/ppermute | solution.py:86
  112.8 12.4 %collective-permute-done.12 = bf16[256,1024]{1,0:T(8,128)(2,1)S(1)} collective-permute-done((bf16[256,1024]{1,0:T(8,128)(2,1)S(1)}, bf16[256,1024]{1,0:T(8,128)(2,1)S(1)}, u32[]{:S(2)}, u32[]{:S(2)}) %collective-permute-start.12) | collective-permute-done | bytes 524320 | tf_op jit(solution)/shard_map/ppermute | solution.py:86
  125.5 19.4 %collective-permute-done.15 = bf16[128,1024]{1,0:T(8,128)(2,1)S(1)} collective-permute-done((bf16[128,1024]{1,0:T(8,128)(2,1)S(1)}, bf16[128,1024]{1,0:T(8,128)(2,1)S(1)}, u32[]{:S(2)}, u32[]{:S(2)}) %collective-permute-start.15) | collective-permute-done | bytes 262176 | tf_op jit(solution)/shard_map/ppermute | solution.py:86
  145.8 12.0 %collective-permute-done.16 = bf16[128,1024]{1,0:T(8,128)(2,1)S(1)} collective-permute-done((bf16[128,1024]{1,0:T(8,128)(2,1)S(1)}, bf16[128,1024]{1,0:T(8,128)(2,1)S(1)}, u32[]{:S(2)}, u32[]{:S(2)}) %collective-permute-start.16) | collective-permute-done | bytes 262176 | tf_op jit(solution)/shard_map/ppermute | solution.py:86
  160.0 10.4 %collective-permute-done.17.refs_1_ = bf16[256,1024]{1,0:T(8,128)(2,1)S(1)} collective-permute-done((bf16[256,1024]{1,0:T(8,128)(2,1)S(1)}, bf16[256,1024]{1,0:T(8,128)(2,1)S(1)}, u32[]{:S(2)}, u32[]{:S(2)}) %collective-permute-start.17) | collective-permute-done | bytes 524320 | tf_op jit(solution)/shard_map/ppermute | solution.py:86
  173.4 3.5 collective-permute-done.19.refs_3_
  176.9 4.2 %collective-permute-done.20.refs_4_ = bf16[128,1024]{1,0:T(8,128)(2,1)S(1)} collective-permute-done((bf16[128,1024]{1,0:T(8,128)(2,1)}, bf16[128,1024]{1,0:T(8,128)(2,1)S(1)}, u32[]{:S(2)}, u32[]{:S(2)}) %collective-permute-start.20) | collective-permute-done | bytes 262176 | tf_op jit(solution)/shard_map/ppermute | solution.py:86
  181.1 9.2 %mlp_both_ways.1 = (bf16[1024,384]{1,0:T(8,128)(2,1)}, bf16[1024,768]{1,0:T(8,128)(2,1)}, bf16[256,1024]{1,0:T(8,128)(2,1)S(1)}, bf16[256,1024]{1,0:T(8,128)(2,1...) custom-call(s32[8]{0:T(128)S(1)} %stack.47.slot_ref, ...), custom_call_target="tpu_custom_call" | custom-call | flops 4899999744 | bytes 12000000 | tf_op jit(solution)/shard_map/mlp_both_ways/pallas_call | solution.py:636
  192.5 6.5 %collective-permute-done.32 = bf16[128,1024]{1,0:T(8,128)(2,1)S(1)} collective-permute-done((bf16[128,1024]{1,0:T(8,128)(2,1)S(1)}, bf16[128,1024]{1,0:T(8,128)(2,1)S(1)}, u32[]{:S(2)}, u32[]{:S(2)}) %collective-permute-start.32) | collective-permute-done | bytes 262176 | tf_op jit(solution)/shard_map/ppermute | solution.py:86
  201.4 6.3 %mlp_grads.1 = (f32[512,1152]{1,0:T(8,128)}, bf16[512,1152]{1,0:T(8,128)(2,1)S(1)}) custom-call(s32[1]{0:T(128)} %bitcast.me_ref.refs_0_, s32[8]{0:T(128)S(1)} %stack.47.slot_ref, bf16[256,1024]{1,0:T(8,128)(2,1)S(1)} %pad_maximum_fusion.7.refs_0_, bf16[256,1024]{1,0:T(8,128)(2,1)S(1)} %collective-permute-done.17.refs_1_, bf16[256,1024]{1,0:T(8,128)(2,1)S(1)} %copy-done.15, ...), custom_call_target="tpu_custom_call" | custom-call | flops 2400000000 | bytes 10000000 | tf_op jit(solution)/shard_map/mlp_grads/pallas_call | solution.py:651
  211.3 5.9 %collective-permute-done.34 = bf16[128,1024]{1,0:T(8,128)(2,1)S(1)} collective-permute-done((bf16[128,1024]{1,0:T(8,128)(2,1)S(1)}, bf16[128,1024]{1,0:T(8,128)(2,1)S(1)}, u32[]{:S(2)}, u32[]{:S(2)}) %collective-permute-start.34) | collective-permute-done | bytes 262176 | tf_op jit(solution)/shard_map/ppermute | solution.py:86
  221.9 2.2 collective-permute-done.22
  230.5 2.4 collective-permute-done.25
  232.9 2.7 collective-permute-done.23
  235.8 3.0 collective-permute-start.26
  240.1 3.8 collective-permute-start.38
  244.3 3.1 collective-permute-start.28
  253.7 15.7 %attention_backward.1 = (bf16[1024,512]{1,0:T(8,128)(2,1)}, f32[2,128]{1,0:T(2,128)S(1)}, f32[1,1024]{1,0:T(1,128)S(1)}, bf16[256,2048]{1,0:T(8,128)(2,1)}, bf16...) custom-call(bf16[256,1024]{1,0:T(8,128)(2,1)S(1)} %pad_maximum_fusio, ...), custom_call_target="tpu_custom_call" | custom-call | flops 4200000000 | bytes 14000000 | tf_op jit(solution)/shard_map/attention_backward/pallas_call | solution.py:675
  269.4 4.6 %attention_grads.1 = (f32[512,768]{1,0:T(8,128)}, bf16[512,768]{1,0:T(8,128)(2,1)S(1)}) custom-call(s32[1]{0:T(128)} %bitcast.me_ref.refs_0_, bf16[256,1024]{1,0:T(8,128)(2,1)S(1)} %copy-done.7, bf16[256,1024]{1,0:T(8,128)(2,1)S(1)} %copy-done.10, bf16[256,1024]{1,0:T(8,128)(2,1)S(1)} %copy-done.13, ...), custom_call_target="tpu_custom_call" | custom-call | flops 1600000000 | bytes 10000000 | tf_op jit(solution)/shard_map/attention_grads/pallas_call | solution.py:698
  275.7 3.0 collective-permute-start.43
  281.4 3.4 collective-permute-done.44.refs_4_
  287.5 3.5 muon_turns.6.refs_0_
  291.1 2.5 collective-permute-start.50
  295.7 3.1 muon_turns.7.refs_0_
  298.9 4.9 %collective-permute-done.55 = f32[2304]{0:T(1024)S(1)} collective-permute-done((f32[2304]{0:T(1024)S(1)}, f32[2304]{0:T(1024)S(1)}, u32[]{:S(2)}, u32[]{:S(2)}) %collective-permute-start.55) | collective-permute-done | bytes 9248 | tf_op jit(solution)/shard_map/ppermute | solution.py:86
  304.0 3.4 collective-permute-start.56
  307.4 2.2 collective-permute-start.57
  309.6 3.1 muon_turns.8.refs_0_
  315.0 2.8 collective-permute-start.58
  317.8 3.1 muon_turns.9.refs_0_
  327.9 2.5 collective-permute-done.63.refs_2_
  333.1 2.4 collective-permute-done.73
  337.1 2.6 collective-permute-start.74
  340.0 2.5 collective-permute-done.74
  343.6 2.9 collective-permute-start.51
  347.6 7.2 %muon_turns.11 = (bf16[64,256]{1,0:T(8,128)(2,1)S(1)}, bf16[64,256]{1,0:T(8,128)(2,1)S(1)}, bf16[64,256]{1,0:T(8,128)(2,1)S(1)}, bf16[64,256]{1,0:T(8,128)(2,1)S(1)}) custom-call(s32[1]{0:T(128)} %bitcast.me_ref.refs_0_, bf16[256,256]{1,0:T(8,128)(2,1)S(1)} %pad_maximum_fusion.19.refs_0_, bf16[256,256]{1,0:T(8,128)(2,1)S(1)} %collective-permute-done.62.refs_1_, ...), custom_call_target="tpu_custom_call" | custom-call | flops 9059696640 | bytes 2000000 | tf_op jit(solution)/shard_map/muon_turns/pallas_call | solution.py:502
  358.8 10.8 %collective-permute-done.51 = bf16[256,2048]{1,0:T(8,128)(2,1)S(1)} collective-permute-done((bf16[256,2048]{1,0:T(8,128)(2,1)S(1)}, bf16[256,2048]{1,0:T(8,128)(2,1)S(1)}, u32[]{:S(2)}, u32[]{:S(2)}) %collective-permute-start.51) | collective-permute-done | bytes 1048608 | tf_op jit(solution)/shard_map/ppermute | solution.py:86
  369.6 3.9 collective-permute-done.49
  376.7 11.4 %collective-permute-done.52 = bf16[128,2048]{1,0:T(8,128)(2,1)S(1)} collective-permute-done((bf16[128,2048]{1,0:T(8,128)(2,1)S(1)}, bf16[128,2048]{1,0:T(8,128)(2,1)S(1)}, u32[]{:S(2)}, u32[]{:S(2)}) %collective-permute-start.52) | collective-permute-done | bytes 524320 | tf_op jit(solution)/shard_map/ppermute | solution.py:86
  (348 shorter events, 112.3 us)
Async XLA Ops:
  7.2 166.2 %all-gather.3.cloned.1.call-start = ((), (), s32[]{:S(2)}) async-start(), calls=%async_computation | async-start | bytes 2359296 | tf_op jit(solution)/shard_map/all_gather | solution.py:600
  17.5 9.8 %collective-permute-start.5 = (bf16[64,1920]{1,0:T(8,128)(2,1)S(1)}, bf16[64,1920]{1,0:T(8,128)(2,1)S(1)}, u32[]{:S(2)}, u32[]{:S(2)}) collective-permute-start(bf16[64,1920]{1,0:T(8,128)(2,1)S(1)} %get-tuple-element.293), channel_id=1, source_target_pairs={{0,64},{8,72},{16,80},{24,88},{32,96},{40,104},{48,112},{56,120},{... | collective-permute-start | bytes 737288 | tf_op jit(solution)/shard_map/ppermute | solution.py:86
  25.0 25.6 %collective-permute-start = (bf16[128,1024]{1,0:T(8,128)(2,1)}, bf16[128,1024]{1,0:T(8,128)(2,1)}, u32[]{:S(2)}, u32[]{:S(2)}) collective-permute-start(bf16[128,1024]{1,0:T(8,128)(2,1)} %fusion.5), channel_id=1, source_target_pairs={{0,1},{1,0},{2,3},{3,2},{4,5},{5,4},{6,7},{7,6},{8,9},{9,8},{10,11... | collective-permute-start | bytes 786440 | tf_op jit(solution)/shard_map/ppermute | solution.py:86
  27.4 12.5 %collective-permute-start.6 = (bf16[128,1920]{1,0:T(8,128)(2,1)S(1)}, bf16[128,1920]{1,0:T(8,128)(2,1)S(1)}, u32[]{:S(2)}, u32[]{:S(2)}) collective-permute-start(bf16[128,1920]{1,0:T(8,128)(2,1)S(1)} %pad_maximum_fusion.11.refs_0_), channel_id=1, source_target_pairs={{0,16},{8,24},{16,32},{24,40},{32,48},{40,56},{48,0},{56,8},{64,80... | collective-permute-start | bytes 1474568 | tf_op jit(solution)/shard_map/ppermute | solution.py:86
  27.7 13.8 %collective-permute-start.7 = (bf16[128,1920]{1,0:T(8,128)(2,1)S(1)}, bf16[128,1920]{1,0:T(8,128)(2,1)S(1)}, u32[]{:S(2)}, u32[]{:S(2)}) collective-permute-start(bf16[128,1920]{1,0:T(8,128)(2,1)S(1)} %pad_maximum_fusion.11.refs_0_), channel_id=1, source_target_pairs={{0,48},{8,56},{16,0},{24,8},{32,16},{40,24},{48,32},{56,40},{64,11... | collective-permute-start | bytes 1474568 | tf_op jit(solution)/shard_map/ppermute | solution.py:86
  41.5 7.5 %collective-permute-start.9 = (bf16[64,1920]{1,0:T(8,128)(2,1)S(1)}, bf16[64,1920]{1,0:T(8,128)(2,1)S(1)}, u32[]{:S(2)}, u32[]{:S(2)}) collective-permute-start(bf16[64,1920]{1,0:T(8,128)(2,1)S(1)} %slice.336), channel_id=1, source_target_pairs={{0,48},{8,56},{16,0},{24,8},{32,16},{40,24},{48,32},{56,40},{64,11... | collective-permute-start | bytes 737288 | tf_op jit(solution)/shard_map/ppermute | solution.py:86
  50.3 28.4 %collective-permute-start.10 = (bf16[512,1920]{1,0:T(8,128)(2,1)}, bf16[512,1920]{1,0:T(8,128)(2,1)S(1)}, u32[]{:S(2)}, u32[]{:S(2)}) collective-permute-start(bf16[512,1920]{1,0:T(8,128)(2,1)} %constant_dynamic-update-slice_fusion.7), channel_id=1, source_target_pairs={{0,8},{8,0},{16,24},{24,16},{32,40},{40,32},{48,56},{56,48},{64,72... | collective-permute-start | bytes 5898248 | tf_op jit(solution)/shard_map/ppermute | solution.py:86
  51.6 14.4 %collective-permute-start.1 = (bf16[256,1024]{1,0:T(8,128)(2,1)S(1)}, bf16[256,1024]{1,0:T(8,128)(2,1)S(1)}, u32[]{:S(2)}, u32[]{:S(2)}) collective-permute-start(bf16[256,1024]{1,0:T(8,128)(2,1)S(1)} %pad_maximum_fusion.2.refs_0_.refs_5_), channel_id=1, source_target_pairs={{0,2},{1,3},{2,4},{3,5},{4,6},{5,7},{6,0},{7,1},{8,10},{9,11},{10,... | collective-permute-start | bytes 1572872 | tf_op jit(solution)/shard_map/ppermute | solution.py:86
  52.2 16.3 %collective-permute-start.2 = (bf16[256,1024]{1,0:T(8,128)(2,1)S(1)}, bf16[256,1024]{1,0:T(8,128)(2,1)S(1)}, u32[]{:S(2)}, u32[]{:S(2)}) collective-permute-start(bf16[256,1024]{1,0:T(8,128)(2,1)S(1)} %pad_maximum_fusion.2.refs_0_.refs_5_), channel_id=1, source_target_pairs={{0,6},{1,7},{2,0},{3,1},{4,2},{5,3},{6,4},{7,5},{8,14},{9,15},{10,... | collective-permute-start | bytes 1572872 | tf_op jit(solution)/shard_map/ppermute | solution.py:86
  66.8 8.2 %collective-permute-start.3 = (bf16[128,1024]{1,0:T(8,128)(2,1)}, bf16[128,1024]{1,0:T(8,128)(2,1)}, u32[]{:S(2)}, u32[]{:S(2)}) collective-permute-start(bf16[128,1024]{1,0:T(8,128)(2,1)} %slice.333), channel_id=1, source_target_pairs={{0,2},{1,3},{2,4},{3,5},{4,6},{5,7},{6,0},{7,1},{8,10},{9,11},{10,... | collective-permute-start | bytes 786440 | tf_op jit(solution)/shard_map/ppermute | solution.py:86
  69.4 9.3 %collective-permute-start.4 = (bf16[128,1024]{1,0:T(8,128)(2,1)}, bf16[128,1024]{1,0:T(8,128)(2,1)}, u32[]{:S(2)}, u32[]{:S(2)}) collective-permute-start(bf16[128,1024]{1,0:T(8,128)(2,1)} %slice.334), channel_id=1, source_target_pairs={{0,6},{1,7},{2,0},{3,1},{4,2},{5,3},{6,4},{7,5},{8,14},{9,15},{10,... | collective-permute-start | bytes 786440 | tf_op jit(solution)/shard_map/ppermute | solution.py:86
  94.5 8.3 %collective-permute-start.11 = (bf16[128,1024]{1,0:T(8,128)(2,1)S(1)}, bf16[128,1024]{1,0:T(8,128)(2,1)S(1)}, u32[]{:S(2)}, u32[]{:S(2)}) collective-permute-start(bf16[128,1024]{1,0:T(8,128)(2,1)S(1)} %get-tuple-element.142), channel_id=1, source_target_pairs={{0,6},{1,7},{2,0},{3,1},{4,2},{5,3},{6,4},{7,5},{8,14},{9,15},{10,... | collective-permute-start | bytes 786440 | tf_op jit(solution)/shard_map/ppermute | solution.py:86
  101.3 11.5 %collective-permute-start.14 = (bf16[256,1024]{1,0:T(8,128)(2,1)S(1)}, bf16[256,1024]{1,0:T(8,128)(2,1)S(1)}, u32[]{:S(2)}, u32[]{:S(2)}) collective-permute-start(bf16[256,1024]{1,0:T(8,128)(2,1)S(1)} %pad_maximum_fusion.6), channel_id=1, source_target_pairs={{0,2},{1,3},{2,4},{3,5},{4,6},{5,7},{6,0},{7,1},{8,10},{9,11},{10,... | collective-permute-start | bytes 1572872 | tf_op jit(solution)/shard_map/ppermute | solution.py:86
  103.0 22.2 %collective-permute-start.12 = (bf16[256,1024]{1,0:T(8,128)(2,1)S(1)}, bf16[256,1024]{1,0:T(8,128)(2,1)S(1)}, u32[]{:S(2)}, u32[]{:S(2)}) collective-permute-start(bf16[256,1024]{1,0:T(8,128)(2,1)S(1)} %pad_maximum_fusion.5), channel_id=1, source_target_pairs={{0,6},{1,7},{2,0},{3,1},{4,2},{5,3},{6,4},{7,5},{8,14},{9,15},{10,... | collective-permute-start | bytes 1572872 | tf_op jit(solution)/shard_map/ppermute | solution.py:86
  125.5 19.5 %collective-permute-start.15 = (bf16[128,1024]{1,0:T(8,128)(2,1)S(1)}, bf16[128,1024]{1,0:T(8,128)(2,1)S(1)}, u32[]{:S(2)}, u32[]{:S(2)}) collective-permute-start(bf16[128,1024]{1,0:T(8,128)(2,1)S(1)} %slice.452), channel_id=1, source_target_pairs={{0,1},{1,0},{2,3},{3,2},{4,5},{5,4},{6,7},{7,6},{8,9},{9,8},{10,11... | collective-permute-start | bytes 786440 | tf_op jit(solution)/shard_map/ppermute | solution.py:86
  145.2 12.6 %collective-permute-start.16 = (bf16[128,1024]{1,0:T(8,128)(2,1)S(1)}, bf16[128,1024]{1,0:T(8,128)(2,1)S(1)}, u32[]{:S(2)}, u32[]{:S(2)}) collective-permute-start(bf16[128,1024]{1,0:T(8,128)(2,1)S(1)} %multiply_convert_fusion), channel_id=1, source_target_pairs={{0,1},{1,0},{2,3},{3,2},{4,5},{5,4},{6,7},{7,6},{8,9},{9,8},{10,11... | collective-permute-start | bytes 786440 | tf_op jit(solution)/shard_map/ppermute | solution.py:86
  157.9 12.5 %collective-permute-start.17 = (bf16[256,1024]{1,0:T(8,128)(2,1)S(1)}, bf16[256,1024]{1,0:T(8,128)(2,1)S(1)}, u32[]{:S(2)}, u32[]{:S(2)}) collective-permute-start(bf16[256,1024]{1,0:T(8,128)(2,1)S(1)} %pad_maximum_fusion.7.refs_0_), channel_id=1, source_target_pairs={{0,2},{1,3},{2,4},{3,5},{4,6},{5,7},{6,0},{7,1},{8,10},{9,11},{10,... | collective-permute-start | bytes 1572872 | tf_op jit(solution)/shard_map/ppermute | solution.py:86
  158.8 13.7 %collective-permute-start.18 = (bf16[256,1024]{1,0:T(8,128)(2,1)S(1)}, bf16[256,1024]{1,0:T(8,128)(2,1)S(1)}, u32[]{:S(2)}, u32[]{:S(2)}) collective-permute-start(bf16[256,1024]{1,0:T(8,128)(2,1)S(1)} %pad_maximum_fusion.7.refs_0_), channel_id=1, source_target_pairs={{0,6},{1,7},{2,0},{3,1},{4,2},{5,3},{6,4},{7,5},{8,14},{9,15},{10,... | collective-permute-start | bytes 1572872 | tf_op jit(solution)/shard_map/ppermute | solution.py:86
  173.3 7.8 %collective-permute-start.20 = (bf16[128,1024]{1,0:T(8,128)(2,1)}, bf16[128,1024]{1,0:T(8,128)(2,1)S(1)}, u32[]{:S(2)}, u32[]{:S(2)}) collective-permute-start(bf16[128,1024]{1,0:T(8,128)(2,1)} %slice.340), channel_id=1, source_target_pairs={{0,6},{1,7},{2,0},{3,1},{4,2},{5,3},{6,4},{7,5},{8,14},{9,15},{10,... | collective-permute-start | bytes 786440 | tf_op jit(solution)/shard_map/ppermute | solution.py:86
  190.2 8.7 %collective-permute-start.32 = (bf16[128,1024]{1,0:T(8,128)(2,1)S(1)}, bf16[128,1024]{1,0:T(8,128)(2,1)S(1)}, u32[]{:S(2)}, u32[]{:S(2)}) collective-permute-start(bf16[128,1024]{1,0:T(8,128)(2,1)S(1)} %get-tuple-element.159), channel_id=1, source_target_pairs={{0,2},{1,3},{2,4},{3,5},{4,6},{5,7},{6,0},{7,1},{8,10},{9,11},{10,... | collective-permute-start | bytes 786440 | tf_op jit(solution)/shard_map/ppermute | solution.py:86
  191.1 8.6 %collective-permute-start.30 = (bf16[128,1024]{1,0:T(8,128)(2,1)S(1)}, bf16[128,1024]{1,0:T(8,128)(2,1)S(1)}, u32[]{:S(2)}, u32[]{:S(2)}) collective-permute-start(bf16[128,1024]{1,0:T(8,128)(2,1)S(1)} %get-tuple-element.157), channel_id=1, source_target_pairs={{0,6},{1,7},{2,0},{3,1},{4,2},{5,3},{6,4},{7,5},{8,14},{9,15},{10,... | collective-permute-start | bytes 786440 | tf_op jit(solution)/shard_map/ppermute | solution.py:86
  199.1 9.2 %collective-permute-start.33 = (bf16[256,1024]{1,0:T(8,128)(2,1)S(1)}, bf16[256,1024]{1,0:T(8,128)(2,1)S(1)}, u32[]{:S(2)}, u32[]{:S(2)}) collective-permute-start(bf16[256,1024]{1,0:T(8,128)(2,1)S(1)} %pad_maximum_fusion.9), channel_id=1, source_target_pairs={{0,2},{1,3},{2,4},{3,5},{4,6},{5,7},{6,0},{7,1},{8,10},{9,11},{10,... | collective-permute-start | bytes 1572872 | tf_op jit(solution)/shard_map/ppermute | solution.py:86
  199.8 10.5 %collective-permute-start.31 = (bf16[256,1024]{1,0:T(8,128)(2,1)S(1)}, bf16[256,1024]{1,0:T(8,128)(2,1)S(1)}, u32[]{:S(2)}, u32[]{:S(2)}) collective-permute-start(bf16[256,1024]{1,0:T(8,128)(2,1)S(1)} %pad_maximum_fusion.8), channel_id=1, source_target_pairs={{0,6},{1,7},{2,0},{3,1},{4,2},{5,3},{6,4},{7,5},{8,14},{9,15},{10,... | collective-permute-start | bytes 1572872 | tf_op jit(solution)/shard_map/ppermute | solution.py:86
  207.7 9.7 %collective-permute-start.21 = (bf16[512,1152]{1,0:T(8,128)(2,1)S(1)}, bf16[512,1152]{1,0:T(8,128)(2,1)S(1)}, u32[]{:S(2)}, u32[]{:S(2)}) collective-permute-start(bf16[512,1152]{1,0:T(8,128)(2,1)S(1)} %get-tuple-element.150), channel_id=1, source_target_pairs={{0,8},{8,0},{16,24},{24,16},{32,40},{40,32},{48,56},{56,48},{64,72... | collective-permute-start | bytes 3538952 | tf_op jit(solution)/shard_map/ppermute | solution.py:86
  227.6 8.0 %collective-permute-start.23 = (bf16[128,1152]{1,0:T(8,128)(2,1)S(1)}, bf16[128,1152]{1,0:T(8,128)(2,1)S(1)}, u32[]{:S(2)}, u32[]{:S(2)}) collective-permute-start(bf16[128,1152]{1,0:T(8,128)(2,1)S(1)} %pad_maximum_fusion.12), channel_id=1, source_target_pairs={{0,48},{8,56},{16,0},{24,8},{32,16},{40,24},{48,32},{56,40},{64,11... | collective-permute-start | bytes 884744 | tf_op jit(solution)/shard_map/ppermute | solution.py:86
  228.4 11.7 %collective-permute-start.36 = (bf16[256,1024]{1,0:T(8,128)(2,1)S(1)}, bf16[256,1024]{1,0:T(8,128)(2,1)S(1)}, u32[]{:S(2)}, u32[]{:S(2)}) collective-permute-start(bf16[256,1024]{1,0:T(8,128)(2,1)S(1)} %pad_maximum_fusion.10.refs_0_.refs_5_), channel_id=1, source_target_pairs={{0,2},{1,3},{2,4},{3,5},{4,6},{5,7},{6,0},{7,1},{8,10},{9,11},{10,... | collective-permute-start | bytes 1572872 | tf_op jit(solution)/shard_map/ppermute | solution.py:86
  230.5 13.3 %collective-permute-start.37 = (bf16[256,1024]{1,0:T(8,128)(2,1)S(1)}, bf16[256,1024]{1,0:T(8,128)(2,1)S(1)}, u32[]{:S(2)}, u32[]{:S(2)}) collective-permute-start(bf16[256,1024]{1,0:T(8,128)(2,1)S(1)} %pad_maximum_fusion.10.refs_0_.refs_5_), channel_id=1, source_target_pairs={{0,6},{1,7},{2,0},{3,1},{4,2},{5,3},{6,4},{7,5},{8,14},{9,15},{10,... | collective-permute-start | bytes 1572872 | tf_op jit(solution)/shard_map/ppermute | solution.py:86
  235.8 8.2 %collective-permute-start.26 = (bf16[64,1152]{1,0:T(8,128)(2,1)S(1)}, bf16[64,1152]{1,0:T(8,128)(2,1)S(1)}, u32[]{:S(2)}, u32[]{:S(2)}) collective-permute-start(bf16[64,1152]{1,0:T(8,128)(2,1)S(1)} %slice.453), channel_id=1, source_target_pairs={{0,64},{8,72},{16,80},{24,88},{32,96},{40,104},{48,112},{56,120},{... | collective-permute-start | bytes 442376 | tf_op jit(solution)/shard_map/ppermute | solution.py:86
  240.1 10.3 %collective-permute-start.38 = (bf16[128,1024]{1,0:T(8,128)(2,1)S(1)}, bf16[128,1024]{1,0:T(8,128)(2,1)S(1)}, u32[]{:S(2)}, u32[]{:S(2)}) collective-permute-start(bf16[128,1024]{1,0:T(8,128)(2,1)S(1)} %slice.352), channel_id=1, source_target_pairs={{0,2},{1,3},{2,4},{3,5},{4,6},{5,7},{6,0},{7,1},{8,10},{9,11},{10,... | collective-permute-start | bytes 786440 | tf_op jit(solution)/shard_map/ppermute | solution.py:86
  243.9 7.7 %collective-permute-start.39 = (bf16[128,1024]{1,0:T(8,128)(2,1)S(1)}, bf16[128,1024]{1,0:T(8,128)(2,1)S(1)}, u32[]{:S(2)}, u32[]{:S(2)}) collective-permute-start(bf16[128,1024]{1,0:T(8,128)(2,1)S(1)} %slice.353), channel_id=1, source_target_pairs={{0,6},{1,7},{2,0},{3,1},{4,2},{5,3},{6,4},{7,5},{8,14},{9,15},{10,... | collective-permute-start | bytes 786440 | tf_op jit(solution)/shard_map/ppermute | solution.py:86
  251.5 17.9 %collective-permute-start.40 = (bf16[256,384]{1,0:T(8,128)(2,1)S(1)}, bf16[256,384]{1,0:T(8,128)(2,1)S(1)}, u32[]{:S(2)}, u32[]{:S(2)}) collective-permute-start(bf16[256,384]{1,0:T(8,128)(2,1)S(1)} %pad_maximum_fusion.15.refs_0_), channel_id=1, source_target_pairs={{0,16},{8,24},{16,32},{24,40},{32,48},{40,56},{48,0},{56,8},{64,80... | collective-permute-start | bytes 589832 | tf_op jit(solution)/shard_map/ppermute | solution.py:86
  253.3 16.1 %collective-permute-start.41 = (bf16[256,384]{1,0:T(8,128)(2,1)S(1)}, bf16[256,384]{1,0:T(8,128)(2,1)S(1)}, u32[]{:S(2)}, u32[]{:S(2)}) collective-permute-start(bf16[256,384]{1,0:T(8,128)(2,1)S(1)} %pad_maximum_fusion.15.refs_0_), channel_id=1, source_target_pairs={{0,48},{8,56},{16,0},{24,8},{32,16},{40,24},{48,32},{56,40},{64,11... | collective-permute-start | bytes 589832 | tf_op jit(solution)/shard_map/ppermute | solution.py:86
  291.1 44.5 %collective-permute-start.50 = (bf16[128,2048]{1,0:T(8,128)(2,1)S(1)}, bf16[128,2048]{1,0:T(8,128)(2,1)S(1)}, u32[]{:S(2)}, u32[]{:S(2)}) collective-permute-start(bf16[128,2048]{1,0:T(8,128)(2,1)S(1)} %get-tuple-element.204), channel_id=1, source_target_pairs={{0,2},{1,3},{2,4},{3,5},{4,6},{5,7},{6,0},{7,1},{8,10},{9,11},{10,... | collective-permute-start | bytes 1572872 | tf_op jit(solution)/shard_map/ppermute | solution.py:86
  293.7 10.2 %collective-permute-start.54 = (bf16[128,768]{1,0:T(8,128)(2,1)S(1)}, bf16[128,768]{1,0:T(8,128)(2,1)S(1)}, u32[]{:S(2)}, u32[]{:S(2)}) collective-permute-start(bf16[128,768]{1,0:T(8,128)(2,1)S(1)} %pad_maximum_fusion.17), channel_id=1, source_target_pairs={{0,16},{8,24},{16,32},{24,40},{32,48},{40,56},{48,0},{56,8},{64,80... | collective-permute-start | bytes 589832 | tf_op jit(solution)/shard_map/ppermute | solution.py:86
  295.0 8.9 %collective-permute-start.53 = (bf16[128,768]{1,0:T(8,128)(2,1)S(1)}, bf16[128,768]{1,0:T(8,128)(2,1)S(1)}, u32[]{:S(2)}, u32[]{:S(2)}) collective-permute-start(bf16[128,768]{1,0:T(8,128)(2,1)S(1)} %pad_maximum_fusion.16), channel_id=1, source_target_pairs={{0,48},{8,56},{16,0},{24,8},{32,16},{40,24},{48,32},{56,40},{64,11... | collective-permute-start | bytes 589832 | tf_op jit(solution)/shard_map/ppermute | solution.py:86
  295.7 8.1 %collective-permute-start.55 = (f32[2304]{0:T(1024)S(1)}, f32[2304]{0:T(1024)S(1)}, u32[]{:S(2)}, u32[]{:S(2)}) collective-permute-start(f32[2304]{0:T(1024)S(1)} %add.335), channel_id=1, source_target_pairs={{0,2},{1,3},{2,0},{3,1},{4,6},{5,7},{6,4},{7,5},{8,10},{9,11},{10,... | collective-permute-start | bytes 27656 | tf_op jit(solution)/shard_map/ppermute | solution.py:86
  304.0 9.0 %collective-permute-start.56 = (bf16[64,768]{1,0:T(8,128)(2,1)S(1)}, bf16[64,768]{1,0:T(8,128)(2,1)S(1)}, u32[]{:S(2)}, u32[]{:S(2)}) collective-permute-start(bf16[64,768]{1,0:T(8,128)(2,1)S(1)} %slice.454), channel_id=1, source_target_pairs={{0,64},{8,72},{16,80},{24,88},{32,96},{40,104},{48,112},{56,120},{... | collective-permute-start | bytes 294920 | tf_op jit(solution)/shard_map/ppermute | solution.py:86
  321.6 15.5 %collective-permute-start.48 = (bf16[128,2048]{1,0:T(8,128)(2,1)S(1)}, bf16[128,2048]{1,0:T(8,128)(2,1)S(1)}, u32[]{:S(2)}, u32[]{:S(2)}) collective-permute-start(bf16[128,2048]{1,0:T(8,128)(2,1)S(1)} %get-tuple-element.202), channel_id=1, source_target_pairs={{0,6},{1,7},{2,0},{3,1},{4,2},{5,3},{6,4},{7,5},{8,14},{9,15},{10,... | collective-permute-start | bytes 1572872 | tf_op jit(solution)/shard_map/ppermute | solution.py:86
  331.1 16.6 %collective-permute-start.65 = (bf16[128,256]{1,0:T(8,128)(2,1)S(1)}, bf16[128,256]{1,0:T(8,128)(2,1)S(1)}, u32[]{:S(2)}, u32[]{:S(2)}) collective-permute-start(bf16[128,256]{1,0:T(8,128)(2,1)S(1)} %slice.381), channel_id=1, source_target_pairs={{0,16},{8,24},{16,32},{24,40},{32,48},{40,56},{48,0},{56,8},{64,80... | collective-permute-start | bytes 196616 | tf_op jit(solution)/shard_map/ppermute | solution.py:86
  333.1 14.5 %collective-permute-start.66 = (bf16[128,256]{1,0:T(8,128)(2,1)S(1)}, bf16[128,256]{1,0:T(8,128)(2,1)S(1)}, u32[]{:S(2)}, u32[]{:S(2)}) collective-permute-start(bf16[128,256]{1,0:T(8,128)(2,1)S(1)} %slice.382), channel_id=1, source_target_pairs={{0,48},{8,56},{16,0},{24,8},{32,16},{40,24},{48,32},{56,40},{64,11... | collective-permute-start | bytes 196616 | tf_op jit(solution)/shard_map/ppermute | solution.py:86
  335.6 8.0 %collective-permute-start.70 = (bf16[64,384]{1,0:T(8,128)(2,1)S(1)}, bf16[64,384]{1,0:T(8,128)(2,1)S(1)}, u32[]{:S(2)}, u32[]{:S(2)}) collective-permute-start(bf16[64,384]{1,0:T(8,128)(2,1)S(1)} %get-tuple-element.235), channel_id=1, source_target_pairs={{0,8},{8,0},{16,24},{24,16},{32,40},{40,32},{48,56},{56,48},{64,72... | collective-permute-start | bytes 147464 | tf_op jit(solution)/shard_map/ppermute | solution.py:86
  335.6 10.9 %collective-permute-start.71 = (bf16[64,384]{1,0:T(8,128)(2,1)S(1)}, bf16[64,384]{1,0:T(8,128)(2,1)S(1)}, u32[]{:S(2)}, u32[]{:S(2)}) collective-permute-start(bf16[64,384]{1,0:T(8,128)(2,1)S(1)} %get-tuple-element.236), channel_id=1, source_target_pairs={{0,64},{8,72},{16,80},{24,88},{32,96},{40,104},{48,112},{56,120},{... | collective-permute-start | bytes 147464 | tf_op jit(solution)/shard_map/ppermute | solution.py:86
  343.6 26.0 %collective-permute-start.51 = (bf16[256,2048]{1,0:T(8,128)(2,1)S(1)}, bf16[256,2048]{1,0:T(8,128)(2,1)S(1)}, u32[]{:S(2)}, u32[]{:S(2)}) collective-permute-start(bf16[256,2048]{1,0:T(8,128)(2,1)S(1)} %pad_maximum_fusion.1), channel_id=1, source_target_pairs={{0,2},{1,3},{2,4},{3,5},{4,6},{5,7},{6,0},{7,1},{8,10},{9,11},{10,... | collective-permute-start | bytes 3145736 | tf_op jit(solution)/shard_map/ppermute | solution.py:86
  346.5 27.0 %collective-permute-start.49 = (bf16[256,2048]{1,0:T(8,128)(2,1)S(1)}, bf16[256,2048]{1,0:T(8,128)(2,1)S(1)}, u32[]{:S(2)}, u32[]{:S(2)}) collective-permute-start(bf16[256,2048]{1,0:T(8,128)(2,1)S(1)} %pad_maximum_fusion), channel_id=1, source_target_pairs={{0,6},{1,7},{2,0},{3,1},{4,2},{5,3},{6,4},{7,5},{8,14},{9,15},{10,... | collective-permute-start | bytes 3145736 | tf_op jit(solution)/shard_map/ppermute | solution.py:86
  354.9 20.4 %collective-permute-start.67 = (bf16[64,256]{1,0:T(8,128)(2,1)S(1)}, bf16[64,256]{1,0:T(8,128)(2,1)S(1)}, u32[]{:S(2)}, u32[]{:S(2)}) collective-permute-start(bf16[64,256]{1,0:T(8,128)(2,1)S(1)} %get-tuple-element.231), channel_id=1, source_target_pairs={{0,8},{8,0},{16,24},{24,16},{32,40},{40,32},{48,56},{56,48},{64,72... | collective-permute-start | bytes 98312 | tf_op jit(solution)/shard_map/ppermute | solution.py:86
  355.8 19.5 %collective-permute-start.68 = (bf16[64,256]{1,0:T(8,128)(2,1)S(1)}, bf16[64,256]{1,0:T(8,128)(2,1)S(1)}, u32[]{:S(2)}, u32[]{:S(2)}) collective-permute-start(bf16[64,256]{1,0:T(8,128)(2,1)S(1)} %get-tuple-element.232), channel_id=1, source_target_pairs={{0,64},{8,72},{16,80},{24,88},{32,96},{40,104},{48,112},{56,120},{... | collective-permute-start | bytes 98312 | tf_op jit(solution)/shard_map/ppermute | solution.py:86
  357.5 17.8 %collective-permute-start.69 = (bf16[64,256]{1,0:T(8,128)(2,1)S(1)}, bf16[64,256]{1,0:T(8,128)(2,1)S(1)}, u32[]{:S(2)}, u32[]{:S(2)}) collective-permute-start(bf16[64,256]{1,0:T(8,128)(2,1)S(1)} %get-tuple-element.233), channel_id=1, source_target_pairs={{0,72},{8,64},{16,88},{24,80},{32,104},{40,96},{48,120},{56,112},{... | collective-permute-start | bytes 98312 | tf_op jit(solution)/shard_map/ppermute | solution.py:86
  374.1 14.0 %collective-permute-start.52 = (bf16[128,2048]{1,0:T(8,128)(2,1)S(1)}, bf16[128,2048]{1,0:T(8,128)(2,1)S(1)}, u32[]{:S(2)}, u32[]{:S(2)}) collective-permute-start(bf16[128,2048]{1,0:T(8,128)(2,1)S(1)} %slice.450), channel_id=1, source_target_pairs={{0,1},{1,0},{2,3},{3,2},{4,5},{5,4},{6,7},{7,6},{8,9},{9,8},{10,11... | collective-permute-start | bytes 1572872 | tf_op jit(solution)/shard_map/ppermute | solution.py:86
  (79 other events, 706.8 us)
Sparse Core Ops, SparseCore 0:
  94.6 62.2 all-gather.2
